TPU v7x, 512 devices: a whole 4x8x8 slice. The times are simulated.
512 devices in a mesh: seq: 128 (over z, y, core), head: 4 (over x).
Axes of the slice: x: 4, y: 8, z: 8, core: 2. Of those that a mesh axis runs over, the one named last changes fastest.
Arguments:
- queries: bfloat16 [16384, 32, 128], P('seq', 'head')
- keys: bfloat16 [16384, 8, 128], P('seq', 'head')
- values: bfloat16 [16384, 8, 128], P('seq', 'head'), may hold values from -6 to 6
- mem_keys: bfloat16 [131072, 8, 128], P('seq', 'head')
- mem_values: bfloat16 [131072, 8, 128], P('seq', 'head'), may hold values from -6 to 6
- mem_ids: int32 [8, 128, 32], P('head', 'seq'), may hold values from 0 to 2047, as said below
- gate_logits: float32 [32], P('head'), may hold values from -3 to 3
Outputs:
- attended: bfloat16 [16384, 4096], P(('seq', 'head'))
Inputs may be any that keep to these rules, and one draw needn't show every extreme that they name: `mem_ids`: ids of memory blocks. The 32 ids of one list differ. Over the 1 lists of the query blocks of one index of seq and one kv head, at most 1 distinct ids lie in any one aligned range of 16 blocks, and some range holds exactly 1.
All inputs are finite; a program needn't handle non-finite values.
Results may differ from a plain program's by a relative error of at most 0.011.
Values may be sent and summed in bfloat16 or wider, within the bound.
No kernel may reach another device: no remote copies, remote signals or barrier semaphores. Data moves between devices by JAX's collectives and lax.ppermute only.
A program may use at most 64 MiB of HBM per device.

v0:
```python
import jax
import jax.numpy as jnp
from jax import lax
from jax.sharding import PartitionSpec as P

QBLK = 128
BLOCK = 64
TOPK = 32


def from_behind(value, axis, by):
    length = lax.axis_size(axis)
    pairs = [(i, i + by) for i in range(length) if 0 <= i + by < length]
    return lax.ppermute(value, axis, pairs)


def attend(query_rows, key_rows, value_rows, allowed):
    score_scale = query_rows.shape[-1] ** (-0.5)
    scores = (
        jnp.einsum("qkgd,ksd->kgqs", query_rows, key_rows, preferred_element_type=jnp.float32)
        * score_scale
    )
    if allowed is not None:
        scores = jnp.where(allowed[None, None, :, :], scores, -1e30)
    highest = jnp.max(scores, axis=3, keepdims=True)
    expo = jnp.exp(scores - highest)
    weights = (expo / jnp.sum(expo, axis=3, keepdims=True)).astype(jnp.bfloat16)
    return jnp.einsum("kgqs,ksd->qkgd", weights, value_rows, preferred_element_type=jnp.float32)


def on_device(queries, keys, values, mem_keys, mem_values, mem_ids, gate_logits):
    tok_rows, q_heads, head_size = queries.shape
    kv_local = keys.shape[1]
    group = q_heads // kv_local
    seq_count = lax.axis_size("seq")
    my_index = lax.axis_index("seq")
    blocks_dev = mem_keys.shape[0] // BLOCK
    capacity = max(1, TOPK // seq_count)
    lists_dev = tok_rows // QBLK
    span = tok_rows + QBLK
    query_groups = queries.reshape(tok_rows, kv_local, group, head_size)
    query_lists = query_groups.reshape(lists_dev, QBLK, kv_local, group, head_size)
    previous = from_behind((keys, values), "seq", 1)
    near_keys = jnp.concatenate([previous[0], keys], axis=0).transpose(1, 0, 2)
    near_values = jnp.concatenate([previous[1], values], axis=0).transpose(1, 0, 2)

    def one_window(operands):
        list_index, query_rows = operands
        start = list_index * QBLK
        key_pos = start - tok_rows + jnp.arange(span, dtype=jnp.int32)
        query_pos = start + jnp.arange(QBLK, dtype=jnp.int32)
        allowed = (key_pos[None, :] <= query_pos[:, None]) & (
            key_pos[None, :] > query_pos[:, None] - tok_rows
        )
        allowed = allowed & ((key_pos[None, :] >= 0) | (my_index > 0))
        return attend(query_rows, near_keys, near_values, allowed)

    list_numbers = jnp.arange(lists_dev, dtype=jnp.int32)
    window_out = lax.map(one_window, (list_numbers, query_lists)).reshape(
        tok_rows, kv_local, group, head_size
    )
    flat_ids = mem_ids.reshape(kv_local, lists_dev * TOPK)
    owner_of = flat_ids // blocks_dev
    local_of = flat_ids % blocks_dev
    count = flat_ids.shape[1]
    order_pos = jnp.arange(count, dtype=jnp.int32)
    same_owner = owner_of[:, :, None] == owner_of[:, None, :]
    same_block = same_owner & (local_of[:, :, None] == local_of[:, None, :])
    earlier = order_pos[None, None, :] < order_pos[None, :, None]
    first_seen = jnp.logical_not(jnp.any(same_block & earlier, axis=2))
    smaller = local_of[:, None, :] < local_of[:, :, None]
    rank_of = jnp.sum((same_owner & first_seen[:, None, :] & smaller).astype(jnp.int32), axis=2)
    head_rows = jnp.arange(kv_local, dtype=jnp.int32)[:, None]
    slot_of = owner_of * capacity + rank_of
    requests = (
        jnp.zeros((kv_local, seq_count * capacity), jnp.int32).at[head_rows, slot_of].max(local_of)
    )
    requests = requests.reshape(kv_local, seq_count, capacity).transpose(1, 0, 2)
    cache_keys = mem_keys.reshape(blocks_dev, BLOCK, kv_local, head_size).transpose(2, 0, 1, 3)
    cache_values = mem_values.reshape(blocks_dev, BLOCK, kv_local, head_size).transpose(2, 0, 1, 3)
    head_index = jnp.arange(kv_local, dtype=jnp.int32)[None, :, None]
    asked = lax.all_to_all(requests, "seq", split_axis=0, concat_axis=0, tiled=True)
    found_keys = cache_keys[head_index, asked]
    found_values = cache_values[head_index, asked]
    fetch_got_keys = lax.all_to_all(found_keys, "seq", split_axis=0, concat_axis=0, tiled=True)
    fetch_got_values = lax.all_to_all(found_values, "seq", split_axis=0, concat_axis=0, tiled=True)
    owner_lists = owner_of.reshape(kv_local, lists_dev, TOPK).transpose(1, 0, 2)
    rank_lists = rank_of.reshape(kv_local, lists_dev, TOPK).transpose(1, 0, 2)
    got_keys, got_values, owner_lists, rank_lists = (
        fetch_got_keys,
        fetch_got_values,
        owner_lists,
        rank_lists,
    )
    list_heads = jnp.arange(kv_local, dtype=jnp.int32)[:, None]

    def one_list(operands):
        query_rows, owners_here, ranks_here = operands
        far_keys = got_keys[owners_here, list_heads, ranks_here].reshape(
            kv_local, TOPK * BLOCK, head_size
        )
        far_values = got_values[owners_here, list_heads, ranks_here].reshape(
            kv_local, TOPK * BLOCK, head_size
        )
        return attend(query_rows, far_keys, far_values, None)

    memory_out = lax.map(one_list, (query_lists, owner_lists, rank_lists)).reshape(
        tok_rows, kv_local, group, head_size
    )
    gate = jax.nn.sigmoid(gate_logits).reshape(kv_local, group)[None, :, :, None]
    mixed = (
        (gate * memory_out + (1.0 - gate) * window_out)
        .reshape(tok_rows, q_heads * head_size)
        .astype(jnp.bfloat16)
    )
    return lax.all_to_all(mixed, "head", split_axis=0, concat_axis=1, tiled=True)


def solution(mesh):
    placed = (
        P("seq", "head", None),
        P("seq", "head", None),
        P("seq", "head", None),
        P("seq", "head", None),
        P("seq", "head", None),
        P("head", "seq", None),
        P("head"),
    )
    return jax.shard_map(
        on_device, mesh=mesh, in_specs=placed, out_specs=P(("seq", "head"), None), check_vma=False
    )
```

profile of v0, /device:TPU:1, one launch (start us, length us, event | category | flops | bytes accessed | tf_op | source)
XLA Modules:
  0.0 279.3 jit_solution(3540715843514825722)
XLA Ops:
  0.0 0.0 copy-start
  0.0 0.7 and_select_fusion.1
  0.8 0.7 and_select_fusion.3
  1.4 0.1 reshape.363
  1.5 0.2 fusion.34
  1.7 0.2 convert_reduce_fusion
  1.9 0.7 fusion.39
  2.6 0.1 reshape.361
  2.7 3.5 %scatter_fusion = s32[2,128]{1,0:T(2,128)S(1)} fusion(s32[2,128]{1,0:T(2,128)S(1)} %broadcast_in_dim.52, s32[64]{0:T(128)S(1)} %reshape.361, s32[64]{0:T(128)S(1)} %reshape.363), kind=kCustom, calls=%fused_computation.4 | custom fusion | flops 64 | bytes 1280 | tf_op jit(solution)/shard_map/scatter-max | solution.py:76
  6.3 0.7 copy.108
  7.0 18.4 %all-to-all-start = ((s32[128,2,1]{1,2,0:T(1,128)}), s32[128,2,1]{1,2,0:T(1,128)S(1)}, u32[]{:S(2)}, u32[]{:S(2)}) async-start(s32[128,2,1]{1,2,0:T(1,128)} %copy.108), calls=%async_computation | async-start | bytes 131072 | tf_op jit(solution)/shard_map/all_to_all | solution.py:82
  25.4 1.1 copy.114
  26.5 10.3 %all-to-all-done = s32[128,2,1]{1,2,0:T(1,128)S(1)} async-done(((s32[128,2,1]{1,2,0:T(1,128)}), s32[128,2,1]{1,2,0:T(1,128)S(1)}, u32[]{:S(2)}, u32[]{:S(2)}) %all-to-all-start) | async-done | bytes 1056 | tf_op jit(solution)/shard_map/all_to_all | solution.py:82
  36.8 0.1 copy.109
  36.9 0.1 copy.112
  37.0 0.1 reshape.335
  37.2 3.4 %gather_fusion.2 = bf16[256,64,128]{2,1,0:T(8,128)(2,1)} fusion(bf16[2,16,64,128]{3,2,1,0:T(8,128)(2,1)S(1)} %bitcast.99, s32[256]{0:T(256)S(1)} %reshape.335), kind=kCustom, calls=%fused_computation.2 | custom fusion | bytes 8390656 | tf_op jit(solution)/shard_map/gather | solution.py:83
  40.5 0.0 copy-start.1
  40.5 7.0 %all-to-all-start.2 = ((bf16[128,2,1,64,128]{4,3,2,1,0:T(8,128)(2,1)}), bf16[128,2,1,64,128]{4,3,2,1,0:T(8,128)(2,1)}, u32[]{:S(2)}, u32[]{:S(2)}) async-start(bf16[128,2,1,64,128]{4,3,2,1,0:T(8,128)(2,1)} %bitcast.102), calls=%async_computation.2 | async-start | bytes 8388608 | tf_op jit(solution)/shard_map/all_to_all | solution.py:85
  47.6 0.0 copy-done.1
  47.6 0.1 copy.107
  47.6 3.4 %gather_fusion = bf16[256,64,128]{2,1,0:T(8,128)(2,1)} fusion(bf16[2,16,64,128]{3,2,1,0:T(8,128)(2,1)S(1)} %bitcast.100, s32[256]{0:T(256)S(1)} %reshape.335), kind=kCustom, calls=%fused_computation | custom fusion | bytes 8390656 | tf_op jit(solution)/shard_map/gather | solution.py:84
  51.0 93.6 %all-to-all-done.2 = bf16[128,2,1,64,128]{4,3,2,1,0:T(8,128)(2,1)} async-done(((bf16[128,2,1,64,128]{4,3,2,1,0:T(8,128)(2,1)}), bf16[128,2,1,64,128]{4,3,2,1,0:T(8,128)(2,1)}, u32[]{:S(2)}, u32[]{:S(2)}) %all-to-all-start.2) | async-done | bytes 4194336 | tf_op jit(solution)/shard_map/all_to_all | solution.py:85
  144.6 0.0 copy-start.2
  144.6 0.0 copy-start.3
  144.6 0.0 copy-start.4
  144.6 16.6 %all-to-all-start.1 = ((bf16[128,2,1,64,128]{4,3,2,1,0:T(8,128)(2,1)}), bf16[128,2,1,64,128]{4,3,2,1,0:T(8,128)(2,1)}, u32[]{:S(2)}, u32[]{:S(2)}) async-start(bf16[128,2,1,64,128]{4,3,2,1,0:T(8,128)(2,1)} %bitcast.101), calls=%async_computation.1 | async-start | bytes 8388608 | tf_op jit(solution)/shard_map/all_to_all | solution.py:86
  161.2 0.0 copy-done.2
  161.2 3.5 %collective-permute-start.1 = (bf16[128,2,128]{2,0,1:T(8,128)(2,1)S(1)}, bf16[128,2,128]{2,0,1:T(8,128)(2,1)S(1)}, u32[]{:S(2)}, u32[]{:S(2)}) collective-permute-start(bf16[128,2,128]{2,0,1:T(8,128)(2,1)S(1)} %copy.122), channel_id=1, source_target_pairs={{0,4},{4,8},{8,12},{12,16},{16,20},{20,24},{24,28},{28,32},{32,36}... | collective-permute-start | bytes 196616 | tf_op jit(solution)/shard_map/ppermute | solution.py:14
  164.7 0.0 copy-done.3
  164.8 0.1 copy.120
  164.9 2.2 collective-permute-start
  167.1 0.0 copy-done.4
  167.2 0.1 mul.46
  167.3 0.1 fusion.29
  167.4 0.1 reshape.341
  167.5 80.9 %collective-permute-done.1 = bf16[128,2,128]{2,0,1:T(8,128)(2,1)S(1)} collective-permute-done((bf16[128,2,128]{2,0,1:T(8,128)(2,1)S(1)}, bf16[128,2,128]{2,0,1:T(8,128)(2,1)S(1)}, u32[]{:S(2)}, u32[]{:S(2)}) %collective-permute-start.1) | collective-permute-done | bytes 65568 | tf_op jit(solution)/shard_map/ppermute | solution.py:14
  248.4 0.0 copy-done
  248.4 0.3 fusion.12
  248.7 0.5 fusion.56
  249.2 1.7 collective-permute-done
  250.9 0.4 convolution_bitcast_fusion
  251.3 0.3 copy.126
  251.6 0.2 reshape.332
  251.8 3.0 %gather_fusion.3 = bf16[64,64,128]{2,1,0:T(8,128)(2,1)S(1)} fusion(bf16[128,2,1,64,128]{4,3,2,1,0:T(8,128)(2,1)} %all-to-all-done.2, s32[64]{0:T(128)S(1)} %reshape.341), kind=kCustom, calls=%fused_computation.3 | custom fusion | bytes 2097920 | tf_op jit(solution)/shard_map/while/body/eval_jaxpr/gather | solution.py:99
  254.8 5.0 %fusion.59 = (f32[2,4,128]{2,1,0:T(4,128)S(1)}, f32[2,4,128,2048]{2,3,1,0:T(8,128)}) fusion(bf16[2,2048,128,1]{2,1,3,0:T(8,128)(2,1)S(1)} %bitcast.104, bf16[128,2,4,128]{3,2,1,0:T(4,128)(2,1)S(1)} %bitcast.96), kind=kOutput, calls=%fused_computation.98 | convolution fusion | flops 543164416 | bytes 9703424 | tf_op jit(solution)/shard_map/while/body/eval_jaxpr/sub | solution.py:26
  259.8 0.0 all-to-all-done.1
  259.8 3.0 %gather_fusion.1 = bf16[64,64,128]{2,1,0:T(8,128)(2,1)S(1)} fusion(bf16[128,2,1,64,128]{4,3,2,1,0:T(8,128)(2,1)} %all-to-all-done.1, s32[64]{0:T(128)S(1)} %reshape.341), kind=kCustom, calls=%fused_computation.1 | custom fusion | bytes 2097920 | tf_op jit(solution)/shard_map/while/body/eval_jaxpr/gather | solution.py:102
  262.8 4.2 %fusion.13 = f32[128,2,4,128]{0,3,2,1:T(8,128)S(1)} fusion(bf16[2,2048,128,1]{2,1,3,0:T(8,128)(2,1)S(1)} %bitcast.103, f32[2,4,128,2048]{2,3,1,0:T(8,128)} %get-tuple-element.44, f32[2,4,128]{2,1,0:T(4,128)S(1)} %get-tuple-element.43), kind=kOutput, calls=%fused_computation.21 | convolution fusion | flops 541065216 | bytes 9965568 | tf_op jit(solution)/shard_map/while/body/eval_jaxpr/kgqs,ksd->qkgd/dot_general | solution.py:28
  267.0 0.3 copy.119
  267.3 0.2 reshape.331
  267.5 0.1 mul.53
  267.6 0.1 mul.47
  267.6 0.1 add_convert_fusion
  267.7 10.9 %all_to_all.31 = bf16[4,32,1024]{2,1,0:T(8,128)(2,1)S(1)} all-to-all(bf16[4,32,1024]{2,1,0:T(8,128)(2,1)S(1)} %add_convert_fusion), channel_id=1, replica_groups=mesh['seq'=128,'head'=4] {'head'}, dimensions={0} | all-to-all | bytes 524288 | tf_op jit(solution)/shard_map/all_to_all | solution.py:116
  278.6 0.7 copy.136
  (15 shorter events, 0.1 us)
Async XLA Ops:
  0.0 248.4 %copy-start = (bf16[128,8,128]{2,1,0:T(8,128)(2,1)S(1)}, bf16[128,8,128]{2,1,0:T(8,128)(2,1)}, u32[]{:S(2)}) copy-start(bf16[128,8,128]{2,1,0:T(8,128)(2,1)} %param.7) | copy-start | bytes 786436
  7.0 29.8 %all-to-all-start = ((s32[128,2,1]{1,2,0:T(1,128)}), s32[128,2,1]{1,2,0:T(1,128)S(1)}, u32[]{:S(2)}, u32[]{:S(2)}) async-start(s32[128,2,1]{1,2,0:T(1,128)} %copy.108), calls=%async_computation | async-start | bytes 131072 | tf_op jit(solution)/shard_map/all_to_all | solution.py:82
  40.5 7.0 %copy-start.1 = (bf16[1024,2,128]{2,1,0:T(2,128)(2,1)S(1)}, bf16[1024,2,128]{2,1,0:T(2,128)(2,1)}, u32[]{:S(2)}) copy-start(bf16[1024,2,128]{2,1,0:T(2,128)(2,1)} %param.11) | copy-start | bytes 1572868
  40.5 104.1 %all-to-all-start.2 = ((bf16[128,2,1,64,128]{4,3,2,1,0:T(8,128)(2,1)}), bf16[128,2,1,64,128]{4,3,2,1,0:T(8,128)(2,1)}, u32[]{:S(2)}, u32[]{:S(2)}) async-start(bf16[128,2,1,64,128]{4,3,2,1,0:T(8,128)(2,1)} %bitcast.102), calls=%async_computation.2 | async-start | bytes 8388608 | tf_op jit(solution)/shard_map/all_to_all | solution.py:85
  144.6 16.6 %copy-start.2 = (bf16[128,2,128]{2,1,0:T(2,128)(2,1)S(1)}, bf16[128,2,128]{2,1,0:T(2,128)(2,1)}, u32[]{:S(2)}) copy-start(bf16[128,2,128]{2,1,0:T(2,128)(2,1)} %param.8) | copy-start | bytes 196612
  144.6 20.2 %copy-start.3 = (bf16[128,2,128]{2,1,0:T(2,128)(2,1)S(1)}, bf16[128,2,128]{2,1,0:T(2,128)(2,1)}, u32[]{:S(2)}) copy-start(bf16[128,2,128]{2,1,0:T(2,128)(2,1)} %param.9) | copy-start | bytes 196612
  144.6 22.5 %copy-start.4 = (f32[8]{0:T(128)S(1)}, f32[8]{0:T(128)}, u32[]{:S(2)}) copy-start(f32[8]{0:T(128)} %param.13) | copy-start | bytes 100
  144.6 115.2 %all-to-all-start.1 = ((bf16[128,2,1,64,128]{4,3,2,1,0:T(8,128)(2,1)}), bf16[128,2,1,64,128]{4,3,2,1,0:T(8,128)(2,1)}, u32[]{:S(2)}, u32[]{:S(2)}) async-start(bf16[128,2,1,64,128]{4,3,2,1,0:T(8,128)(2,1)} %bitcast.101), calls=%async_computation.1 | async-start | bytes 8388608 | tf_op jit(solution)/shard_map/all_to_all | solution.py:86
  161.2 87.2 %collective-permute-start.1 = (bf16[128,2,128]{2,0,1:T(8,128)(2,1)S(1)}, bf16[128,2,128]{2,0,1:T(8,128)(2,1)S(1)}, u32[]{:S(2)}, u32[]{:S(2)}) collective-permute-start(bf16[128,2,128]{2,0,1:T(8,128)(2,1)S(1)} %copy.122), channel_id=1, source_target_pairs={{0,4},{4,8},{8,12},{12,16},{16,20},{20,24},{24,28},{28,32},{32,36}... | collective-permute-start | bytes 196616 | tf_op jit(solution)/shard_map/ppermute | solution.py:14
  164.9 86.0 %collective-permute-start = (bf16[128,2,128]{0,2,1:T(8,128)(2,1)S(1)}, bf16[128,2,128]{0,2,1:T(8,128)(2,1)S(1)}, u32[]{:S(2)}, u32[]{:S(2)}) collective-permute-start(bf16[128,2,128]{0,2,1:T(8,128)(2,1)S(1)} %copy.120), channel_id=1, source_target_pairs={{0,4},{4,8},{8,12},{12,16},{16,20},{20,24},{24,28},{28,32},{32,36}... | collective-permute-start | bytes 196616 | tf_op jit(solution)/shard_map/ppermute | solution.py:14
where the time goes:
time: 283 us; the launch traced here: 279 us
  waiting for transfers between devices  186 us (66%)
  starting transfers between devices  47.8 us (17%)
  local copies, waits for them, and re-layouts  17.2 us (6%)
  blocking collectives  10.9 us (4%)
  matrix products  10.4 us (4%)
  other arithmetic  6.33 us (2%)
    all_to_all x1, waiting for transfers between devices, on_device(): lax.all_to_all(found_keys, 'seq', split_axis=0, concat_axis=0, tiled=True)  93.6 us
    ppermute x2, waiting for transfers between devices, from_behind(): return lax.ppermute(value, axis, pairs)  82.6 us
    all_to_all x1, starting transfers between devices, on_device(): lax.all_to_all(requests, 'seq', split_axis=0, concat_axis=0, tiled=True)  18.4 us
    all_to_all x1, starting transfers between devices, on_device(): lax.all_to_all(found_values, 'seq', split_axis=0, concat_axis=0, tiled=True)  16.6 us
    all_to_all x1, blocking collectives, on_device(): lax.all_to_all(mixed, 'head', split_axis=0, concat_axis=1, tiled=True)  10.9 us
    all_to_all x1, waiting for transfers between devices, on_device(): lax.all_to_all(requests, 'seq', split_axis=0, concat_axis=0, tiled=True)  10.3 us
    all_to_all x1, starting transfers between devices, on_device(): lax.all_to_all(found_keys, 'seq', split_axis=0, concat_axis=0, tiled=True)  7.02 us
    ppermute x2, starting transfers between devices, from_behind(): return lax.ppermute(value, axis, pairs)  5.78 us
  transfers between devices with their start and end apart: 5, of which 4 were waited for; matrix products, arithmetic and copies ran while one was open for 5% of the time, Pallas kernels for 0%

commit v1 on v0

v1 whole, which is shorter than its diff:
```python
import functools
import math

import jax
import jax.numpy as jnp
from jax import lax
from jax.experimental import pallas as pl
from jax.experimental.pallas import tpu as pltpu
from jax.sharding import Mesh
from jax.sharding import PartitionSpec as P

Z, Y, X = 8, 8, 4
LINE = 8
BLOCK = 64
TOPK = 32
BLK_DEV = 16
HEAD = 128
ROWS = 512
QROWS = ROWS + 16
CHUNK = 2 * BLK_DEV * BLOCK
CHUNKS = 2 * LINE
LISTS = 2 * LINE
OROWS = HEAD + 16
STEP = 4
LOWEST = -3.0e38
EXPO = HEAD**-0.5 * math.log2(math.e)
SEQ = ("z", "y", "core")


def seq_index(z, y, core):
    return (z * Y + y) * 2 + core


Y_LINES = [[[seq_index(z, y, core) for y in range(Y)] for z in range(Z)] for core in range(2)]
Z_LINES = [[[seq_index(z, y, core) for z in range(Z)] for y in range(Y)] for core in range(2)]
KV_LINES = Y_LINES[0] + Z_LINES[1]
Q_LINES = Z_LINES[0] + Y_LINES[1]


def along(value, by):
    pairs = [(line[i], line[(i + by) % LINE]) for line in KV_LINES for i in range(LINE)]
    return lax.ppermute(value, SEQ, pairs)


def window_kernel(first_ref, q_ref, k_ref, v_ref, o_ref):
    for rc in range(2):
        s = lax.dot_general(
            k_ref[pl.ds(128 * rc, 256), :],
            q_ref[rc, :ROWS, :],
            (((1,), (1,)), ((), ())),
            preferred_element_type=jnp.float32,
        )
        kpos = lax.broadcasted_iota(jnp.int32, s.shape, 0) - 128
        qpos = lax.broadcasted_iota(jnp.int32, s.shape, 1) & 127
        allowed = (kpos <= qpos) & (kpos > qpos - 128)
        if rc == 0:
            allowed = allowed & ((kpos >= 0) | (first_ref[0] == 0))
        s = jnp.where(allowed, s, LOWEST)
        top = jnp.max(s, axis=0, keepdims=True)
        p = jnp.exp2((s - top) * EXPO)
        total = jnp.sum(p, axis=0, keepdims=True)
        out = lax.dot_general(
            v_ref[pl.ds(128 * rc, 256), :],
            p.astype(jnp.bfloat16),
            (((0,), (0,)), ((), ())),
            preferred_element_type=jnp.float32,
        )
        o_ref[rc] = out / total


def memory_kernel(count_ref, place_ref, q_ref, *rest):
    chunks = rest[:CHUNKS]
    o_ref, kv, acc, top_s, sum_s, sems = rest[CHUNKS:]
    copies = [
        pltpu.make_async_copy(chunks[j], kv.at[pl.ds(j * CHUNK, CHUNK)], sems.at[j])
        for j in range(CHUNKS)
    ]
    for copy in copies:
        copy.start()
    for copy in copies:
        copy.wait()

    def one_list(index, carry):
        count = count_ref[index]
        top_s[...] = jnp.full((1, ROWS), LOWEST, jnp.float32)
        sum_s[...] = jnp.zeros((1, ROWS), jnp.float32)
        acc[...] = jnp.zeros((HEAD, ROWS), jnp.float32)

        def one_step(step, inner):
            places = [pl.multiple_of(place_ref[index * BLK_DEV + step * STEP + i], BLOCK) for i in range(STEP)]
            keys = jnp.concatenate([kv[pl.ds(at, BLOCK), :] for at in places], axis=0)
            values = jnp.concatenate(
                [kv[pl.ds(at + BLK_DEV * BLOCK, BLOCK), :] for at in places], axis=0
            )
            s = lax.dot_general(
                keys, q_ref[index, :ROWS, :], (((1,), (1,)), ((), ())), preferred_element_type=jnp.float32
            )
            rows = lax.broadcasted_iota(jnp.int32, s.shape, 0)
            s = jnp.where(rows < (count - step * STEP) * BLOCK, s, LOWEST)
            top = jnp.maximum(top_s[...], jnp.max(s, axis=0, keepdims=True))
            p = jnp.exp2((s - top) * EXPO)
            alpha = jnp.exp2((top_s[...] - top) * EXPO)
            sum_s[...] = sum_s[...] * alpha + jnp.sum(p, axis=0, keepdims=True)
            acc[...] = acc[...] * alpha + lax.dot_general(
                values, p.astype(jnp.bfloat16), (((0,), (0,)), ((), ())), preferred_element_type=jnp.float32
            )
            top_s[...] = top
            return inner

        lax.fori_loop(0, (count + STEP - 1) // STEP, one_step, 0)
        total = sum_s[...]
        some = total > 0.0
        safe = jnp.where(some, total, 1.0)
        o_ref[index, :HEAD, :] = (acc[...] / safe).astype(jnp.bfloat16)
        level = jnp.where(some, top_s[...] * EXPO + jnp.log2(safe), LOWEST)
        high = level.astype(jnp.bfloat16).astype(jnp.float32)
        mid = (level - high).astype(jnp.bfloat16).astype(jnp.float32)
        low = level - high - mid
        rows = lax.broadcasted_iota(jnp.int32, (16, ROWS), 0)
        pieces = jnp.where(rows == 0, high, jnp.where(rows == 1, mid, jnp.where(rows == 2, low, 0.0)))
        o_ref[index, HEAD:, :] = pieces.astype(jnp.bfloat16)
        return carry

    lax.fori_loop(0, LISTS, one_list, 0)


def merge_kernel(part_ref, window_ref, gate_ref, o_ref):
    gate = gate_ref[...]
    for rc in range(2):
        levels = []
        for i in range(LINE):
            pieces = part_ref[i, rc, HEAD:, :].astype(jnp.float32)
            levels.append(pieces[0:1, :] + pieces[1:2, :] + pieces[2:3, :])
        top = functools.reduce(jnp.maximum, levels)
        shares = [jnp.exp2(level - top) for level in levels]
        total = functools.reduce(jnp.add, shares)
        mixed = (1.0 - gate) * window_ref[rc]
        scale = gate / total
        for i in range(LINE):
            mixed = mixed + part_ref[i, rc, :HEAD, :].astype(jnp.float32) * (shares[i] * scale)
        for g in range(4):
            flat = mixed[:, g * 128 : (g + 1) * 128].T.astype(jnp.bfloat16)
            for x in range(X):
                o_ref[x * 2 + rc, :, g * 128 : (g + 1) * 128] = flat[x * 32 : (x + 1) * 32, :]


def on_device(queries, keys, values, mem_keys, mem_values, mem_ids, gate_logits):
    z, y, core = lax.axis_index("z"), lax.axis_index("y"), lax.axis_index("core")
    first_core = core == 0

    def mine_and_other(array):
        return jnp.where(first_core, array[0], array[1]), jnp.where(first_core, array[1], array[0])

    def by_core(mine, other):
        return jnp.where(first_core, mine, other), jnp.where(first_core, other, mine)

    mk_mine, mk_other = mine_and_other(mem_keys.transpose(1, 0, 2))
    mv_mine, mv_other = mine_and_other(mem_values.transpose(1, 0, 2))
    chunk_a = jnp.concatenate([mk_mine, mv_mine], axis=0)
    q_mine, q_other = mine_and_other(
        queries.reshape(128, 2, 4, HEAD).transpose(1, 2, 0, 3).reshape(2, ROWS, HEAD)
    )
    ids = jnp.concatenate([mem_ids // 64, mem_ids % 64], axis=2).astype(jnp.bfloat16)
    ids = jnp.pad(ids, ((0, 0), (0, 15), (0, HEAD - 2 * TOPK)))
    ids_mine, ids_other = mine_and_other(ids)
    k_mine, k_other = mine_and_other(keys.transpose(1, 0, 2))
    v_mine, v_other = mine_and_other(values.transpose(1, 0, 2))
    swap = [(0, 1), (1, 0)]
    small = lax.ppermute(
        jnp.concatenate([q_other, ids_other, k_other, v_other], axis=0), "core", swap
    )
    chunk_b = lax.ppermute(jnp.concatenate([mk_other, mv_other], axis=0), "core", swap)

    q_list = jnp.stack(by_core(jnp.concatenate([q_mine, ids_mine], axis=0), small[:QROWS]))
    gathered = lax.all_gather(q_list, SEQ, axis_index_groups=Q_LINES, tiled=True)

    parts = {("a", 0): chunk_a, ("b", 0): chunk_b}
    for hop in range(1, 4):
        for name in ("a", "b"):
            parts[name, -hop % LINE] = along(parts[name, (1 - hop) % LINE], 1)
            parts[name, hop] = along(parts[name, hop - 1], -1)
    parts["a", 4] = along(parts["a", 5], 1)
    parts["b", 4] = along(parts["b", 3], -1)
    chunks = [parts["a", d] for d in range(LINE)] + [parts["b", d] for d in range(LINE)]

    k_first, k_second = by_core(k_mine, small[QROWS : QROWS + 128])
    v_first, v_second = by_core(v_mine, small[QROWS + 128 :])
    chips = Z * Y
    onward = [(2 * i + c, 2 * i + 2 + c) for i in range(chips - 1) for c in range(2)]
    before = lax.ppermute(jnp.concatenate([k_second, v_second], axis=0), SEQ, onward)
    near_keys = jnp.concatenate([before[:128], k_first, k_second], axis=0)
    near_values = jnp.concatenate([before[128:], v_first, v_second], axis=0)
    is_first = ((z == 0) & (y == 0)).astype(jnp.int32).reshape(1)
    window = pl.pallas_call(
        window_kernel,
        out_shape=jax.ShapeDtypeStruct((2, HEAD, ROWS), jnp.float32),
        grid_spec=pltpu.PrefetchScalarGridSpec(
            num_scalar_prefetch=1,
            grid=(1,),
            in_specs=[
                pl.BlockSpec((2, QROWS, HEAD), lambda i, s: (0, 0, 0)),
                pl.BlockSpec((384, HEAD), lambda i, s: (0, 0)),
                pl.BlockSpec((384, HEAD), lambda i, s: (0, 0)),
            ],
            out_specs=pl.BlockSpec((2, HEAD, ROWS), lambda i, s: (0, 0, 0)),
        ),
        compiler_params=pltpu.CompilerParams(vmem_limit_bytes=24 << 20),
        cost_estimate=pl.CostEstimate(
            flops=4 * 2 * ROWS * 256 * HEAD, bytes_accessed=1 << 20, transcendentals=2 * ROWS * 256
        ),
        name="window",
    )(is_first, q_list, near_keys, near_values)

    coded = gathered[:, ROWS, : 2 * TOPK].astype(jnp.int32)
    wanted = coded[:, :TOPK] * 64 + coded[:, TOPK:]
    owner, local = wanted // BLK_DEV, wanted % BLK_DEV
    owner_z, owner_y, owner_core = owner // (2 * Y), (owner // 2) % Y, owner % 2
    here = jnp.where(first_core, owner_z == z, owner_y == y)
    delta = jnp.where(first_core, owner_y - y, owner_z - z) % LINE
    slot = delta + jnp.where(owner_core == core, 0, LINE)
    place = slot * CHUNK + local * BLOCK
    rank = jnp.sum(
        (here[:, None, :] & (jnp.arange(TOPK)[None, None, :] < jnp.arange(TOPK)[None, :, None])).astype(jnp.int32),
        axis=2,
    )
    match = here[:, :, None] & (rank[:, :, None] == jnp.arange(BLK_DEV)[None, None, :])
    places = jnp.sum(jnp.where(match, place[:, :, None], 0), axis=1)
    counts = jnp.sum(here.astype(jnp.int32), axis=1)

    partial = pl.pallas_call(
        memory_kernel,
        out_shape=jax.ShapeDtypeStruct((LISTS, OROWS, ROWS), jnp.bfloat16),
        grid_spec=pltpu.PrefetchScalarGridSpec(
            num_scalar_prefetch=2,
            grid=(1,),
            in_specs=[pl.BlockSpec((LISTS, QROWS, HEAD), lambda i, s, t: (0, 0, 0))]
            + [pl.BlockSpec(memory_space=pl.ANY)] * CHUNKS,
            out_specs=pl.BlockSpec((LISTS, OROWS, ROWS), lambda i, s, t: (0, 0, 0)),
            scratch_shapes=[
                pltpu.VMEM((CHUNKS * CHUNK, HEAD), jnp.bfloat16),
                pltpu.VMEM((HEAD, ROWS), jnp.float32),
                pltpu.VMEM((1, ROWS), jnp.float32),
                pltpu.VMEM((1, ROWS), jnp.float32),
                pltpu.SemaphoreType.DMA((CHUNKS,)),
            ],
        ),
        compiler_params=pltpu.CompilerParams(vmem_limit_bytes=40 << 20),
        cost_estimate=pl.CostEstimate(
            flops=4 * 64 * ROWS * BLOCK * HEAD, bytes_accessed=12 << 20, transcendentals=64 * ROWS * BLOCK
        ),
        name="memory",
    )(counts, places.reshape(-1), gathered, *chunks)

    returned = lax.all_to_all(
        partial, SEQ, split_axis=0, concat_axis=0, axis_index_groups=Q_LINES, tiled=True
    ).reshape(LINE, 2, OROWS, ROWS)
    gate = jax.nn.sigmoid(gate_logits).reshape(2, 4)
    gate = jnp.repeat(jnp.where(first_core, gate[0], gate[1]), 128)[None, :]
    mixed = pl.pallas_call(
        merge_kernel,
        out_shape=jax.ShapeDtypeStruct((2 * X, 32, ROWS), jnp.bfloat16),
        compiler_params=pltpu.CompilerParams(vmem_limit_bytes=24 << 20),
        cost_estimate=pl.CostEstimate(flops=1 << 22, bytes_accessed=4 << 20, transcendentals=1 << 13),
        name="merge",
    )(returned, window, gate)
    rows = lax.all_to_all(mixed, ("head", "core"), split_axis=0, concat_axis=0, tiled=True)
    return rows.transpose(1, 0, 2).reshape(32, 2 * X * ROWS)


def solution(mesh):
    fine = Mesh(mesh.devices.reshape(Z, Y, 2, X), ("z", "y", "core", "head"))
    placed = (
        P(SEQ, "head", None),
        P(SEQ, "head", None),
        P(SEQ, "head", None),
        P(SEQ, "head", None),
        P(SEQ, "head", None),
        P("head", SEQ, None),
        P("head"),
    )
    return jax.shard_map(
        on_device, mesh=fine, in_specs=placed, out_specs=P(SEQ + ("head",), None), check_vma=False
    )
```

time: 283 us -> 171 us (0.60)
  waiting for transfers between devices: 186 us -> 45.5 us
  starting transfers between devices: 47.8 us -> 67.4 us
  Pallas kernels: 0 us -> 16.1 us
  between operations: 0.27 us -> 13.8 us
  local copies, waits for them, and re-layouts: 17.2 us -> 6.76 us
  matrix products: 10.4 us -> 0 us
  blocking collectives: 10.9 us -> 15.5 us
    all_to_all x3 -> x1, waiting for transfers between devices: 104 us -> 5.53 us  [on_device(): lax.all_to_all(partial, SEQ, split_axis=0, concat_axis=0, axis_index_grou...]
    ppermute x2 -> x17, starting transfers between devices: 5.78 us -> 59.4 us  [the longest x14 45 us: along(): return lax.ppermute(value, SEQ, pairs)]
    ppermute x2 -> x17, waiting for transfers between devices: 82.6 us -> 39.9 us  [the longest x1 22.9 us: on_device(): lax.ppermute(jnp.concatenate([k_second, v_second], axis=0), SEQ, onward)]
    all_to_all x3 -> x1, starting transfers between devices: 42 us -> 7.97 us  [on_device(): lax.all_to_all(partial, SEQ, split_axis=0, concat_axis=0, axis_index_grou...]
    pallas_call x0 -> x3, Pallas kernels: none -> 16.1 us  [the longest x1 14.6 us: on_device(): pl.pallas_call(memory_kernel, out_shape=jax.ShapeDtypeStruct((LISTS, OROW...]
    gather x4 -> x0, local copies, waits for them, and re-layouts: 12.7 us -> none  [the longest x1 3.36 us: on_device(): found_values = cache_values[head_index, asked]]
    sub x2 -> x0, matrix products: 5.47 us -> none  [attend(): expo = jnp.exp(scores - highest)]
    dot_general x3 -> x0, matrix products: 4.92 us -> none  [the longest x2 4.62 us: attend(): jnp.einsum('kgqs,ksd->qkgd', weights, value_rows, preferred_element_type=...]
  transfers between devices with their start and end apart: 5 -> 19, of which waited for: 4 -> 8; matrix products, arithmetic and copies ran while one was open for 5% -> 1% of each run, Pallas kernels for 0% -> 1%
where the time goes in v1:
time: 171 us; the launch traced here: 169 us
  starting transfers between devices  67.4 us (39%)
  waiting for transfers between devices  45.5 us (27%)
  Pallas kernels  16.1 us (9%)
  blocking collectives  15.5 us (9%)
  between operations  13.8 us (8%)
  local copies, waits for them, and re-layouts  6.76 us (4%)
  other arithmetic  3.7 us (2%)
    ppermute x14, starting transfers between devices, along(): return lax.ppermute(value, SEQ, pairs)  45 us
    ppermute x1, waiting for transfers between devices, on_device(): lax.ppermute(jnp.concatenate([k_second, v_second], axis=0), SEQ, onward)  22.9 us
    ppermute x14, waiting for transfers between devices, along(): return lax.ppermute(value, SEQ, pairs)  16 us
    all_to_all x1, blocking collectives, on_device(): lax.all_to_all(mixed, ('head', 'core'), split_axis=0, concat_axis=0, tile...  15.5 us
    pallas_call x1, Pallas kernels, on_device(): pl.pallas_call(memory_kernel, out_shape=jax.ShapeDtypeStruct((LISTS, OROW...  14.6 us
    ppermute x1, starting transfers between devices, on_device(): lax.ppermute(jnp.concatenate([q_other, ids_other, k_other, v_other], axis...  8.79 us
    all_to_all x1, starting transfers between devices, on_device(): lax.all_to_all(partial, SEQ, split_axis=0, concat_axis=0, axis_index_grou...  7.97 us
    all_to_all x1, waiting for transfers between devices, on_device(): lax.all_to_all(partial, SEQ, split_axis=0, concat_axis=0, axis_index_grou...  5.53 us
  transfers between devices with their start and end apart: 19, of which 8 were waited for; matrix products, arithmetic and copies ran while one was open for 1% of the time, Pallas kernels for 1%

profile of v1, /device:TPU:1, one launch (start us, length us, event | category | flops | bytes accessed | tf_op | source)
XLA Modules:
  0.0 168.8 jit_solution(3401201946748085947)
XLA Ops:
  6.5 0.8 fusion.20
  7.3 0.9 copy.41
  8.2 0.9 copy.40
  9.0 1.0 copy.39
  10.0 0.1 fusion.14
  10.2 8.8 %collective-permute-start = (bf16[784,128]{1,0:T(8,128)(2,1)S(1)}, bf16[784,128]{1,0:T(8,128)(2,1)S(1)}, u32[]{:S(2)}, u32[]{:S(2)}) collective-permute-start(bf16[784,128]{1,0:T(8,128)(2,1)S(1)} %pad_maximum_fusion.3), channel_id=1, source_target_pairs={{0,4},{4,0},{1,5},{5,1},{2,6},{6,2},{3,7},{7,3},{8,12},{12,8},{9,1... | collective-permute-start | bytes 602120 | tf_op jit(solution)/shard_map/ppermute | solution.py:169
  19.0 1.1 collective-permute-done
  20.0 0.1 select_bitcast_fusion.5
  20.1 0.7 pad_maximum_fusion.2.q_ref
  20.8 0.0 all-gather.2.cloned.1.call-update
  20.9 0.1 copy.38
  21.0 0.1 copy.37
  21.0 0.1 select_bitcast_fusion
  21.2 2.3 %collective-permute-start.8 = (bf16[2048,128]{1,0:T(8,128)(2,1)S(1)}, bf16[2048,128]{1,0:T(8,128)(2,1)S(1)}, u32[]{:S(2)}, u32[]{:S(2)}) collective-permute-start(bf16[2048,128]{1,0:T(8,128)(2,1)S(1)} %pad_maximum_fusion.1), channel_id=1, source_target_pairs={{0,4},{4,0},{1,5},{5,1},{2,6},{6,2},{3,7},{7,3},{8,12},{12,8},{9,1... | collective-permute-start | bytes 1572872 | tf_op jit(solution)/shard_map/ppermute | solution.py:172
  23.5 1.9 %collective-permute-start.4 = (bf16[2048,128]{1,0:T(8,128)(2,1)S(1)}, bf16[2048,128]{1,0:T(8,128)(2,1)S(1)}, u32[]{:S(2)}, u32[]{:S(2)}) collective-permute-start(bf16[2048,128]{1,0:T(8,128)(2,1)S(1)} %pad_maximum_fusion.rest_0_), channel_id=1, source_target_pairs={{0,8},{8,16},{16,24},{24,32},{32,40},{40,48},{48,56},{56,0},{64,72... | collective-permute-start | bytes 1572872 | tf_op jit(solution)/shard_map/ppermute | solution.py:42
  25.4 0.0 collective-permute-done.8.rest_8_
  25.4 5.3 %collective-permute-start.9 = (bf16[2048,128]{1,0:T(8,128)(2,1)S(1)}, bf16[2048,128]{1,0:T(8,128)(2,1)S(1)}, u32[]{:S(2)}, u32[]{:S(2)}) collective-permute-start(bf16[2048,128]{1,0:T(8,128)(2,1)S(1)} %collective-permute-done.8.rest_8_), channel_id=1, source_target_pairs={{0,56},{8,0},{16,8},{24,16},{32,24},{40,32},{48,40},{56,48},{64,12... | collective-permute-start | bytes 1572872 | tf_op jit(solution)/shard_map/ppermute | solution.py:42
  30.7 3.4 %collective-permute-start.1 = (bf16[2048,128]{1,0:T(8,128)(2,1)S(1)}, bf16[2048,128]{1,0:T(8,128)(2,1)S(1)}, u32[]{:S(2)}, u32[]{:S(2)}) collective-permute-start(bf16[2048,128]{1,0:T(8,128)(2,1)S(1)} %pad_maximum_fusion.rest_0_), channel_id=1, source_target_pairs={{0,56},{8,0},{16,8},{24,16},{32,24},{40,32},{48,40},{56,48},{64,12... | collective-permute-start | bytes 1572872 | tf_op jit(solution)/shard_map/ppermute | solution.py:42
  34.1 1.4 collective-permute-done.4.rest_7_
  35.5 1.9 %collective-permute-start.5 = (bf16[2048,128]{1,0:T(8,128)(2,1)S(1)}, bf16[2048,128]{1,0:T(8,128)(2,1)S(1)}, u32[]{:S(2)}, u32[]{:S(2)}) collective-permute-start(bf16[2048,128]{1,0:T(8,128)(2,1)S(1)} %collective-permute-done.4.rest_7_), channel_id=1, source_target_pairs={{0,8},{8,16},{16,24},{24,32},{32,40},{40,48},{48,56},{56,0},{64,72... | collective-permute-start | bytes 1572872 | tf_op jit(solution)/shard_map/ppermute | solution.py:42
  37.4 1.9 %collective-permute-start.13 = (bf16[2048,128]{1,0:T(8,128)(2,1)S(1)}, bf16[2048,128]{1,0:T(8,128)(2,1)}, u32[]{:S(2)}, u32[]{:S(2)}) collective-permute-start(bf16[2048,128]{1,0:T(8,128)(2,1)S(1)} %collective-permute-done.8.rest_8_), channel_id=1, source_target_pairs={{0,8},{8,16},{16,24},{24,32},{32,40},{40,48},{48,56},{56,0},{64,72... | collective-permute-start | bytes 1572872 | tf_op jit(solution)/shard_map/ppermute | solution.py:42
  39.4 0.0 collective-permute-done.9.rest_9_
  39.4 4.6 %collective-permute-start.10 = (bf16[2048,128]{1,0:T(8,128)(2,1)S(1)}, bf16[2048,128]{1,0:T(8,128)(2,1)}, u32[]{:S(2)}, u32[]{:S(2)}) collective-permute-start(bf16[2048,128]{1,0:T(8,128)(2,1)S(1)} %collective-permute-done.9.rest_9_), channel_id=1, source_target_pairs={{0,56},{8,0},{16,8},{24,16},{32,24},{40,32},{48,40},{56,48},{64,12... | collective-permute-start | bytes 1572872 | tf_op jit(solution)/shard_map/ppermute | solution.py:42
  44.0 2.0 %collective-permute-done.1.rest_1_ = bf16[2048,128]{1,0:T(8,128)(2,1)S(1)} collective-permute-done((bf16[2048,128]{1,0:T(8,128)(2,1)S(1)}, bf16[2048,128]{1,0:T(8,128)(2,1)S(1)}, u32[]{:S(2)}, u32[]{:S(2)}) %collective-permute-start.1) | collective-permute-done | bytes 524320 | tf_op jit(solution)/shard_map/ppermute | solution.py:42
  46.0 5.4 %collective-permute-start.2 = (bf16[2048,128]{1,0:T(8,128)(2,1)S(1)}, bf16[2048,128]{1,0:T(8,128)(2,1)}, u32[]{:S(2)}, u32[]{:S(2)}) collective-permute-start(bf16[2048,128]{1,0:T(8,128)(2,1)S(1)} %collective-permute-done.1.rest_1_), channel_id=1, source_target_pairs={{0,56},{8,0},{16,8},{24,16},{32,24},{40,32},{48,40},{56,48},{64,12... | collective-permute-start | bytes 1572872 | tf_op jit(solution)/shard_map/ppermute | solution.py:42
  51.4 0.0 collective-permute-done.5.rest_6_
  51.5 1.9 %collective-permute-start.6 = (bf16[2048,128]{1,0:T(8,128)(2,1)S(1)}, bf16[2048,128]{1,0:T(8,128)(2,1)}, u32[]{:S(2)}, u32[]{:S(2)}) collective-permute-start(bf16[2048,128]{1,0:T(8,128)(2,1)S(1)} %collective-permute-done.5.rest_6_), channel_id=1, source_target_pairs={{0,8},{8,16},{16,24},{24,32},{32,40},{40,48},{48,56},{56,0},{64,72... | collective-permute-start | bytes 1572872 | tf_op jit(solution)/shard_map/ppermute | solution.py:42
  53.4 5.4 %collective-permute-done.13.rest_15_ = bf16[2048,128]{1,0:T(8,128)(2,1)} collective-permute-done((bf16[2048,128]{1,0:T(8,128)(2,1)S(1)}, bf16[2048,128]{1,0:T(8,128)(2,1)}, u32[]{:S(2)}, u32[]{:S(2)}) %collective-permute-start.13) | collective-permute-done | bytes 524320 | tf_op jit(solution)/shard_map/ppermute | solution.py:42
  58.8 1.9 %collective-permute-start.14 = (bf16[2048,128]{1,0:T(8,128)(2,1)}, bf16[2048,128]{1,0:T(8,128)(2,1)}, u32[]{:S(2)}, u32[]{:S(2)}) collective-permute-start(bf16[2048,128]{1,0:T(8,128)(2,1)} %collective-permute-done.13.rest_15_), channel_id=1, source_target_pairs={{0,8},{8,16},{16,24},{24,32},{32,40},{40,48},{48,56},{56,0},{64,72... | collective-permute-start | bytes 1572872 | tf_op jit(solution)/shard_map/ppermute | solution.py:42
  60.7 0.0 collective-permute-done.10.rest_10_
  60.8 4.6 %collective-permute-start.11 = (bf16[2048,128]{1,0:T(8,128)(2,1)}, bf16[2048,128]{1,0:T(8,128)(2,1)}, u32[]{:S(2)}, u32[]{:S(2)}) collective-permute-start(bf16[2048,128]{1,0:T(8,128)(2,1)} %collective-permute-done.10.rest_10_), channel_id=1, source_target_pairs={{0,56},{8,0},{16,8},{24,16},{32,24},{40,32},{48,40},{56,48},{64,12... | collective-permute-start | bytes 1572872 | tf_op jit(solution)/shard_map/ppermute | solution.py:42
  65.4 0.0 collective-permute-done.2.rest_2_
  65.4 3.8 %collective-permute-start.3 = (bf16[2048,128]{1,0:T(8,128)(2,1)}, bf16[2048,128]{1,0:T(8,128)(2,1)}, u32[]{:S(2)}, u32[]{:S(2)}) collective-permute-start(bf16[2048,128]{1,0:T(8,128)(2,1)} %collective-permute-done.2.rest_2_), channel_id=1, source_target_pairs={{0,56},{8,0},{16,8},{24,16},{32,24},{40,32},{48,40},{56,48},{64,12... | collective-permute-start | bytes 1572872 | tf_op jit(solution)/shard_map/ppermute | solution.py:42
  69.1 0.0 collective-permute-done.6.rest_5_
  69.1 1.9 %collective-permute-start.7 = (bf16[2048,128]{1,0:T(8,128)(2,1)}, bf16[2048,128]{1,0:T(8,128)(2,1)}, u32[]{:S(2)}, u32[]{:S(2)}) collective-permute-start(bf16[2048,128]{1,0:T(8,128)(2,1)} %collective-permute-done.6.rest_5_), channel_id=1, source_target_pairs={{0,8},{8,16},{16,24},{24,32},{32,40},{40,48},{48,56},{56,0},{64,72... | collective-permute-start | bytes 1572872 | tf_op jit(solution)/shard_map/ppermute | solution.py:42
  71.1 1.5 collective-permute-done.14.rest_14_
  72.6 1.9 %collective-permute-start.15 = (bf16[2048,128]{1,0:T(8,128)(2,1)}, bf16[2048,128]{1,0:T(8,128)(2,1)}, u32[]{:S(2)}, u32[]{:S(2)}) collective-permute-start(bf16[2048,128]{1,0:T(8,128)(2,1)} %collective-permute-done.14.rest_14_), channel_id=1, source_target_pairs={{0,8},{8,16},{16,24},{24,32},{32,40},{40,48},{48,56},{56,0},{64,72... | collective-permute-start | bytes 1572872 | tf_op jit(solution)/shard_map/ppermute | solution.py:42
  74.5 0.0 collective-permute-done.11.rest_11_
  74.5 4.6 %collective-permute-start.12 = (bf16[2048,128]{1,0:T(8,128)(2,1)}, bf16[2048,128]{1,0:T(8,128)(2,1)}, u32[]{:S(2)}, u32[]{:S(2)}) collective-permute-start(bf16[2048,128]{1,0:T(8,128)(2,1)} %collective-permute-done.11.rest_11_), channel_id=1, source_target_pairs={{0,56},{8,0},{16,8},{24,16},{32,24},{40,32},{48,40},{56,48},{64,12... | collective-permute-start | bytes 1572872 | tf_op jit(solution)/shard_map/ppermute | solution.py:42
  79.1 0.0 all-gather.2.cloned.1.call-done.q_ref
  79.1 0.8 slice_convert_fusion
  79.9 0.1 fusion.11
  80.0 0.1 convert_reduce_fusion.1
  80.2 0.4 convert_reduce_fusion
  80.5 0.3 select_reduce_fusion
  80.9 0.1 reshape.101.place_ref
  80.9 0.0 collective-permute-done.3.rest_3_
  81.0 0.0 collective-permute-done.7.rest_4_
  81.0 5.5 %collective-permute-done.15.rest_13_ = bf16[2048,128]{1,0:T(8,128)(2,1)} collective-permute-done((bf16[2048,128]{1,0:T(8,128)(2,1)}, bf16[2048,128]{1,0:T(8,128)(2,1)}, u32[]{:S(2)}, u32[]{:S(2)}) %collective-permute-start.15) | collective-permute-done | bytes 524320 | tf_op jit(solution)/shard_map/ppermute | solution.py:42
  86.5 0.0 collective-permute-done.12.rest_12_
  86.5 1.6 copy-done.2
  88.1 14.6 %memory.1 = bf16[16,144,512]{2,1,0:T(8,128)(2,1)S(1)} custom-call(s32[16]{0:T(128)S(1)} %get-tuple-element.7.count_ref, s32[256]{0:T(256)S(1)} %reshape.101.place_ref, bf16[16,528,128]{2,1,0:T(8,128)(2,1)S(1)} %copy-done.2, bf16[2048,128]{1,0:T(8,128)(2,1)S(1)} %pad_maximum_fusion.rest_0_, bf16[2048,128]{1,0:T(8,128)(2,1)S(1)} %collective-permute-done.1.rest_1_, ...), custom_call_target="tpu_custom_call" | custom-call | flops 1073741824 | bytes 12582912 | tf_op jit(solution)/shard_map/memory/pallas_call | solution.py:230
  102.8 1.4 copy-done
  104.2 8.0 %all-to-all-start = ((bf16[16,144,512]{2,1,0:T(8,128)(2,1)}), bf16[16,144,512]{2,1,0:T(8,128)(2,1)S(1)}, u32[]{:S(2)}, u32[]{:S(2)}) async-start(bf16[16,144,512]{2,1,0:T(8,128)(2,1)} %copy-done), calls=%async_computation | async-start | bytes 4718592 | tf_op jit(solution)/shard_map/all_to_all | solution.py:254
  112.2 0.0 copy-done.5
  112.2 3.4 %collective-permute-start.16 = (bf16[256,128]{1,0:T(8,128)(2,1)S(1)}, bf16[256,128]{1,0:T(8,128)(2,1)S(1)}, u32[]{:S(2)}, u32[]{:S(2)}) collective-permute-start(bf16[256,128]{1,0:T(8,128)(2,1)S(1)} %pad_maximum_fusion.7), channel_id=1, source_target_pairs={{0,8},{4,12},{8,16},{12,20},{16,24},{20,28},{24,32},{28,36},{32,40... | collective-permute-start | bytes 196616 | tf_op jit(solution)/shard_map/ppermute | solution.py:190
  115.6 0.1 broadcast_select_fusion.4
  115.7 22.9 %collective-permute-done.16 = bf16[256,128]{1,0:T(8,128)(2,1)S(1)} collective-permute-done((bf16[256,128]{1,0:T(8,128)(2,1)S(1)}, bf16[256,128]{1,0:T(8,128)(2,1)S(1)}, u32[]{:S(2)}, u32[]{:S(2)}) %collective-permute-start.16) | collective-permute-done | bytes 65568 | tf_op jit(solution)/shard_map/ppermute | solution.py:190
  138.6 0.8 window.1.window_ref
  139.4 5.5 %all-to-all-done = bf16[16,144,512]{2,1,0:T(8,128)(2,1)S(1)} async-done(((bf16[16,144,512]{2,1,0:T(8,128)(2,1)}), bf16[16,144,512]{2,1,0:T(8,128)(2,1)S(1)}, u32[]{:S(2)}, u32[]{:S(2)}) %all-to-all-start) | async-done | bytes 2359328 | tf_op jit(solution)/shard_map/all_to_all | solution.py:254
  145.0 0.1 broadcast_in_dim.28
  145.0 0.7 merge.1
  145.7 15.5 %all_to_all.10 = bf16[8,32,512]{2,1,0:T(8,128)(2,1)S(1)} all-to-all(bf16[8,32,512]{2,1,0:T(8,128)(2,1)S(1)} %merge.1), channel_id=1, replica_groups=mesh['z'=8,'y'=8,'core'=2,'head'=4] {'head','core'}, dimensions={0} | all-to-all | bytes 524288 | tf_op jit(solution)/shard_map/all_to_all | solution.py:266
  161.2 0.7 copy.31
  (24 shorter events, 0.2 us)
Async XLA Ops:
  6.5 14.3 %copy-start.3 = (bf16[1024,2,128]{2,1,0:T(2,128)(2,1)S(1)}, bf16[1024,2,128]{2,1,0:T(2,128)(2,1)}, u32[]{:S(2)}) copy-start(bf16[1024,2,128]{2,1,0:T(2,128)(2,1)} %param.10) | copy-start | bytes 1572868
  6.5 14.4 %copy-start.4 = (bf16[1024,2,128]{2,1,0:T(2,128)(2,1)S(1)}, bf16[1024,2,128]{2,1,0:T(2,128)(2,1)}, u32[]{:S(2)}) copy-start(bf16[1024,2,128]{2,1,0:T(2,128)(2,1)} %param.11) | copy-start | bytes 1572868
  6.5 72.6 %all-gather.2.cloned.1.call-start = ((), (), s32[]{:S(2)}) async-start(), calls=%async_computation.2 | async-start | bytes 2433024 | tf_op jit(solution)/shard_map/all_gather | solution.py:175
  10.2 9.8 %collective-permute-start = (bf16[784,128]{1,0:T(8,128)(2,1)S(1)}, bf16[784,128]{1,0:T(8,128)(2,1)S(1)}, u32[]{:S(2)}, u32[]{:S(2)}) collective-permute-start(bf16[784,128]{1,0:T(8,128)(2,1)S(1)} %pad_maximum_fusion.3), channel_id=1, source_target_pairs={{0,4},{4,0},{1,5},{5,1},{2,6},{6,2},{3,7},{7,3},{8,12},{12,8},{9,1... | collective-permute-start | bytes 602120 | tf_op jit(solution)/shard_map/ppermute | solution.py:169
  21.2 4.3 %collective-permute-start.8 = (bf16[2048,128]{1,0:T(8,128)(2,1)S(1)}, bf16[2048,128]{1,0:T(8,128)(2,1)S(1)}, u32[]{:S(2)}, u32[]{:S(2)}) collective-permute-start(bf16[2048,128]{1,0:T(8,128)(2,1)S(1)} %pad_maximum_fusion.1), channel_id=1, source_target_pairs={{0,4},{4,0},{1,5},{5,1},{2,6},{6,2},{3,7},{7,3},{8,12},{12,8},{9,1... | collective-permute-start | bytes 1572872 | tf_op jit(solution)/shard_map/ppermute | solution.py:172
  23.5 12.0 %collective-permute-start.4 = (bf16[2048,128]{1,0:T(8,128)(2,1)S(1)}, bf16[2048,128]{1,0:T(8,128)(2,1)S(1)}, u32[]{:S(2)}, u32[]{:S(2)}) collective-permute-start(bf16[2048,128]{1,0:T(8,128)(2,1)S(1)} %pad_maximum_fusion.rest_0_), channel_id=1, source_target_pairs={{0,8},{8,16},{16,24},{24,32},{32,40},{40,48},{48,56},{56,0},{64,72... | collective-permute-start | bytes 1572872 | tf_op jit(solution)/shard_map/ppermute | solution.py:42
  25.4 13.9 %collective-permute-start.9 = (bf16[2048,128]{1,0:T(8,128)(2,1)S(1)}, bf16[2048,128]{1,0:T(8,128)(2,1)S(1)}, u32[]{:S(2)}, u32[]{:S(2)}) collective-permute-start(bf16[2048,128]{1,0:T(8,128)(2,1)S(1)} %collective-permute-done.8.rest_8_), channel_id=1, source_target_pairs={{0,56},{8,0},{16,8},{24,16},{32,24},{40,32},{48,40},{56,48},{64,12... | collective-permute-start | bytes 1572872 | tf_op jit(solution)/shard_map/ppermute | solution.py:42
  30.7 15.3 %collective-permute-start.1 = (bf16[2048,128]{1,0:T(8,128)(2,1)S(1)}, bf16[2048,128]{1,0:T(8,128)(2,1)S(1)}, u32[]{:S(2)}, u32[]{:S(2)}) collective-permute-start(bf16[2048,128]{1,0:T(8,128)(2,1)S(1)} %pad_maximum_fusion.rest_0_), channel_id=1, source_target_pairs={{0,56},{8,0},{16,8},{24,16},{32,24},{40,32},{48,40},{56,48},{64,12... | collective-permute-start | bytes 1572872 | tf_op jit(solution)/shard_map/ppermute | solution.py:42
  35.5 15.9 %collective-permute-start.5 = (bf16[2048,128]{1,0:T(8,128)(2,1)S(1)}, bf16[2048,128]{1,0:T(8,128)(2,1)S(1)}, u32[]{:S(2)}, u32[]{:S(2)}) collective-permute-start(bf16[2048,128]{1,0:T(8,128)(2,1)S(1)} %collective-permute-done.4.rest_7_), channel_id=1, source_target_pairs={{0,8},{8,16},{16,24},{24,32},{32,40},{40,48},{48,56},{56,0},{64,72... | collective-permute-start | bytes 1572872 | tf_op jit(solution)/shard_map/ppermute | solution.py:42
  37.4 21.4 %collective-permute-start.13 = (bf16[2048,128]{1,0:T(8,128)(2,1)S(1)}, bf16[2048,128]{1,0:T(8,128)(2,1)}, u32[]{:S(2)}, u32[]{:S(2)}) collective-permute-start(bf16[2048,128]{1,0:T(8,128)(2,1)S(1)} %collective-permute-done.8.rest_8_), channel_id=1, source_target_pairs={{0,8},{8,16},{16,24},{24,32},{32,40},{40,48},{48,56},{56,0},{64,72... | collective-permute-start | bytes 1572872 | tf_op jit(solution)/shard_map/ppermute | solution.py:42
  39.4 21.4 %collective-permute-start.10 = (bf16[2048,128]{1,0:T(8,128)(2,1)S(1)}, bf16[2048,128]{1,0:T(8,128)(2,1)}, u32[]{:S(2)}, u32[]{:S(2)}) collective-permute-start(bf16[2048,128]{1,0:T(8,128)(2,1)S(1)} %collective-permute-done.9.rest_9_), channel_id=1, source_target_pairs={{0,56},{8,0},{16,8},{24,16},{32,24},{40,32},{48,40},{56,48},{64,12... | collective-permute-start | bytes 1572872 | tf_op jit(solution)/shard_map/ppermute | solution.py:42
  46.0 19.3 %collective-permute-start.2 = (bf16[2048,128]{1,0:T(8,128)(2,1)S(1)}, bf16[2048,128]{1,0:T(8,128)(2,1)}, u32[]{:S(2)}, u32[]{:S(2)}) collective-permute-start(bf16[2048,128]{1,0:T(8,128)(2,1)S(1)} %collective-permute-done.1.rest_1_), channel_id=1, source_target_pairs={{0,56},{8,0},{16,8},{24,16},{32,24},{40,32},{48,40},{56,48},{64,12... | collective-permute-start | bytes 1572872 | tf_op jit(solution)/shard_map/ppermute | solution.py:42
  51.5 17.7 %collective-permute-start.6 = (bf16[2048,128]{1,0:T(8,128)(2,1)S(1)}, bf16[2048,128]{1,0:T(8,128)(2,1)}, u32[]{:S(2)}, u32[]{:S(2)}) collective-permute-start(bf16[2048,128]{1,0:T(8,128)(2,1)S(1)} %collective-permute-done.5.rest_6_), channel_id=1, source_target_pairs={{0,8},{8,16},{16,24},{24,32},{32,40},{40,48},{48,56},{56,0},{64,72... | collective-permute-start | bytes 1572872 | tf_op jit(solution)/shard_map/ppermute | solution.py:42
  58.8 13.8 %collective-permute-start.14 = (bf16[2048,128]{1,0:T(8,128)(2,1)}, bf16[2048,128]{1,0:T(8,128)(2,1)}, u32[]{:S(2)}, u32[]{:S(2)}) collective-permute-start(bf16[2048,128]{1,0:T(8,128)(2,1)} %collective-permute-done.13.rest_15_), channel_id=1, source_target_pairs={{0,8},{8,16},{16,24},{24,32},{32,40},{40,48},{48,56},{56,0},{64,72... | collective-permute-start | bytes 1572872 | tf_op jit(solution)/shard_map/ppermute | solution.py:42
  60.8 13.8 %collective-permute-start.11 = (bf16[2048,128]{1,0:T(8,128)(2,1)}, bf16[2048,128]{1,0:T(8,128)(2,1)}, u32[]{:S(2)}, u32[]{:S(2)}) collective-permute-start(bf16[2048,128]{1,0:T(8,128)(2,1)} %collective-permute-done.10.rest_10_), channel_id=1, source_target_pairs={{0,56},{8,0},{16,8},{24,16},{32,24},{40,32},{48,40},{56,48},{64,12... | collective-permute-start | bytes 1572872 | tf_op jit(solution)/shard_map/ppermute | solution.py:42
  65.4 15.6 %collective-permute-start.3 = (bf16[2048,128]{1,0:T(8,128)(2,1)}, bf16[2048,128]{1,0:T(8,128)(2,1)}, u32[]{:S(2)}, u32[]{:S(2)}) collective-permute-start(bf16[2048,128]{1,0:T(8,128)(2,1)} %collective-permute-done.2.rest_2_), channel_id=1, source_target_pairs={{0,56},{8,0},{16,8},{24,16},{32,24},{40,32},{48,40},{56,48},{64,12... | collective-permute-start | bytes 1572872 | tf_op jit(solution)/shard_map/ppermute | solution.py:42
  69.1 11.8 %collective-permute-start.7 = (bf16[2048,128]{1,0:T(8,128)(2,1)}, bf16[2048,128]{1,0:T(8,128)(2,1)}, u32[]{:S(2)}, u32[]{:S(2)}) collective-permute-start(bf16[2048,128]{1,0:T(8,128)(2,1)} %collective-permute-done.6.rest_5_), channel_id=1, source_target_pairs={{0,8},{8,16},{16,24},{24,32},{32,40},{40,48},{48,56},{56,0},{64,72... | collective-permute-start | bytes 1572872 | tf_op jit(solution)/shard_map/ppermute | solution.py:42
  72.6 13.9 %collective-permute-start.15 = (bf16[2048,128]{1,0:T(8,128)(2,1)}, bf16[2048,128]{1,0:T(8,128)(2,1)}, u32[]{:S(2)}, u32[]{:S(2)}) collective-permute-start(bf16[2048,128]{1,0:T(8,128)(2,1)} %collective-permute-done.14.rest_14_), channel_id=1, source_target_pairs={{0,8},{8,16},{16,24},{24,32},{32,40},{40,48},{48,56},{56,0},{64,72... | collective-permute-start | bytes 1572872 | tf_op jit(solution)/shard_map/ppermute | solution.py:42
  74.5 12.0 %collective-permute-start.12 = (bf16[2048,128]{1,0:T(8,128)(2,1)}, bf16[2048,128]{1,0:T(8,128)(2,1)}, u32[]{:S(2)}, u32[]{:S(2)}) collective-permute-start(bf16[2048,128]{1,0:T(8,128)(2,1)} %collective-permute-done.11.rest_11_), channel_id=1, source_target_pairs={{0,56},{8,0},{16,8},{24,16},{32,24},{40,32},{48,40},{56,48},{64,12... | collective-permute-start | bytes 1572872 | tf_op jit(solution)/shard_map/ppermute | solution.py:42
  86.5 1.6 copy-start.2
  102.8 1.4 copy-start
  104.2 8.0 %copy-start.5 = (f32[8]{0:T(128)S(1)}, f32[8]{0:T(128)}, u32[]{:S(2)}) copy-start(f32[8]{0:T(128)} %param.13) | copy-start | bytes 100
  104.2 34.4 %copy-start.1 = (bf16[2,528,128]{2,1,0:T(8,128)(2,1)S(1)}, bf16[2,528,128]{2,1,0:T(8,128)(2,1)}, u32[]{:S(2)}) copy-start(bf16[2,528,128]{2,1,0:T(8,128)(2,1)} %pad_maximum_fusion.2.q_ref) | copy-start | bytes 811012
  104.2 40.8 %all-to-all-start = ((bf16[16,144,512]{2,1,0:T(8,128)(2,1)}), bf16[16,144,512]{2,1,0:T(8,128)(2,1)S(1)}, u32[]{:S(2)}, u32[]{:S(2)}) async-start(bf16[16,144,512]{2,1,0:T(8,128)(2,1)} %copy-done), calls=%async_computation | async-start | bytes 4718592 | tf_op jit(solution)/shard_map/all_to_all | solution.py:254
  112.2 26.3 %collective-permute-start.16 = (bf16[256,128]{1,0:T(8,128)(2,1)S(1)}, bf16[256,128]{1,0:T(8,128)(2,1)S(1)}, u32[]{:S(2)}, u32[]{:S(2)}) collective-permute-start(bf16[256,128]{1,0:T(8,128)(2,1)S(1)} %pad_maximum_fusion.7), channel_id=1, source_target_pairs={{0,8},{4,12},{8,16},{12,20},{16,24},{20,28},{24,32},{28,36},{32,40... | collective-permute-start | bytes 196616 | tf_op jit(solution)/shard_map/ppermute | solution.py:190
Sparse Core Ops, SparseCore 0:
  21.0 40.6 all-gather.1

commit v2 on v1

v2 whole, which is shorter than its diff:
```python
import functools
import math

import jax
import jax.numpy as jnp
from jax import lax
from jax.experimental import pallas as pl
from jax.experimental.pallas import tpu as pltpu
from jax.sharding import Mesh
from jax.sharding import PartitionSpec as P

Z, Y, X = 8, 8, 4
LINE = 8
BLOCK = 64
TOPK = 32
BLK_DEV = 16
HEAD = 128
ROWS = 512
QROWS = ROWS + 16
PAIR = 2 * BLOCK
SHARE = BLK_DEV * PAIR
LISTS = 2 * LINE
OROWS = 2 * HEAD + 16
STEP = 4
LOWEST = -3.0e38
EXPO = HEAD**-0.5 * math.log2(math.e)
SEQ = ("z", "y", "core")


def seq_index(z, y, core):
    return (z * Y + y) * 2 + core


Y_LINES = [[[seq_index(z, y, core) for y in range(Y)] for z in range(Z)] for core in range(2)]
Z_LINES = [[[seq_index(z, y, core) for z in range(Z)] for y in range(Y)] for core in range(2)]
KV_LINES = Y_LINES[0] + Z_LINES[1]
Q_LINES = Z_LINES[0] + Y_LINES[1]
Q_PLANES = [[i * X + x for i in line for x in range(X)] for line in Q_LINES]


def shift(value, lines, by):
    return lax.ppermute(value, SEQ, [(line[i], line[(i + by) % LINE]) for line in lines for i in range(LINE)])


def window_kernel(first_ref, gate_ref, q_ref, k_ref, v_ref, o_ref):
    for rc in range(2):
        s = lax.dot_general(
            k_ref[pl.ds(128 * rc, 256), :],
            q_ref[rc * QROWS : rc * QROWS + ROWS, :],
            (((1,), (1,)), ((), ())),
            preferred_element_type=jnp.float32,
        )
        kpos = lax.broadcasted_iota(jnp.int32, s.shape, 0) - 128
        column = lax.broadcasted_iota(jnp.int32, s.shape, 1)
        qpos = (column >> 7) * 32 + (column & 31)
        allowed = (kpos <= qpos) & (kpos > qpos - 128)
        if rc == 0:
            allowed = allowed & ((kpos >= 0) | (first_ref[0] == 0))
        s = jnp.where(allowed, s, LOWEST)
        top = jnp.max(s, axis=0, keepdims=True)
        p = jnp.exp2((s - top) * EXPO)
        total = jnp.sum(p, axis=0, keepdims=True)
        out = lax.dot_general(
            v_ref[pl.ds(128 * rc, 256), :],
            p.astype(jnp.bfloat16),
            (((0,), (0,)), ((), ())),
            preferred_element_type=jnp.float32,
        )
        out = (out * ((1.0 - gate_ref[...]) / total)).astype(jnp.bfloat16)
        for x in range(X):
            o_ref[x, rc * HEAD : (rc + 1) * HEAD, :] = out[:, x * 128 : (x + 1) * 128]


def memory_kernel(count_ref, place_ref, pos_ref, gate_ref, *rest):
    q_refs = rest[: LINE + 1]
    kv_ref, o_ref, buf, stage, acc, top_s, sum_s, in_sems, out_sems = rest[LINE + 1 :]
    buf[...] = jnp.zeros(buf.shape, buf.dtype)

    def fetch(peer, rc, k):
        at = pl.multiple_of(place_ref[(peer * 2 + rc) * BLK_DEV + k], PAIR)
        return pltpu.make_async_copy(
            kv_ref.at[pl.ds(at, PAIR)], buf.at[peer % 2, rc, k], in_sems.at[peer % 2, rc, k]
        )

    def fetch_all(peer):
        for rc in range(2):
            def start(k, carry):
                fetch(peer, rc, k).start()
                return carry

            lax.fori_loop(0, count_ref[peer * 2 + rc], start, 0)

    def fetch_wait(peer):
        for rc in range(2):
            def wait(k, carry):
                fetch(peer, rc, k).wait()
                return carry

            lax.fori_loop(0, count_ref[peer * 2 + rc], wait, 0)

    def send(peer):
        to = lax.rem(pos_ref[0] + peer, LINE) * X
        return pltpu.make_async_copy(stage.at[peer % 2], o_ref.at[pl.ds(to, X)], out_sems.at[peer % 2])

    fetch_all(0)
    for peer in range(LINE):
        slot = peer % 2
        if peer + 1 < LINE:
            fetch_all(peer + 1)
        counts = [count_ref[peer * 2 + rc] for rc in range(2)]
        top_s[...] = jnp.full((2, 1, ROWS), LOWEST, jnp.float32)
        sum_s[...] = jnp.zeros((2, 1, ROWS), jnp.float32)
        acc[...] = jnp.zeros((2, HEAD, ROWS), jnp.float32)
        if peer == LINE // 2:
            sources = [(q_refs[peer], 0), (q_refs[LINE], 0)]
        else:
            q_ref = q_refs[peer]
            sources = [(q_ref, 0), (q_ref, QROWS)]
        fetch_wait(peer)

        def one_step(step, carry):
            for rc in range(2):
                q_ref, first = sources[rc]
                blocks = pl.ds(step * STEP, STEP)
                keys = buf[slot, rc, blocks, :BLOCK, :].reshape(STEP * BLOCK, HEAD)
                values = buf[slot, rc, blocks, BLOCK:, :].reshape(STEP * BLOCK, HEAD)
                s = lax.dot_general(
                    keys,
                    q_ref[first : first + ROWS, :],
                    (((1,), (1,)), ((), ())),
                    preferred_element_type=jnp.float32,
                )
                rows = lax.broadcasted_iota(jnp.int32, s.shape, 0)
                s = jnp.where(rows < (counts[rc] - step * STEP) * BLOCK, s, LOWEST)
                top = jnp.maximum(top_s[rc], jnp.max(s, axis=0, keepdims=True))
                live = (step * STEP < counts[rc]).astype(jnp.float32)
                p = jnp.exp2((s - top) * EXPO) * live
                alpha = jnp.exp2((top_s[rc] - top) * EXPO)
                sum_s[rc] = sum_s[rc] * alpha + jnp.sum(p, axis=0, keepdims=True)
                acc[rc] = acc[rc] * alpha + lax.dot_general(
                    values, p.astype(jnp.bfloat16), (((0,), (0,)), ((), ())), preferred_element_type=jnp.float32
                )
                top_s[rc] = top
            return carry

        lax.fori_loop(0, (jnp.maximum(counts[0], counts[1]) + STEP - 1) // STEP, one_step, 0)
        if peer >= 2:
            send(peer - 2).wait()
        rows = lax.broadcasted_iota(jnp.int32, (16, ROWS), 0)
        pieces = jnp.zeros((16, ROWS), jnp.float32)
        for rc in range(2):
            total = sum_s[rc]
            some = total > 0.0
            safe = jnp.where(some, total, 1.0)
            out = (acc[rc] * (gate_ref[...] / safe)).astype(jnp.bfloat16)
            level = jnp.where(some, top_s[rc] * EXPO + jnp.log2(safe), LOWEST)
            high = level.astype(jnp.bfloat16).astype(jnp.float32)
            mid = (level - high).astype(jnp.bfloat16).astype(jnp.float32)
            for i, piece in enumerate((high, mid, level - high - mid)):
                pieces = jnp.where(rows == 3 * rc + i, piece, pieces)
            for x in range(X):
                stage[slot, x, rc * HEAD : (rc + 1) * HEAD, :] = out[:, x * 128 : (x + 1) * 128]
        pieces = pieces.astype(jnp.bfloat16)
        for x in range(X):
            stage[slot, x, 2 * HEAD :, :] = pieces[:, x * 128 : (x + 1) * 128]
        send(peer).start()
    send(LINE - 2).wait()
    send(LINE - 1).wait()


def merge_kernel(core_ref, part_ref, window_ref, mine_ref, other_ref):
    first_core = core_ref[0] == 0

    def one_head(x, carry):
        flat = []
        for rc in range(2):
            levels = []
            for i in range(LINE):
                pieces = part_ref[i, x, 2 * HEAD :, :].astype(jnp.float32)
                levels.append(pieces[3 * rc : 3 * rc + 1] + pieces[3 * rc + 1 : 3 * rc + 2] + pieces[3 * rc + 2 : 3 * rc + 3])
            top = functools.reduce(jnp.maximum, levels)
            shares = [jnp.exp2(level - top) for level in levels]
            inverse = 1.0 / functools.reduce(jnp.add, shares)
            mixed = window_ref[x, rc * HEAD : (rc + 1) * HEAD, :].astype(jnp.float32)
            for i in range(LINE):
                mixed = mixed + part_ref[i, x, rc * HEAD : (rc + 1) * HEAD, :].astype(jnp.float32) * (shares[i] * inverse)
            flat.append(mixed.T)
        mine = jnp.where(first_core, flat[0], flat[1]).astype(jnp.bfloat16)
        other = jnp.where(first_core, flat[1], flat[0]).astype(jnp.bfloat16)
        for g in range(4):
            mine_ref[x * 4 + g] = mine[g * 32 : (g + 1) * 32, :]
            other_ref[x * 4 + g] = other[g * 32 : (g + 1) * 32, :]
        return carry

    lax.fori_loop(0, X, one_head, 0)


def on_device(queries, keys, values, mem_keys, mem_values, mem_ids, gate_logits):
    z, y, core = lax.axis_index("z"), lax.axis_index("y"), lax.axis_index("core")
    first_core = core == 0

    def mine_and_other(array):
        return jnp.where(first_core, array[0], array[1]), jnp.where(first_core, array[1], array[0])

    def by_core(mine, other):
        return jnp.where(first_core, mine, other), jnp.where(first_core, other, mine)

    blocks = (BLK_DEV, BLOCK, 2, HEAD)
    cache = jnp.stack([mem_keys.reshape(blocks), mem_values.reshape(blocks)])
    cache_mine, cache_other = mine_and_other(cache.transpose(3, 1, 0, 2, 4).reshape(2, SHARE, HEAD))
    q_mine, q_other = mine_and_other(
        queries.reshape(X, 32, 2, 4, HEAD).transpose(2, 0, 3, 1, 4).reshape(2, ROWS, HEAD)
    )
    ids = jnp.concatenate([mem_ids // 64, mem_ids % 64], axis=2).astype(jnp.bfloat16)
    ids = jnp.pad(ids, ((0, 0), (0, 15), (0, HEAD - 2 * TOPK)))
    ids_mine, ids_other = mine_and_other(ids)
    k_mine, k_other = mine_and_other(keys.transpose(1, 0, 2))
    v_mine, v_other = mine_and_other(values.transpose(1, 0, 2))
    swap = [(0, 1), (1, 0)]
    swapped = lax.ppermute(
        jnp.concatenate([cache_other, q_other, ids_other, k_other, v_other], axis=0), "core", swap
    )
    cache = jnp.concatenate([cache_mine, swapped[:SHARE]], axis=0)
    gathered = lax.all_gather(cache, SEQ, axis_index_groups=KV_LINES, tiled=True)
    swapped = swapped[SHARE:]

    q_list = jnp.concatenate(by_core(jnp.concatenate([q_mine, ids_mine], axis=0), swapped[:QROWS]), axis=0)
    lists = {0: q_list}
    for hop in range(1, 4):
        lists[-hop % LINE] = shift(lists[(1 - hop) % LINE], Q_LINES, 1)
        lists[hop] = shift(lists[hop - 1], Q_LINES, -1)
    lists[4] = shift(lists[5][:QROWS], Q_LINES, 1)
    lists[LINE] = shift(lists[3][QROWS:], Q_LINES, -1)
    lists = [lists[d] for d in range(LINE + 1)]

    gate = jax.nn.sigmoid(gate_logits).reshape(2, 4)
    gate = jnp.where(first_core, gate[0], gate[1])
    gate = jnp.broadcast_to(gate[None, :, None], (X, 4, 32)).reshape(1, ROWS)

    k_first, k_second = by_core(k_mine, swapped[QROWS : QROWS + 128])
    v_first, v_second = by_core(v_mine, swapped[QROWS + 128 :])
    chips = Z * Y
    onward = [(2 * i + c, 2 * i + 2 + c) for i in range(chips - 1) for c in range(2)]
    before = lax.ppermute(jnp.concatenate([k_second, v_second], axis=0), SEQ, onward)
    near_keys = jnp.concatenate([before[:128], k_first, k_second], axis=0)
    near_values = jnp.concatenate([before[128:], v_first, v_second], axis=0)
    is_first = ((z == 0) & (y == 0)).astype(jnp.int32).reshape(1)
    window = pl.pallas_call(
        window_kernel,
        out_shape=jax.ShapeDtypeStruct((X, 2 * HEAD, 128), jnp.bfloat16),
        grid_spec=pltpu.PrefetchScalarGridSpec(
            num_scalar_prefetch=1,
            grid=(1,),
            in_specs=[
                pl.BlockSpec((1, ROWS), lambda i, s: (0, 0)),
                pl.BlockSpec((2 * QROWS, HEAD), lambda i, s: (0, 0)),
                pl.BlockSpec((384, HEAD), lambda i, s: (0, 0)),
                pl.BlockSpec((384, HEAD), lambda i, s: (0, 0)),
            ],
            out_specs=pl.BlockSpec((X, 2 * HEAD, 128), lambda i, s: (0, 0, 0)),
        ),
        compiler_params=pltpu.CompilerParams(vmem_limit_bytes=24 << 20),
        cost_estimate=pl.CostEstimate(
            flops=4 * 2 * ROWS * 256 * HEAD, bytes_accessed=1 << 20, transcendentals=2 * ROWS * 256
        ),
        name="window",
    )(is_first, gate, q_list, near_keys, near_values)
    window = lax.all_to_all(window, "head", split_axis=0, concat_axis=0, tiled=True)

    coded = []
    for d in range(LINE):
        if d == LINE // 2:
            coded += [lists[d][ROWS : ROWS + 1], lists[LINE][ROWS : ROWS + 1]]
        else:
            coded += [lists[d][ROWS : ROWS + 1], lists[d][QROWS + ROWS : QROWS + ROWS + 1]]
    coded = jnp.concatenate(coded, axis=0)[:, : 2 * TOPK].astype(jnp.int32)
    wanted = coded[:, :TOPK] * 64 + coded[:, TOPK:]
    owner, local = wanted // BLK_DEV, wanted % BLK_DEV
    owner_z, owner_y, owner_core = owner // (2 * Y), (owner // 2) % Y, owner % 2
    here = jnp.where(first_core, owner_z == z, owner_y == y)
    slot = jnp.where(first_core, owner_y, owner_z) * 2 + (owner_core != core).astype(jnp.int32)
    place = slot * SHARE + local * PAIR
    rank = jnp.sum(
        (here[:, None, :] & (jnp.arange(TOPK)[None, None, :] < jnp.arange(TOPK)[None, :, None])).astype(jnp.int32),
        axis=2,
    )
    match = here[:, :, None] & (rank[:, :, None] == jnp.arange(BLK_DEV)[None, None, :])
    places = jnp.sum(jnp.where(match, place[:, :, None], 0), axis=1)
    counts = jnp.sum(here.astype(jnp.int32), axis=1)
    position = jnp.where(first_core, z, y).astype(jnp.int32).reshape(1)

    smem = pl.BlockSpec(memory_space=pltpu.SMEM)
    vmem = pl.BlockSpec(memory_space=pltpu.VMEM)
    partial = pl.pallas_call(
        memory_kernel,
        out_shape=jax.ShapeDtypeStruct((LINE * X, OROWS, 128), jnp.bfloat16),
        in_specs=[smem] * 3 + [vmem] * (LINE + 2) + [pl.BlockSpec(memory_space=pltpu.HBM)],
        out_specs=pl.BlockSpec(memory_space=pltpu.HBM),
        scratch_shapes=[
            pltpu.VMEM((2, 2, BLK_DEV, PAIR, HEAD), jnp.bfloat16),
            pltpu.VMEM((2, X, OROWS, 128), jnp.bfloat16),
            pltpu.VMEM((2, HEAD, ROWS), jnp.float32),
            pltpu.VMEM((2, 1, ROWS), jnp.float32),
            pltpu.VMEM((2, 1, ROWS), jnp.float32),
            pltpu.SemaphoreType.DMA((2, 2, BLK_DEV)),
            pltpu.SemaphoreType.DMA((2,)),
        ],
        compiler_params=pltpu.CompilerParams(vmem_limit_bytes=40 << 20),
        cost_estimate=pl.CostEstimate(
            flops=4 * 64 * ROWS * BLOCK * HEAD, bytes_accessed=6 << 20, transcendentals=64 * ROWS * BLOCK
        ),
        name="memory",
    )(counts, places.reshape(-1), position, gate, *lists, gathered)

    returned = lax.all_to_all(
        partial, SEQ + ("head",), split_axis=0, concat_axis=0, axis_index_groups=Q_PLANES, tiled=True
    ).reshape(LINE, X, OROWS, 128)
    block = pl.BlockSpec((4 * X, 32, HEAD), lambda i, s: (0, 0, 0))
    mine, other = pl.pallas_call(
        merge_kernel,
        out_shape=[jax.ShapeDtypeStruct((4 * X, 32, HEAD), jnp.bfloat16)] * 2,
        grid_spec=pltpu.PrefetchScalarGridSpec(
            num_scalar_prefetch=1,
            grid=(1,),
            in_specs=[
                pl.BlockSpec((LINE, X, OROWS, 128), lambda i, s: (0, 0, 0, 0)),
                pl.BlockSpec((X, 2 * HEAD, 128), lambda i, s: (0, 0, 0)),
            ],
            out_specs=[block, block],
        ),
        compiler_params=pltpu.CompilerParams(vmem_limit_bytes=24 << 20),
        cost_estimate=pl.CostEstimate(flops=1 << 22, bytes_accessed=4 << 20, transcendentals=1 << 13),
        name="merge",
    )(core.astype(jnp.int32).reshape(1), returned, window)
    theirs = lax.ppermute(other, "core", swap)
    heads = jnp.stack([a.reshape(X, 4, 32, HEAD) for a in by_core(mine, theirs)], axis=1)
    return heads.transpose(3, 0, 1, 2, 4).reshape(32, 8 * X * HEAD)


def solution(mesh):
    fine = Mesh(mesh.devices.reshape(Z, Y, 2, X), ("z", "y", "core", "head"))
    placed = (
        P(SEQ, "head", None),
        P(SEQ, "head", None),
        P(SEQ, "head", None),
        P(SEQ, "head", None),
        P(SEQ, "head", None),
        P("head", SEQ, None),
        P("head"),
    )
    return jax.shard_map(
        on_device, mesh=fine, in_specs=placed, out_specs=P(SEQ + ("head",), None), check_vma=False
    )
```

time: 171 us -> 171 us (level)
  blocking collectives: 15.5 us -> 46.9 us
  starting transfers between devices: 67.4 us -> 42.7 us
  waiting for transfers between devices: 45.5 us -> 31.8 us
  local copies, waits for them, and re-layouts: 6.76 us -> 16 us
    all_to_all x1, blocking collectives: 15.5 us -> 46.9 us  [on_device(): lax.all_to_all(partial, SEQ + ('head',), split_axis=0, concat_axis=0, axi...]
    ppermute x1, waiting for transfers between devices: 22.9 us -> 0.01 us  [on_device(): lax.ppermute(jnp.concatenate([k_second, v_second], axis=0), SEQ, onward)]
    ppermute x16 -> x10, starting transfers between devices: 56 us -> 38 us  [the longest x8 26 us: shift(): lax.ppermute(value, SEQ, [(line[i], line[(i + by) % LINE]) for line in li...]
    all_gather x1, waiting for transfers between devices: 0.02 us -> 16.8 us  [on_device(): lax.all_gather(cache, SEQ, axis_index_groups=KV_LINES, tiled=True)]
    unnamed x16 -> x28, local copies, waits for them, and re-layouts: 4.89 us -> 11.3 us
    all_to_all x1, waiting for transfers between devices: 5.53 us -> 0.01 us  [on_device(): lax.all_to_all(window, 'head', split_axis=0, concat_axis=0, tiled=True)]
    all_to_all x1, starting transfers between devices: 7.97 us -> 3.41 us  [on_device(): lax.all_to_all(window, 'head', split_axis=0, concat_axis=0, tiled=True)]
    another operation x0 -> x2, local copies, waits for them, and re-layouts: none -> 2.31 us  [on_device(): cache = jnp.stack([mem_keys.reshape(blocks), mem_values.reshape(blocks)])]
  transfers between devices with their start and end apart: 19 -> 13, of which waited for: 8 -> 7; matrix products, arithmetic and copies ran while one was open for 1% -> 1% of each run, Pallas kernels for 1% -> 9%
where the time goes in v2:
time: 171 us; the launch traced here: 170 us
  blocking collectives  46.9 us (27%)
  starting transfers between devices  42.7 us (25%)
  waiting for transfers between devices  31.8 us (19%)
  local copies, waits for them, and re-layouts  16 us (9%)
  Pallas kernels  15.9 us (9%)
  between operations  13.9 us (8%)
  other arithmetic  3.31 us (2%)
    all_to_all x1, blocking collectives, on_device(): lax.all_to_all(partial, SEQ + ('head',), split_axis=0, concat_axis=0, axi...  46.9 us
    ppermute x8, starting transfers between devices, shift(): lax.ppermute(value, SEQ, [(line[i], line[(i + by) % LINE]) for line in li...  26 us
    all_gather x1, waiting for transfers between devices, on_device(): lax.all_gather(cache, SEQ, axis_index_groups=KV_LINES, tiled=True)  16.8 us
    pallas_call x1, Pallas kernels, on_device(): pl.pallas_call(memory_kernel, out_shape=jax.ShapeDtypeStruct((LINE * X, O...  13.4 us
    ppermute x8, waiting for transfers between devices, shift(): lax.ppermute(value, SEQ, [(line[i], line[(i + by) % LINE]) for line in li...  12.2 us
    unnamed x28, local copies, waits for them, and re-layouts  11.3 us
    ppermute x1, starting transfers between devices, on_device(): lax.ppermute(jnp.concatenate([cache_other, q_other, ids_other, k_other, v...  8.79 us
  transfers between devices with their start and end apart: 13, of which 7 were waited for; matrix products, arithmetic and copies ran while one was open for 1% of the time, Pallas kernels for 9%

profile of v2, /device:TPU:1, one launch (start us, length us, event | category | flops | bytes accessed | tf_op | source)
XLA Modules:
  0.0 170.4 jit_solution(13266090961180158988)
XLA Ops:
  6.5 0.0 all-gather.2.cloned.1.call-start
  6.5 0.7 fusion.17
  7.2 0.9 copy.25
  8.1 0.9 copy.24
  8.9 1.0 copy.23
  9.9 1.2 copy.15
  11.1 1.2 copy.16
  12.3 0.1 maximum_bitcast_fusion
  12.4 0.1 broadcast_select_fusion
  12.5 0.1 fusion.11
  12.6 0.0 copy-start.11
  12.7 8.8 %collective-permute-start = (bf16[2832,128]{1,0:T(8,128)(2,1)S(1)}, bf16[2832,128]{1,0:T(8,128)(2,1)S(1)}, u32[]{:S(2)}, u32[]{:S(2)}) collective-permute-start(bf16[2832,128]{1,0:T(8,128)(2,1)S(1)} %bitcast_dynamic-update-slice_fusion), channel_id=1, source_target_pairs={{0,4},{4,0},{1,5},{5,1},{2,6},{6,2},{3,7},{7,3},{8,12},{12,8},{9,1... | collective-permute-start | bytes 2174984 | tf_op jit(solution)/shard_map/ppermute | solution.py:220
  21.5 1.8 %collective-permute-done = bf16[2832,128]{1,0:T(8,128)(2,1)S(1)} collective-permute-done((bf16[2832,128]{1,0:T(8,128)(2,1)S(1)}, bf16[2832,128]{1,0:T(8,128)(2,1)S(1)}, u32[]{:S(2)}, u32[]{:S(2)}) %collective-permute-start) | collective-permute-done | bytes 725024 | tf_op jit(solution)/shard_map/ppermute | solution.py:220
  23.4 1.1 pad_maximum_fusion
  24.4 0.0 all-gather.2.cloned.1.call-update
  24.5 0.1 broadcast_select_fusion.10
  24.6 0.1 broadcast_in_dim.12
  24.7 0.1 reshape.116.gate_ref
  24.8 1.3 collective-permute-start.9
  26.1 0.1 broadcast_select_fusion.2
  26.2 1.9 %collective-permute-start.4 = (bf16[1056,128]{1,0:T(8,128)(2,1)S(1)}, bf16[1056,128]{1,0:T(8,128)(2,1)S(1)}, u32[]{:S(2)}, u32[]{:S(2)}) collective-permute-start(bf16[1056,128]{1,0:T(8,128)(2,1)S(1)} %pad_maximum_fusion.1.rest_0_.q_ref), channel_id=1, source_target_pairs={{0,64},{64,128},{128,192},{192,256},{256,320},{320,384},{384,448},... | collective-permute-start | bytes 811016 | tf_op jit(solution)/shard_map/ppermute | solution.py:42
  28.2 4.6 %collective-permute-start.1 = (bf16[1056,128]{1,0:T(8,128)(2,1)S(1)}, bf16[1056,128]{1,0:T(8,128)(2,1)S(1)}, u32[]{:S(2)}, u32[]{:S(2)}) collective-permute-start(bf16[1056,128]{1,0:T(8,128)(2,1)S(1)} %pad_maximum_fusion.1.rest_0_.q_ref), channel_id=1, source_target_pairs={{0,448},{64,0},{128,64},{192,128},{256,192},{320,256},{384,320},{4... | collective-permute-start | bytes 811016 | tf_op jit(solution)/shard_map/ppermute | solution.py:42
  32.7 0.0 collective-permute-done.9
  32.8 1.6 window.1
  34.4 3.4 %all-to-all-start.1 = ((bf16[4,256,128]{2,1,0:T(8,128)(2,1)}), bf16[4,256,128]{2,1,0:T(8,128)(2,1)S(1)}, u32[]{:S(2)}, u32[]{:S(2)}) async-start(bf16[4,256,128]{2,1,0:T(8,128)(2,1)} %window.1), calls=%async_computation.1 | async-start | bytes 524288 | tf_op jit(solution)/shard_map/all_to_all | solution.py:268
  37.8 0.0 collective-permute-done.4.rest_7_
  37.8 1.9 %collective-permute-start.5 = (bf16[1056,128]{1,0:T(8,128)(2,1)S(1)}, bf16[1056,128]{1,0:T(8,128)(2,1)S(1)}, u32[]{:S(2)}, u32[]{:S(2)}) collective-permute-start(bf16[1056,128]{1,0:T(8,128)(2,1)S(1)} %collective-permute-done.4.rest_7_), channel_id=1, source_target_pairs={{0,64},{64,128},{128,192},{192,256},{256,320},{320,384},{384,448},... | collective-permute-start | bytes 811016 | tf_op jit(solution)/shard_map/ppermute | solution.py:42
  39.8 0.0 collective-permute-done.1.rest_1_
  39.8 0.0 copy-start.3
  39.8 4.6 %collective-permute-start.2 = (bf16[1056,128]{1,0:T(8,128)(2,1)S(1)}, bf16[1056,128]{1,0:T(8,128)(2,1)S(1)}, u32[]{:S(2)}, u32[]{:S(2)}) collective-permute-start(bf16[1056,128]{1,0:T(8,128)(2,1)S(1)} %collective-permute-done.1.rest_1_), channel_id=1, source_target_pairs={{0,448},{64,0},{128,64},{192,128},{256,192},{320,256},{384,320},{4... | collective-permute-start | bytes 811016 | tf_op jit(solution)/shard_map/ppermute | solution.py:42
  44.4 5.1 %collective-permute-done.5.rest_6_ = bf16[1056,128]{1,0:T(8,128)(2,1)S(1)} collective-permute-done((bf16[1056,128]{1,0:T(8,128)(2,1)S(1)}, bf16[1056,128]{1,0:T(8,128)(2,1)S(1)}, u32[]{:S(2)}, u32[]{:S(2)}) %collective-permute-start.5) | collective-permute-done | bytes 270368 | tf_op jit(solution)/shard_map/ppermute | solution.py:42
  49.5 1.9 %collective-permute-start.6 = (bf16[1056,128]{1,0:T(8,128)(2,1)S(1)}, bf16[1056,128]{1,0:T(8,128)(2,1)S(1)}, u32[]{:S(2)}, u32[]{:S(2)}) collective-permute-start(bf16[1056,128]{1,0:T(8,128)(2,1)S(1)} %collective-permute-done.5.rest_6_), channel_id=1, source_target_pairs={{0,64},{64,128},{128,192},{192,256},{256,320},{320,384},{384,448},... | collective-permute-start | bytes 811016 | tf_op jit(solution)/shard_map/ppermute | solution.py:42
  51.4 0.0 collective-permute-done.2.rest_2_
  51.5 4.6 %collective-permute-start.3 = (bf16[1056,128]{1,0:T(8,128)(2,1)S(1)}, bf16[1056,128]{1,0:T(8,128)(2,1)S(1)}, u32[]{:S(2)}, u32[]{:S(2)}) collective-permute-start(bf16[1056,128]{1,0:T(8,128)(2,1)S(1)} %collective-permute-done.2.rest_2_), channel_id=1, source_target_pairs={{0,448},{64,0},{128,64},{192,128},{256,192},{320,256},{384,320},{4... | collective-permute-start | bytes 811016 | tf_op jit(solution)/shard_map/ppermute | solution.py:42
  56.1 0.7 copy-done.5
  56.8 0.7 copy-done.7
  57.5 3.7 %collective-permute-done.6.rest_5_ = bf16[1056,128]{1,0:T(8,128)(2,1)S(1)} collective-permute-done((bf16[1056,128]{1,0:T(8,128)(2,1)S(1)}, bf16[1056,128]{1,0:T(8,128)(2,1)S(1)}, u32[]{:S(2)}, u32[]{:S(2)}) %collective-permute-start.6) | collective-permute-done | bytes 270368 | tf_op jit(solution)/shard_map/ppermute | solution.py:42
  61.2 1.9 %collective-permute-start.7 = (bf16[528,128]{1,0:T(8,128)(2,1)S(1)}, bf16[528,128]{1,0:T(8,128)(2,1)S(1)}, u32[]{:S(2)}, u32[]{:S(2)}) collective-permute-start(bf16[528,128]{1,0:T(8,128)(2,1)S(1)} %slice.195), channel_id=1, source_target_pairs={{0,64},{64,128},{128,192},{192,256},{256,320},{320,384},{384,448},... | collective-permute-start | bytes 405512 | tf_op jit(solution)/shard_map/ppermute | solution.py:42
  63.2 0.0 collective-permute-done.3.rest_3_
  63.2 4.6 %collective-permute-start.8 = (bf16[528,128]{1,0:T(8,128)(2,1)S(1)}, bf16[528,128]{1,0:T(8,128)(2,1)S(1)}, u32[]{:S(2)}, u32[]{:S(2)}) collective-permute-start(bf16[528,128]{1,0:T(8,128)(2,1)S(1)} %slice.197), channel_id=1, source_target_pairs={{0,448},{64,0},{128,64},{192,128},{256,192},{320,256},{384,320},{4... | collective-permute-start | bytes 405512 | tf_op jit(solution)/shard_map/ppermute | solution.py:42
  67.8 2.2 %collective-permute-done.7.rest_4_ = bf16[528,128]{1,0:T(8,128)(2,1)S(1)} collective-permute-done((bf16[528,128]{1,0:T(8,128)(2,1)S(1)}, bf16[528,128]{1,0:T(8,128)(2,1)S(1)}, u32[]{:S(2)}, u32[]{:S(2)}) %collective-permute-start.7) | collective-permute-done | bytes 135200 | tf_op jit(solution)/shard_map/ppermute | solution.py:42
  70.0 1.1 collective-permute-done.8.rest_8_
  71.1 0.1 concatenate.40
  71.2 0.1 fusion.10
  71.3 0.1 convert_reduce_fusion.1
  71.5 0.4 convert_reduce_fusion
  71.8 0.3 select_reduce_fusion
  72.2 0.1 reshape.114.place_ref
  72.2 16.8 %all-gather.2.cloned.1.call-done.rest_9_ = bf16[32768,128]{1,0:T(8,128)(2,1)} async-done(((bf16[4096,128]{1,0:T(8,128)(2,1)}), bf16[32768,128]{1,0:T(8,128)(2,1)}) %all-gather.2.cloned.1.call-update) | async-done | bytes 8388624 | tf_op jit(solution)/shard_map/all_gather | solution.py:224
  89.1 0.0 copy-done.3
  89.1 3.4 %copy-done = bf16[32768,128]{1,0:T(8,128)(2,1)S(1)} copy-done((bf16[32768,128]{1,0:T(8,128)(2,1)S(1)}, bf16[32768,128]{1,0:T(8,128)(2,1)}, u32[]{:S(2)}) %copy-start) | copy-done | bytes 8388632
  92.5 1.0 copy-done.2
  93.4 1.0 copy-done.4
  94.4 1.0 copy-done.6
  95.3 1.0 copy-done.8
  96.3 0.9 copy-done.10
  97.2 13.4 %memory.1 = bf16[32,272,128]{2,1,0:T(8,128)(2,1)S(1)} custom-call(s32[16]{0:T(128)S(1)} %get-tuple-element.11.count_ref, s32[256]{0:T(256)S(1)} %reshape.114.place_ref, s32[1]{0:T(128)} %bitcast.15.pos_ref, f32[1,512]{1,0:T(1,128)S(1)} %reshape.116.gate_ref, bf16[1056,128]{1,0:T(8,128)(2,1)S(1)} %pad_maximum_fusion.1.rest_0_.q_ref, ...), custom_call_target="tpu_custom_call" | custom-call | flops 1073741824 | bytes 6291456 | tf_op jit(solution)/shard_map/memory/pallas_call | solution.py:294
  110.5 0.0 all-to-all-done.1.window_ref
  110.5 46.9 %all_to_all.10 = bf16[32,272,128]{2,1,0:T(8,128)(2,1)S(1)} all-to-all(bf16[32,272,128]{2,1,0:T(8,128)(2,1)S(1)} %memory.1), channel_id=1, replica_groups={{0,1,2,3,64,65,66,67,128,129,130,131,192,193,194,195,256,257,258,259,32..., dimensions={0} | all-to-all | bytes 4456448 | tf_op jit(solution)/shard_map/all_to_all | solution.py:315
  157.4 0.9 merge.1
  158.3 3.2 %collective-permute-start.10 = (bf16[16,32,128]{2,1,0:T(8,128)(2,1)S(1)}, bf16[16,32,128]{2,1,0:T(8,128)(2,1)S(1)}, u32[]{:S(2)}, u32[]{:S(2)}) collective-permute-start(bf16[16,32,128]{2,1,0:T(8,128)(2,1)S(1)} %get-tuple-element.8), channel_id=1, source_target_pairs={{0,4},{4,0},{1,5},{5,1},{2,6},{6,2},{3,7},{7,3},{8,12},{12,8},{9,1... | collective-permute-start | bytes 393224 | tf_op jit(solution)/shard_map/ppermute | solution.py:335
  161.5 1.0 collective-permute-done.10
  162.6 0.1 copy.19
  162.7 0.9 reshape.120
  (44 shorter events, 0.4 us)
Async XLA Ops:
  6.5 82.5 %all-gather.2.cloned.1.call-start = ((), (), s32[]{:S(2)}) async-start(), calls=%async_computation.2 | async-start | bytes 9437184 | tf_op jit(solution)/shard_map/all_gather | solution.py:224
  12.6 11.8 %copy-start.11 = (f32[8]{0:T(128)S(1)}, f32[8]{0:T(128)}, u32[]{:S(2)}) copy-start(f32[8]{0:T(128)} %param.13) | copy-start | bytes 100
  12.7 10.6 %collective-permute-start = (bf16[2832,128]{1,0:T(8,128)(2,1)S(1)}, bf16[2832,128]{1,0:T(8,128)(2,1)S(1)}, u32[]{:S(2)}, u32[]{:S(2)}) collective-permute-start(bf16[2832,128]{1,0:T(8,128)(2,1)S(1)} %bitcast_dynamic-update-slice_fusion), channel_id=1, source_target_pairs={{0,4},{4,0},{1,5},{5,1},{2,6},{6,2},{3,7},{7,3},{8,12},{12,8},{9,1... | collective-permute-start | bytes 2174984 | tf_op jit(solution)/shard_map/ppermute | solution.py:220
  24.8 7.9 %collective-permute-start.9 = (bf16[256,128]{1,0:T(8,128)(2,1)S(1)}, bf16[256,128]{1,0:T(8,128)(2,1)S(1)}, u32[]{:S(2)}, u32[]{:S(2)}) collective-permute-start(bf16[256,128]{1,0:T(8,128)(2,1)S(1)} %pad_maximum_fusion.5), channel_id=1, source_target_pairs={{0,8},{4,12},{8,16},{12,20},{16,24},{20,28},{24,32},{28,36},{32,40... | collective-permute-start | bytes 196616 | tf_op jit(solution)/shard_map/ppermute | solution.py:244
  26.2 11.6 %collective-permute-start.4 = (bf16[1056,128]{1,0:T(8,128)(2,1)S(1)}, bf16[1056,128]{1,0:T(8,128)(2,1)S(1)}, u32[]{:S(2)}, u32[]{:S(2)}) collective-permute-start(bf16[1056,128]{1,0:T(8,128)(2,1)S(1)} %pad_maximum_fusion.1.rest_0_.q_ref), channel_id=1, source_target_pairs={{0,64},{64,128},{128,192},{192,256},{256,320},{320,384},{384,448},... | collective-permute-start | bytes 811016 | tf_op jit(solution)/shard_map/ppermute | solution.py:42
  28.2 11.6 %collective-permute-start.1 = (bf16[1056,128]{1,0:T(8,128)(2,1)S(1)}, bf16[1056,128]{1,0:T(8,128)(2,1)S(1)}, u32[]{:S(2)}, u32[]{:S(2)}) collective-permute-start(bf16[1056,128]{1,0:T(8,128)(2,1)S(1)} %pad_maximum_fusion.1.rest_0_.q_ref), channel_id=1, source_target_pairs={{0,448},{64,0},{128,64},{192,128},{256,192},{320,256},{384,320},{4... | collective-permute-start | bytes 811016 | tf_op jit(solution)/shard_map/ppermute | solution.py:42
  34.4 76.1 %all-to-all-start.1 = ((bf16[4,256,128]{2,1,0:T(8,128)(2,1)}), bf16[4,256,128]{2,1,0:T(8,128)(2,1)S(1)}, u32[]{:S(2)}, u32[]{:S(2)}) async-start(bf16[4,256,128]{2,1,0:T(8,128)(2,1)} %window.1), calls=%async_computation.1 | async-start | bytes 524288 | tf_op jit(solution)/shard_map/all_to_all | solution.py:268
  37.8 51.2 %copy-start.1 = (bf16[1056,128]{1,0:T(8,128)(2,1)}, bf16[1056,128]{1,0:T(8,128)(2,1)S(1)}, u32[]{:S(2)}) copy-start(bf16[1056,128]{1,0:T(8,128)(2,1)S(1)} %collective-permute-done.4.rest_7_) | copy-start | bytes 811012
  37.8 11.7 %collective-permute-start.5 = (bf16[1056,128]{1,0:T(8,128)(2,1)S(1)}, bf16[1056,128]{1,0:T(8,128)(2,1)S(1)}, u32[]{:S(2)}, u32[]{:S(2)}) collective-permute-start(bf16[1056,128]{1,0:T(8,128)(2,1)S(1)} %collective-permute-done.4.rest_7_), channel_id=1, source_target_pairs={{0,64},{64,128},{128,192},{192,256},{256,320},{320,384},{384,448},... | collective-permute-start | bytes 811016 | tf_op jit(solution)/shard_map/ppermute | solution.py:42
  39.8 49.3 %copy-start.3 = (bf16[1056,128]{1,0:T(8,128)(2,1)}, bf16[1056,128]{1,0:T(8,128)(2,1)S(1)}, u32[]{:S(2)}) copy-start(bf16[1056,128]{1,0:T(8,128)(2,1)S(1)} %collective-permute-done.1.rest_1_) | copy-start | bytes 811012
  39.8 11.7 %collective-permute-start.2 = (bf16[1056,128]{1,0:T(8,128)(2,1)S(1)}, bf16[1056,128]{1,0:T(8,128)(2,1)S(1)}, u32[]{:S(2)}, u32[]{:S(2)}) collective-permute-start(bf16[1056,128]{1,0:T(8,128)(2,1)S(1)} %collective-permute-done.1.rest_1_), channel_id=1, source_target_pairs={{0,448},{64,0},{128,64},{192,128},{256,192},{320,256},{384,320},{4... | collective-permute-start | bytes 811016 | tf_op jit(solution)/shard_map/ppermute | solution.py:42
  49.5 11.7 %collective-permute-start.6 = (bf16[1056,128]{1,0:T(8,128)(2,1)S(1)}, bf16[1056,128]{1,0:T(8,128)(2,1)S(1)}, u32[]{:S(2)}, u32[]{:S(2)}) collective-permute-start(bf16[1056,128]{1,0:T(8,128)(2,1)S(1)} %collective-permute-done.5.rest_6_), channel_id=1, source_target_pairs={{0,64},{64,128},{128,192},{192,256},{256,320},{320,384},{384,448},... | collective-permute-start | bytes 811016 | tf_op jit(solution)/shard_map/ppermute | solution.py:42
  51.5 11.7 %collective-permute-start.3 = (bf16[1056,128]{1,0:T(8,128)(2,1)S(1)}, bf16[1056,128]{1,0:T(8,128)(2,1)S(1)}, u32[]{:S(2)}, u32[]{:S(2)}) collective-permute-start(bf16[1056,128]{1,0:T(8,128)(2,1)S(1)} %collective-permute-done.2.rest_2_), channel_id=1, source_target_pairs={{0,448},{64,0},{128,64},{192,128},{256,192},{320,256},{384,320},{4... | collective-permute-start | bytes 811016 | tf_op jit(solution)/shard_map/ppermute | solution.py:42
  56.1 0.7 copy-start.5
  56.8 0.7 copy-start.7
  61.2 8.8 %collective-permute-start.7 = (bf16[528,128]{1,0:T(8,128)(2,1)S(1)}, bf16[528,128]{1,0:T(8,128)(2,1)S(1)}, u32[]{:S(2)}, u32[]{:S(2)}) collective-permute-start(bf16[528,128]{1,0:T(8,128)(2,1)S(1)} %slice.195), channel_id=1, source_target_pairs={{0,64},{64,128},{128,192},{192,256},{256,320},{320,384},{384,448},... | collective-permute-start | bytes 405512 | tf_op jit(solution)/shard_map/ppermute | solution.py:42
  63.2 8.0 %collective-permute-start.8 = (bf16[528,128]{1,0:T(8,128)(2,1)S(1)}, bf16[528,128]{1,0:T(8,128)(2,1)S(1)}, u32[]{:S(2)}, u32[]{:S(2)}) collective-permute-start(bf16[528,128]{1,0:T(8,128)(2,1)S(1)} %slice.197), channel_id=1, source_target_pairs={{0,448},{64,0},{128,64},{192,128},{256,192},{320,256},{384,320},{4... | collective-permute-start | bytes 405512 | tf_op jit(solution)/shard_map/ppermute | solution.py:42
  71.1 17.9 %copy-start.9 = (bf16[528,128]{1,0:T(8,128)(2,1)}, bf16[528,128]{1,0:T(8,128)(2,1)S(1)}, u32[]{:S(2)}) copy-start(bf16[528,128]{1,0:T(8,128)(2,1)S(1)} %collective-permute-done.8.rest_8_) | copy-start | bytes 405508
  89.1 3.4 %copy-start = (bf16[32768,128]{1,0:T(8,128)(2,1)S(1)}, bf16[32768,128]{1,0:T(8,128)(2,1)}, u32[]{:S(2)}) copy-start(bf16[32768,128]{1,0:T(8,128)(2,1)} %all-gather.2.cloned.1.call-done.rest_9_) | copy-start | bytes 25165828
  92.5 1.0 copy-start.2
  93.4 1.0 copy-start.4
  94.4 1.0 copy-start.6
  95.3 1.0 copy-start.8
  96.3 0.9 copy-start.10
  158.3 4.2 %collective-permute-start.10 = (bf16[16,32,128]{2,1,0:T(8,128)(2,1)S(1)}, bf16[16,32,128]{2,1,0:T(8,128)(2,1)S(1)}, u32[]{:S(2)}, u32[]{:S(2)}) collective-permute-start(bf16[16,32,128]{2,1,0:T(8,128)(2,1)S(1)} %get-tuple-element.8), channel_id=1, source_target_pairs={{0,4},{4,0},{1,5},{5,1},{2,6},{6,2},{3,7},{7,3},{8,12},{12,8},{9,1... | collective-permute-start | bytes 393224 | tf_op jit(solution)/shard_map/ppermute | solution.py:335
Sparse Core Ops, SparseCore 0:
  24.6 64.4 all-gather.1

commit v3 on v2

v3 whole, which is shorter than its diff:
```python
import functools
import math

import jax
import jax.numpy as jnp
from jax import lax
from jax.experimental import pallas as pl
from jax.experimental.pallas import tpu as pltpu
from jax.sharding import Mesh
from jax.sharding import PartitionSpec as P

Z, Y, X = 8, 8, 4
LINE = 8
BLOCK = 64
TOPK = 32
BLK_DEV = 16
HEAD = 128
ROWS = 512
QROWS = ROWS + 16
PAIR = 2 * BLOCK
SHARE = BLK_DEV * PAIR
CACHE = 2 * SHARE
SHARD = CACHE + 2 * BLK_DEV + 2 * QROWS
OROWS = 2 * HEAD + 16
STEP = 4
LOWEST = -3.0e38
EXPO = HEAD**-0.5 * math.log2(math.e)
SEQ = ("z", "y", "core")


def seq_index(z, y, core):
    return (z * Y + y) * 2 + core


Y_LINES = [[[seq_index(z, y, core) for y in range(Y)] for z in range(Z)] for core in range(2)]
Z_LINES = [[[seq_index(z, y, core) for z in range(Z)] for y in range(Y)] for core in range(2)]
KV_LINES = Y_LINES[0] + Z_LINES[1]
Q_LINES = Z_LINES[0] + Y_LINES[1]


def scaled(x):
    largest = jnp.max(jnp.abs(x), axis=1, keepdims=True)
    power = 14.0 - jnp.floor(jnp.log2(jnp.maximum(largest, 1e-37)))
    power = jnp.clip(power, -113.0, 126.0)
    return (x * jnp.exp2(power)).astype(jnp.bfloat16), jnp.broadcast_to(power, x.shape).T[0:1, :]


def restored(x, power_row):
    down = jnp.broadcast_to(jnp.exp2(-power_row), (128, 128)).T
    return (x.astype(jnp.float32) * down).astype(jnp.bfloat16)


def pack_kernel(core_ref, k_ref, v_ref, q_ref, ids_ref, mine_ref, mine_powers_ref, mine_q_ref, other_ref, powers):
    core = core_ref[0]

    def cache(head, out_ref):
        def one_block(b, carry):
            at = pl.multiple_of(b * BLOCK, BLOCK)
            rows = jnp.concatenate([k_ref[head, pl.ds(at, BLOCK), :], v_ref[head, pl.ds(at, BLOCK), :]], axis=0)
            out, row = scaled(rows.astype(jnp.float32))
            out_ref[pl.ds(pl.multiple_of(b * PAIR, PAIR), PAIR), :] = out
            powers[pl.ds(b, 1), :] = row
            return carry

        lax.fori_loop(0, BLK_DEV, one_block, 0, unroll=4)
        return powers[...].astype(jnp.bfloat16)

    def queries(head, out_ref, first):
        rows = lax.broadcasted_iota(jnp.int32, (16, 128), 0)
        extra = ids_ref[head].astype(jnp.float32)
        for i in range(ROWS // 128):
            out, row = scaled(q_ref[head, i * 128 : (i + 1) * 128, :].astype(jnp.float32))
            out_ref[first + i * 128 : first + (i + 1) * 128, :] = out
            extra = jnp.where(rows == i, row, extra)
        out_ref[first + ROWS : first + QROWS, :] = extra.astype(jnp.bfloat16)

    mine_powers_ref[...] = cache(core, mine_ref)
    other_ref[SHARE : SHARE + BLK_DEV, :] = cache(1 - core, other_ref)
    queries(1 - core, mine_q_ref, 0)
    queries(core, other_ref, SHARE + BLK_DEV)


def window_kernel(first_ref, q_ref, k_ref, v_ref, o_ref):
    for rc in range(2):
        s = lax.dot_general(
            k_ref[pl.ds(128 * rc, 256), :],
            q_ref[rc],
            (((1,), (1,)), ((), ())),
            preferred_element_type=jnp.float32,
        )
        kpos = lax.broadcasted_iota(jnp.int32, s.shape, 0) - 128
        qpos = lax.broadcasted_iota(jnp.int32, s.shape, 1) & 127
        allowed = (kpos <= qpos) & (kpos > qpos - 128)
        if rc == 0:
            allowed = allowed & ((kpos >= 0) | (first_ref[0] == 0))
        s = jnp.where(allowed, s, LOWEST)
        top = jnp.max(s, axis=0, keepdims=True)
        p = jnp.exp2((s - top) * EXPO)
        total = jnp.sum(p, axis=0, keepdims=True)
        out = lax.dot_general(
            v_ref[pl.ds(128 * rc, 256), :],
            p.astype(jnp.bfloat16),
            (((0,), (0,)), ((), ())),
            preferred_element_type=jnp.float32,
        )
        o_ref[rc] = out / total


def memory_kernel(count_ref, place_ref, power_at_ref, q_ref, powers_ref, kv_ref, o_ref, buf, stage, q_buf, acc, top_s, sum_s, in_sems, out_sems):
    buf[...] = jnp.zeros(buf.shape, buf.dtype)

    def fetch(peer, rc, k):
        at = pl.multiple_of(place_ref[(peer * 2 + rc) * BLK_DEV + k], 16)
        return pltpu.make_async_copy(
            kv_ref.at[pl.ds(at, PAIR)], buf.at[peer % 2, rc, k], in_sems.at[peer % 2, rc, k]
        )

    def fetch_all(peer):
        for rc in range(2):
            def start(k, carry):
                fetch(peer, rc, k).start()
                return carry

            lax.fori_loop(0, count_ref[peer * 2 + rc], start, 0)

    def fetch_wait(peer):
        for rc in range(2):
            def wait(k, carry):
                fetch(peer, rc, k).wait()
                return carry

            lax.fori_loop(0, count_ref[peer * 2 + rc], wait, 0)

    def send(peer):
        return pltpu.make_async_copy(stage.at[peer % 2], o_ref.at[peer], out_sems.at[peer % 2])

    fetch_all(0)
    for peer in range(LINE):
        slot = peer % 2
        if peer + 1 < LINE:
            fetch_all(peer + 1)
        counts = [count_ref[peer * 2 + rc] for rc in range(2)]
        top_s[...] = jnp.full((2, 1, ROWS), LOWEST, jnp.float32)
        sum_s[...] = jnp.zeros((2, 1, ROWS), jnp.float32)
        acc[...] = jnp.zeros((2, HEAD, ROWS), jnp.float32)
        for rc in range(2):
            first = (peer * 2 + rc) * QROWS
            extra = q_ref[first + ROWS : first + QROWS, :].astype(jnp.float32)
            for i in range(ROWS // 128):
                q_buf[rc, i * 128 : (i + 1) * 128, :] = restored(
                    q_ref[first + i * 128 : first + (i + 1) * 128, :], extra[i : i + 1, :]
                )
        fetch_wait(peer)

        def one_step(step, carry):
            for rc in range(2):
                pairs = []
                for i in range(STEP):
                    at = power_at_ref[(peer * 2 + rc) * BLK_DEV + step * STEP + i]
                    pairs.append(restored(buf[slot, rc, step * STEP + i], powers_ref[pl.ds(at, 1), :]))
                keys = jnp.concatenate([pair[:BLOCK] for pair in pairs], axis=0)
                values = jnp.concatenate([pair[BLOCK:] for pair in pairs], axis=0)
                s = lax.dot_general(
                    keys, q_buf[rc], (((1,), (1,)), ((), ())), preferred_element_type=jnp.float32
                )
                rows = lax.broadcasted_iota(jnp.int32, s.shape, 0)
                s = jnp.where(rows < (counts[rc] - step * STEP) * BLOCK, s, LOWEST)
                top = jnp.maximum(top_s[rc], jnp.max(s, axis=0, keepdims=True))
                live = (step * STEP < counts[rc]).astype(jnp.float32)
                p = jnp.exp2((s - top) * EXPO) * live
                alpha = jnp.exp2((top_s[rc] - top) * EXPO)
                sum_s[rc] = sum_s[rc] * alpha + jnp.sum(p, axis=0, keepdims=True)
                acc[rc] = acc[rc] * alpha + lax.dot_general(
                    values, p.astype(jnp.bfloat16), (((0,), (0,)), ((), ())), preferred_element_type=jnp.float32
                )
                top_s[rc] = top
            return carry

        lax.fori_loop(0, (jnp.maximum(counts[0], counts[1]) + STEP - 1) // STEP, one_step, 0)
        if peer >= 2:
            send(peer - 2).wait()
        rows = lax.broadcasted_iota(jnp.int32, (16, ROWS), 0)
        pieces = jnp.zeros((16, ROWS), jnp.float32)
        for rc in range(2):
            total = sum_s[rc]
            some = total > 0.0
            safe = jnp.where(some, total, 1.0)
            stage[slot, rc * HEAD : (rc + 1) * HEAD, :] = (acc[rc] / safe).astype(jnp.bfloat16)
            level = jnp.where(some, top_s[rc] * EXPO + jnp.log2(safe), LOWEST)
            high = level.astype(jnp.bfloat16).astype(jnp.float32)
            mid = (level - high).astype(jnp.bfloat16).astype(jnp.float32)
            for i, piece in enumerate((high, mid, level - high - mid)):
                pieces = jnp.where(rows == 3 * rc + i, piece, pieces)
        stage[slot, 2 * HEAD :, :] = pieces.astype(jnp.bfloat16)
        send(peer).start()
    send(LINE - 2).wait()
    send(LINE - 1).wait()


def merge_kernel(part_ref, window_ref, gate_ref, o_ref):
    gate = gate_ref[...]
    for rc in range(2):
        levels = []
        for i in range(LINE):
            pieces = part_ref[i, 2 * HEAD :, :].astype(jnp.float32)[3 * rc : 3 * rc + 3, :]
            levels.append(pieces[0:1] + pieces[1:2] + pieces[2:3])
        top = functools.reduce(jnp.maximum, levels)
        shares = [jnp.exp2(level - top) for level in levels]
        scale = gate / functools.reduce(jnp.add, shares)
        mixed = (1.0 - gate) * window_ref[rc]
        for i in range(LINE):
            mixed = mixed + part_ref[i, rc * HEAD : (rc + 1) * HEAD, :].astype(jnp.float32) * (shares[i] * scale)
        for g in range(4):
            flat = mixed[:, g * 128 : (g + 1) * 128].T.astype(jnp.bfloat16)
            for x in range(X):
                o_ref[x * 2 + rc, :, g * 128 : (g + 1) * 128] = flat[x * 32 : (x + 1) * 32, :]


def on_device(queries, keys, values, mem_keys, mem_values, mem_ids, gate_logits):
    z, y, core = lax.axis_index("z"), lax.axis_index("y"), lax.axis_index("core")
    first_core = core == 0
    smem = pl.BlockSpec(memory_space=pltpu.SMEM)
    vmem = pl.BlockSpec(memory_space=pltpu.VMEM)
    swap = [(0, 1), (1, 0)]

    def mine_and_other(array):
        return jnp.where(first_core, array[0], array[1]), jnp.where(first_core, array[1], array[0])

    def by_core(mine, other):
        return jnp.where(first_core, mine, other), jnp.where(first_core, other, mine)

    by_head = queries.reshape(128, 2, 4, HEAD).transpose(1, 2, 0, 3).reshape(2, ROWS, HEAD)
    ids = jnp.concatenate([mem_ids // 64, mem_ids % 64], axis=2).astype(jnp.bfloat16)
    ids = jnp.pad(ids, ((0, 0), (4, 11), (0, HEAD - 2 * TOPK)))
    mine, mine_powers, mine_q, other = pl.pallas_call(
        pack_kernel,
        out_shape=[
            jax.ShapeDtypeStruct((SHARE, HEAD), jnp.bfloat16),
            jax.ShapeDtypeStruct((BLK_DEV, HEAD), jnp.bfloat16),
            jax.ShapeDtypeStruct((QROWS, HEAD), jnp.bfloat16),
            jax.ShapeDtypeStruct((SHARE + BLK_DEV + QROWS, HEAD), jnp.bfloat16),
        ],
        in_specs=[smem] + [vmem] * 4,
        out_specs=[vmem] * 4,
        scratch_shapes=[pltpu.VMEM((BLK_DEV, HEAD), jnp.float32)],
        compiler_params=pltpu.CompilerParams(vmem_limit_bytes=16 << 20),
        cost_estimate=pl.CostEstimate(flops=1 << 22, bytes_accessed=3 << 20, transcendentals=1 << 13),
        name="pack",
    )(
        core.astype(jnp.int32).reshape(1),
        mem_keys.transpose(1, 0, 2),
        mem_values.transpose(1, 0, 2),
        by_head,
        ids,
    )
    theirs = lax.ppermute(other, "core", swap)
    their_cache, their_powers, their_q = jnp.split(theirs, [SHARE, SHARE + BLK_DEV])
    shard = jnp.concatenate(
        [mine, their_cache, mine_powers, their_powers, *by_core(mine_q, their_q)], axis=0
    ).astype(jnp.float16)
    gathered = lax.all_gather(shard, SEQ, axis_index_groups=KV_LINES, tiled=True)
    parts = gathered.reshape(LINE, SHARD, HEAD)
    lists = lax.ppermute(parts[:, SHARD - 2 * QROWS :], "core", swap)
    lists = lists.reshape(2 * LINE * QROWS, HEAD).astype(jnp.bfloat16)
    cache = gathered.astype(jnp.bfloat16)
    powers = parts[:, CACHE : CACHE + 2 * BLK_DEV].reshape(2 * LINE * BLK_DEV, HEAD).astype(jnp.float32)

    coded = lists.reshape(2 * LINE, QROWS, HEAD)[:, ROWS + 4, : 2 * TOPK].astype(jnp.int32)
    wanted = coded[:, :TOPK] * 64 + coded[:, TOPK:]
    owner, local = wanted // BLK_DEV, wanted % BLK_DEV
    owner_z, owner_y, owner_core = owner // (2 * Y), (owner // 2) % Y, owner % 2
    here = jnp.where(first_core, owner_z == z, owner_y == y)
    position = jnp.where(first_core, owner_y, owner_z)
    index = (position * 2 + (owner_core != core).astype(jnp.int32)) * BLK_DEV + local
    rank = jnp.sum(
        (here[:, None, :] & (jnp.arange(TOPK)[None, None, :] < jnp.arange(TOPK)[None, :, None])).astype(jnp.int32),
        axis=2,
    )
    match = here[:, :, None] & (rank[:, :, None] == jnp.arange(BLK_DEV)[None, None, :])
    indices = jnp.sum(jnp.where(match, index[:, :, None], 0), axis=1).reshape(-1)
    places = (indices // (2 * BLK_DEV)) * SHARD + (indices % (2 * BLK_DEV)) * PAIR
    counts = jnp.sum(here.astype(jnp.int32), axis=1)

    partial = pl.pallas_call(
        memory_kernel,
        out_shape=jax.ShapeDtypeStruct((LINE, OROWS, ROWS), jnp.bfloat16),
        in_specs=[smem] * 3 + [vmem] * 2 + [pl.BlockSpec(memory_space=pltpu.HBM)],
        out_specs=pl.BlockSpec(memory_space=pltpu.HBM),
        scratch_shapes=[
            pltpu.VMEM((2, 2, BLK_DEV, PAIR, HEAD), jnp.bfloat16),
            pltpu.VMEM((2, OROWS, ROWS), jnp.bfloat16),
            pltpu.VMEM((2, ROWS, HEAD), jnp.bfloat16),
            pltpu.VMEM((2, HEAD, ROWS), jnp.float32),
            pltpu.VMEM((2, 1, ROWS), jnp.float32),
            pltpu.VMEM((2, 1, ROWS), jnp.float32),
            pltpu.SemaphoreType.DMA((2, 2, BLK_DEV)),
            pltpu.SemaphoreType.DMA((2,)),
        ],
        compiler_params=pltpu.CompilerParams(vmem_limit_bytes=24 << 20),
        cost_estimate=pl.CostEstimate(
            flops=4 * 64 * ROWS * BLOCK * HEAD, bytes_accessed=6 << 20, transcendentals=64 * ROWS * BLOCK
        ),
        name="memory",
    )(counts, places, indices, lists, powers, cache)
    returned = lax.all_to_all(
        partial, SEQ, split_axis=0, concat_axis=0, axis_index_groups=Q_LINES, tiled=True
    )

    q_mine, q_other = mine_and_other(by_head)
    k_mine, k_other = mine_and_other(keys.transpose(1, 0, 2))
    v_mine, v_other = mine_and_other(values.transpose(1, 0, 2))
    near = lax.ppermute(jnp.concatenate([q_other, k_other, v_other], axis=0), "core", swap)
    q_first, q_second = by_core(q_mine, near[:ROWS])
    k_first, k_second = by_core(k_mine, near[ROWS : ROWS + 128])
    v_first, v_second = by_core(v_mine, near[ROWS + 128 :])
    onward = [(2 * i + c, 2 * i + 2 + c) for i in range(Z * Y - 1) for c in range(2)]
    before = lax.ppermute(jnp.concatenate([k_second, v_second], axis=0), SEQ, onward)
    is_first = ((z == 0) & (y == 0)).astype(jnp.int32).reshape(1)
    window = pl.pallas_call(
        window_kernel,
        out_shape=jax.ShapeDtypeStruct((2, HEAD, ROWS), jnp.float32),
        in_specs=[smem] + [vmem] * 3,
        out_specs=vmem,
        compiler_params=pltpu.CompilerParams(vmem_limit_bytes=16 << 20),
        cost_estimate=pl.CostEstimate(
            flops=4 * 2 * ROWS * 256 * HEAD, bytes_accessed=1 << 20, transcendentals=2 * ROWS * 256
        ),
        name="window",
    )(
        is_first,
        jnp.stack([q_first, q_second]),
        jnp.concatenate([before[:128], k_first, k_second], axis=0),
        jnp.concatenate([before[128:], v_first, v_second], axis=0),
    )

    gate = jax.nn.sigmoid(gate_logits).reshape(2, 4)
    gate = jnp.repeat(jnp.where(first_core, gate[0], gate[1]), 128)[None, :]
    mixed = pl.pallas_call(
        merge_kernel,
        out_shape=jax.ShapeDtypeStruct((2 * X, 32, ROWS), jnp.bfloat16),
        in_specs=[vmem] * 3,
        out_specs=vmem,
        compiler_params=pltpu.CompilerParams(vmem_limit_bytes=16 << 20),
        cost_estimate=pl.CostEstimate(flops=1 << 22, bytes_accessed=4 << 20, transcendentals=1 << 13),
        name="merge",
    )(returned, window, gate)
    rows = lax.all_to_all(mixed, ("head", "core"), split_axis=0, concat_axis=0, tiled=True)
    return rows.transpose(1, 0, 2).reshape(32, 2 * X * ROWS)


def solution(mesh):
    fine = Mesh(mesh.devices.reshape(Z, Y, 2, X), ("z", "y", "core", "head"))
    placed = (
        P(SEQ, "head", None),
        P(SEQ, "head", None),
        P(SEQ, "head", None),
        P(SEQ, "head", None),
        P(SEQ, "head", None),
        P("head", SEQ, None),
        P("head"),
    )
    return jax.shard_map(
        on_device, mesh=fine, in_specs=placed, out_specs=P(SEQ + ("head",), None), check_vma=False
    )
```

time: 171 us -> 172 us (level)
  blocking collectives: 46.9 us -> 67.5 us
  starting transfers between devices: 42.7 us -> 23.6 us
  between operations: 13.9 us -> 0.31 us
  Pallas kernels: 15.9 us -> 27 us
  other arithmetic: 3.31 us -> 13.8 us
  waiting for transfers between devices: 31.8 us -> 26.6 us
  local copies, waits for them, and re-layouts: 16 us -> 12.7 us
    all_gather x0 -> x1, blocking collectives: none -> 55.2 us  [on_device(): lax.all_gather(shard, SEQ, axis_index_groups=KV_LINES, tiled=True)]
    all_to_all x1, blocking collectives: 46.9 us -> 12.4 us  [on_device(): lax.all_to_all(mixed, ('head', 'core'), split_axis=0, concat_axis=0, tile...]
    ppermute x9 -> x2, starting transfers between devices: 34.8 us -> 4.23 us  [the longest x1 2.3 us: on_device(): lists = lax.ppermute(parts[:, SHARD - 2 * QROWS:], 'core', swap)]
    ppermute x1, waiting for transfers between devices: 0.01 us -> 18.2 us  [on_device(): lax.ppermute(jnp.concatenate([k_second, v_second], axis=0), SEQ, onward)]
    all_gather x1 -> x0, waiting for transfers between devices: 16.8 us -> none  [on_device(): lax.all_gather(cache, SEQ, axis_index_groups=KV_LINES, tiled=True)]
    ppermute x9 -> x2, waiting for transfers between devices: 14 us -> 1.29 us  [the longest x1 1.29 us: on_device(): lax.ppermute(jnp.concatenate([q_other, k_other, v_other], axis=0), 'core'...]
    convert_element_type x1 -> x5, other arithmetic: 0.01 us -> 11.7 us  [the longest x1 9.46 us: on_device(): cache = gathered.astype(jnp.bfloat16)]
    pallas_call x3 -> x4, Pallas kernels: 15.9 us -> 27 us  [the longest x1 23.5 us: on_device(): pl.pallas_call(memory_kernel, out_shape=jax.ShapeDtypeStruct((LINE, OROWS...]
  transfers between devices with their start and end apart: 13 -> 5, of which waited for: 7 -> 4; matrix products, arithmetic and copies ran while one was open for 1% -> 6% of each run, Pallas kernels for 9% -> 0%
where the time goes in v3:
time: 172 us
  blocking collectives  67.5 us (39%)
  Pallas kernels  27 us (16%)
  waiting for transfers between devices  26.6 us (15%)
  starting transfers between devices  23.6 us (14%)
  other arithmetic  13.8 us (8%)
  local copies, waits for them, and re-layouts  12.7 us (7%)
    all_gather x1, blocking collectives, on_device(): lax.all_gather(shard, SEQ, axis_index_groups=KV_LINES, tiled=True)  55.2 us
    pallas_call x1, Pallas kernels, on_device(): pl.pallas_call(memory_kernel, out_shape=jax.ShapeDtypeStruct((LINE, OROWS...  23.5 us
    ppermute x1, waiting for transfers between devices, on_device(): lax.ppermute(jnp.concatenate([k_second, v_second], axis=0), SEQ, onward)  18.2 us
    all_to_all x1, blocking collectives, on_device(): lax.all_to_all(mixed, ('head', 'core'), split_axis=0, concat_axis=0, tile...  12.4 us
    convert_element_type x1, other arithmetic, on_device(): cache = gathered.astype(jnp.bfloat16)  9.46 us
    ppermute x1, starting transfers between devices, on_device(): theirs = lax.ppermute(other, 'core', swap)  8.79 us
    unnamed x16, local copies, waits for them, and re-layouts  8.21 us
    all_to_all x1, starting transfers between devices, on_device(): lax.all_to_all(partial, SEQ, split_axis=0, concat_axis=0, axis_index_grou...  7.2 us
  transfers between devices with their start and end apart: 5, of which 4 were waited for; matrix products, arithmetic and copies ran while one was open for 6% of the time, Pallas kernels for 0%

profile of v3, /device:TPU:1, one launch (start us, length us, event | category | flops | bytes accessed | tf_op | source)
XLA Modules:
  0.0 171.5 jit_solution(9657820193619178258)
XLA Ops:
  0.0 1.0 copy.39
  1.0 0.7 fusion.20
  1.7 1.3 copy_bitcast_fusion
  3.0 0.1 fusion.6.ids_ref
  3.1 2.0 %pack.1 = (bf16[2048,128]{1,0:T(8,128)(2,1)S(1)}, bf16[16,128]{1,0:T(8,128)(2,1)S(1)}, bf16[528,128]{1,0:T(8,128)(2,1)S(1)}, bf16[2592,128]{1,0:T(8,128)(2,1)S(1)}) custom-call(s32[1]{0:T(128)} %bitcast.core_ref, bf16[2,1024,128]{2,1,0:T(8,128)(2,1)S(1)} %get-tuple-element.36.k_ref, bf16[2,1024,128]{2,1,0:T(8,128)(2,1)S(1)} %get-tuple-element.35.v_ref, ...), custom_call_target="tpu_custom_call" | custom-call | flops 4194304 | bytes 3145728 | tf_op jit(solution)/shard_map/pack/pallas_call | solution.py:235
  5.2 8.8 %collective-permute-start = (bf16[2592,128]{1,0:T(8,128)(2,1)S(1)}, bf16[2592,128]{1,0:T(8,128)(2,1)S(1)}, u32[]{:S(2)}, u32[]{:S(2)}) collective-permute-start(bf16[2592,128]{1,0:T(8,128)(2,1)S(1)} %get-tuple-element.10), channel_id=1, source_target_pairs={{0,4},{4,0},{1,5},{5,1},{2,6},{6,2},{3,7},{7,3},{8,12},{12,8},{9,1... | collective-permute-start | bytes 1990664 | tf_op jit(solution)/shard_map/ppermute | solution.py:256
  14.0 1.7 collective-permute-done
  15.7 0.1 slice_dynamic-update-slice_fusion
  15.8 0.1 select_dynamic-update-slice_fusion.1
  15.8 0.1 select_dynamic-update-slice_fusion
  15.9 0.3 convert_element_type.45
  16.2 55.2 %all-gather.1 = f16[41472,128]{1,0:T(8,128)(2,1)S(1)} all-gather(f16[5184,128]{1,0:T(8,128)(2,1)S(1)} %convert_element_type.45), channel_id=1, replica_groups={{0,8,16,24,32,40,48,56},{64,72,80,88,96,104,112,120},{128,136,144,152,1..., dimensions={0}, use_global_device_ids=true | all-gather | bytes 11943936 | tf_op jit(solution)/shard_map/all_gather | solution.py:261
  71.3 0.0 copy-start.1
  71.3 4.0 %copy-done.1 = f16[41472,128]{1,0:T(8,128)(2,1)} copy-done((f16[41472,128]{1,0:T(8,128)(2,1)}, f16[41472,128]{1,0:T(8,128)(2,1)S(1)}, u32[]{:S(2)}) %copy-start.1) | copy-done | bytes 10616856
  75.4 0.4 slice.82
  75.8 2.3 %collective-permute-start.1 = (f16[8,1056,128]{2,1,0:T(8,128)(2,1)S(1)}, f16[8,1056,128]{2,1,0:T(8,128)(2,1)}, u32[]{:S(2)}, u32[]{:S(2)}) collective-permute-start(f16[8,1056,128]{2,1,0:T(8,128)(2,1)S(1)} %slice.82), channel_id=1, source_target_pairs={{0,4},{4,0},{1,5},{5,1},{2,6},{6,2},{3,7},{7,3},{8,12},{12,8},{9,1... | collective-permute-start | bytes 6488072 | tf_op jit(solution)/shard_map/ppermute | solution.py:263
  78.1 0.9 slice.86
  79.0 9.5 %convert_element_type.56.kv_ref = bf16[41472,128]{1,0:T(8,128)(2,1)} convert(f16[41472,128]{1,0:T(8,128)(2,1)} %copy-done.1) | non-fusion elementwise | flops 5308416 | bytes 21233664 | tf_op jit(solution)/shard_map/convert_element_type | solution.py:265
  88.5 0.0 collective-permute-done.1
  88.5 2.0 %convert_element_type.46 = bf16[8,1056,128]{2,1,0:T(8,128)(2,1)S(1)} convert(f16[8,1056,128]{2,1,0:T(8,128)(2,1)} %collective-permute-done.1) | non-fusion elementwise | flops 1081344 | bytes 4325376 | tf_op jit(solution)/shard_map/convert_element_type | solution.py:264
  90.5 0.1 fusion.11
  90.6 0.1 convert_reduce_fusion.1
  90.7 0.4 convert_reduce_fusion
  91.1 0.3 select_reduce_fusion
  91.4 0.1 reshape.105.power_at_ref
  91.5 0.0 copy-start
  91.5 4.0 %copy-done = bf16[41472,128]{1,0:T(8,128)(2,1)S(1)} copy-done((bf16[41472,128]{1,0:T(8,128)(2,1)S(1)}, bf16[41472,128]{1,0:T(8,128)(2,1)}, u32[]{:S(2)}) %copy-start) | copy-done | bytes 10616856
  95.6 23.5 %memory.1 = bf16[8,272,512]{2,1,0:T(8,128)(2,1)} custom-call(s32[16]{0:T(128)S(1)} %get-tuple-element.15.count_ref, s32[256]{0:T(256)S(1)} %fusion.18.place_ref, s32[256]{0:T(256)S(1)} %reshape.105.power_at_ref, bf16[8448,128]{1,0:T(8,128)(2,1)S(1)} %bitcast.50, f32[256,128]{1,0:T(8,128)S(1)} %bitcast_convert_fusion.powers_ref, bf16[41472,128]{1,0:T(8,128)(2,1)S(1)} %copy-done), custom_call_target="tpu_custom_call" | custom-call | flops 1073741824 | bytes 6291456 | tf_op jit(solution)/shard_map/memory/pallas_call | solution.py:284
  119.1 0.0 copy-start.2
  119.1 0.0 copy-start.3
  119.1 7.2 %all-to-all-start = ((bf16[8,272,512]{2,1,0:T(8,128)(2,1)}), bf16[8,272,512]{2,1,0:T(8,128)(2,1)S(1)}, u32[]{:S(2)}, u32[]{:S(2)}) async-start(bf16[8,272,512]{2,1,0:T(8,128)(2,1)} %memory.1), calls=%async_computation | async-start | bytes 4456448 | tf_op jit(solution)/shard_map/all_to_all | solution.py:305
  126.3 0.0 copy-done.2
  126.3 0.0 copy-start.4
  126.3 0.0 copy-done.3
  126.4 1.9 %collective-permute-start.2 = (bf16[768,128]{1,0:T(8,128)(2,1)S(1)}, bf16[768,128]{1,0:T(8,128)(2,1)S(1)}, u32[]{:S(2)}, u32[]{:S(2)}) collective-permute-start(bf16[768,128]{1,0:T(8,128)(2,1)S(1)} %pad_maximum_fusion.1), channel_id=1, source_target_pairs={{0,4},{4,0},{1,5},{5,1},{2,6},{6,2},{3,7},{7,3},{8,12},{12,8},{9,1... | collective-permute-start | bytes 589832 | tf_op jit(solution)/shard_map/ppermute | solution.py:312
  128.4 0.0 copy-done.4
  128.4 0.1 broadcast_select_fusion.4
  128.5 1.3 collective-permute-done.2
  129.8 3.4 %collective-permute-start.3 = (bf16[256,128]{1,0:T(8,128)(2,1)S(1)}, bf16[256,128]{1,0:T(8,128)(2,1)S(1)}, u32[]{:S(2)}, u32[]{:S(2)}) collective-permute-start(bf16[256,128]{1,0:T(8,128)(2,1)S(1)} %pad_maximum_fusion.4), channel_id=1, source_target_pairs={{0,8},{4,12},{8,16},{12,20},{16,24},{20,28},{24,32},{28,36},{32,40... | collective-permute-start | bytes 196616 | tf_op jit(solution)/shard_map/ppermute | solution.py:317
  133.2 18.2 %collective-permute-done.3 = bf16[256,128]{1,0:T(8,128)(2,1)S(1)} collective-permute-done((bf16[256,128]{1,0:T(8,128)(2,1)S(1)}, bf16[256,128]{1,0:T(8,128)(2,1)S(1)}, u32[]{:S(2)}, u32[]{:S(2)}) %collective-permute-start.3) | collective-permute-done | bytes 65568 | tf_op jit(solution)/shard_map/ppermute | solution.py:317
  151.4 0.8 window.1.window_ref
  152.3 5.4 %all-to-all-done.part_ref = bf16[8,272,512]{2,1,0:T(8,128)(2,1)S(1)} async-done(((bf16[8,272,512]{2,1,0:T(8,128)(2,1)}), bf16[8,272,512]{2,1,0:T(8,128)(2,1)S(1)}, u32[]{:S(2)}, u32[]{:S(2)}) %all-to-all-start) | async-done | bytes 2228256 | tf_op jit(solution)/shard_map/all_to_all | solution.py:305
  157.7 0.1 broadcast_in_dim.24
  157.8 0.6 merge.1
  158.4 12.4 %all_to_all.10 = bf16[8,32,512]{2,1,0:T(8,128)(2,1)S(1)} all-to-all(bf16[8,32,512]{2,1,0:T(8,128)(2,1)S(1)} %merge.1), channel_id=1, replica_groups=mesh['z'=8,'y'=8,'core'=2,'head'=4] {'head','core'}, dimensions={0} | all-to-all | bytes 524288 | tf_op jit(solution)/shard_map/all_to_all | solution.py:347
  170.8 0.7 copy.27
  (22 shorter events, 0.3 us)
Async XLA Ops:
  5.2 10.5 %collective-permute-start = (bf16[2592,128]{1,0:T(8,128)(2,1)S(1)}, bf16[2592,128]{1,0:T(8,128)(2,1)S(1)}, u32[]{:S(2)}, u32[]{:S(2)}) collective-permute-start(bf16[2592,128]{1,0:T(8,128)(2,1)S(1)} %get-tuple-element.10), channel_id=1, source_target_pairs={{0,4},{4,0},{1,5},{5,1},{2,6},{6,2},{3,7},{7,3},{8,12},{12,8},{9,1... | collective-permute-start | bytes 1990664 | tf_op jit(solution)/shard_map/ppermute | solution.py:256
  71.3 4.0 %copy-start.1 = (f16[41472,128]{1,0:T(8,128)(2,1)}, f16[41472,128]{1,0:T(8,128)(2,1)S(1)}, u32[]{:S(2)}) copy-start(f16[41472,128]{1,0:T(8,128)(2,1)S(1)} %all-gather.1) | copy-start | bytes 31850500
  75.8 12.7 %collective-permute-start.1 = (f16[8,1056,128]{2,1,0:T(8,128)(2,1)S(1)}, f16[8,1056,128]{2,1,0:T(8,128)(2,1)}, u32[]{:S(2)}, u32[]{:S(2)}) collective-permute-start(f16[8,1056,128]{2,1,0:T(8,128)(2,1)S(1)} %slice.82), channel_id=1, source_target_pairs={{0,4},{4,0},{1,5},{5,1},{2,6},{6,2},{3,7},{7,3},{8,12},{12,8},{9,1... | collective-permute-start | bytes 6488072 | tf_op jit(solution)/shard_map/ppermute | solution.py:263
  91.5 4.0 %copy-start = (bf16[41472,128]{1,0:T(8,128)(2,1)S(1)}, bf16[41472,128]{1,0:T(8,128)(2,1)}, u32[]{:S(2)}) copy-start(bf16[41472,128]{1,0:T(8,128)(2,1)} %convert_element_type.56.kv_ref) | copy-start | bytes 31850500
  119.1 7.2 %copy-start.2 = (bf16[128,2,128]{2,1,0:T(2,128)(2,1)S(1)}, bf16[128,2,128]{2,1,0:T(2,128)(2,1)}, u32[]{:S(2)}) copy-start(bf16[128,2,128]{2,1,0:T(2,128)(2,1)} %param.9) | copy-start | bytes 196612
  119.1 7.2 %copy-start.3 = (bf16[128,2,128]{2,1,0:T(2,128)(2,1)S(1)}, bf16[128,2,128]{2,1,0:T(2,128)(2,1)}, u32[]{:S(2)}) copy-start(bf16[128,2,128]{2,1,0:T(2,128)(2,1)} %param.8) | copy-start | bytes 196612
  119.1 38.6 %all-to-all-start = ((bf16[8,272,512]{2,1,0:T(8,128)(2,1)}), bf16[8,272,512]{2,1,0:T(8,128)(2,1)S(1)}, u32[]{:S(2)}, u32[]{:S(2)}) async-start(bf16[8,272,512]{2,1,0:T(8,128)(2,1)} %memory.1), calls=%async_computation | async-start | bytes 4456448 | tf_op jit(solution)/shard_map/all_to_all | solution.py:305
  126.3 2.1 %copy-start.4 = (f32[8]{0:T(128)S(1)}, f32[8]{0:T(128)}, u32[]{:S(2)}) copy-start(f32[8]{0:T(128)} %param.13) | copy-start | bytes 100
  126.4 3.3 %collective-permute-start.2 = (bf16[768,128]{1,0:T(8,128)(2,1)S(1)}, bf16[768,128]{1,0:T(8,128)(2,1)S(1)}, u32[]{:S(2)}, u32[]{:S(2)}) collective-permute-start(bf16[768,128]{1,0:T(8,128)(2,1)S(1)} %pad_maximum_fusion.1), channel_id=1, source_target_pairs={{0,4},{4,0},{1,5},{5,1},{2,6},{6,2},{3,7},{7,3},{8,12},{12,8},{9,1... | collective-permute-start | bytes 589832 | tf_op jit(solution)/shard_map/ppermute | solution.py:312
  129.8 21.6 %collective-permute-start.3 = (bf16[256,128]{1,0:T(8,128)(2,1)S(1)}, bf16[256,128]{1,0:T(8,128)(2,1)S(1)}, u32[]{:S(2)}, u32[]{:S(2)}) collective-permute-start(bf16[256,128]{1,0:T(8,128)(2,1)S(1)} %pad_maximum_fusion.4), channel_id=1, source_target_pairs={{0,8},{4,12},{8,16},{12,20},{16,24},{20,28},{24,32},{28,36},{32,40... | collective-permute-start | bytes 196616 | tf_op jit(solution)/shard_map/ppermute | solution.py:317

commit v4 on v3

--- a/solution.py
+++ b/solution.py
@@ -50,8 +50,12 @@
     return (x.astype(jnp.float32) * down).astype(jnp.bfloat16)
 
 
-def pack_kernel(core_ref, k_ref, v_ref, q_ref, ids_ref, mine_ref, mine_powers_ref, mine_q_ref, other_ref, powers):
-    core = core_ref[0]
+def pack_kernel(
+    where_ref, k_ref, v_ref, q_ref, ids_ref, mine_ref, mine_powers_ref, mine_q_ref, other_ref, place_ref, powers
+):
+    for i in range(3):
+        place_ref[i : i + 1, :] = jnp.full((1, 128), where_ref[i], jnp.int32)
+    core = where_ref[2]
 
     def cache(head, out_ref):
         def one_block(b, carry):
@@ -110,7 +114,7 @@
     buf[...] = jnp.zeros(buf.shape, buf.dtype)
 
     def fetch(peer, rc, k):
-        at = pl.multiple_of(place_ref[(peer * 2 + rc) * BLK_DEV + k], 16)
+        at = pl.multiple_of(place_ref[peer * 2 + rc, k], 16)
         return pltpu.make_async_copy(
             kv_ref.at[pl.ds(at, PAIR)], buf.at[peer % 2, rc, k], in_sems.at[peer % 2, rc, k]
         )
@@ -156,7 +160,7 @@
             for rc in range(2):
                 pairs = []
                 for i in range(STEP):
-                    at = power_at_ref[(peer * 2 + rc) * BLK_DEV + step * STEP + i]
+                    at = power_at_ref[peer * 2 + rc, step * STEP + i]
                     pairs.append(restored(buf[slot, rc, step * STEP + i], powers_ref[pl.ds(at, 1), :]))
                 keys = jnp.concatenate([pair[:BLOCK] for pair in pairs], axis=0)
                 values = jnp.concatenate([pair[BLOCK:] for pair in pairs], axis=0)
@@ -232,22 +236,23 @@
     by_head = queries.reshape(128, 2, 4, HEAD).transpose(1, 2, 0, 3).reshape(2, ROWS, HEAD)
     ids = jnp.concatenate([mem_ids // 64, mem_ids % 64], axis=2).astype(jnp.bfloat16)
     ids = jnp.pad(ids, ((0, 0), (4, 11), (0, HEAD - 2 * TOPK)))
-    mine, mine_powers, mine_q, other = pl.pallas_call(
+    mine, mine_powers, mine_q, other, placed = pl.pallas_call(
         pack_kernel,
         out_shape=[
             jax.ShapeDtypeStruct((SHARE, HEAD), jnp.bfloat16),
             jax.ShapeDtypeStruct((BLK_DEV, HEAD), jnp.bfloat16),
             jax.ShapeDtypeStruct((QROWS, HEAD), jnp.bfloat16),
             jax.ShapeDtypeStruct((SHARE + BLK_DEV + QROWS, HEAD), jnp.bfloat16),
+            jax.ShapeDtypeStruct((8, 128), jnp.int32),
         ],
         in_specs=[smem] + [vmem] * 4,
-        out_specs=[vmem] * 4,
+        out_specs=[vmem] * 5,
         scratch_shapes=[pltpu.VMEM((BLK_DEV, HEAD), jnp.float32)],
         compiler_params=pltpu.CompilerParams(vmem_limit_bytes=16 << 20),
         cost_estimate=pl.CostEstimate(flops=1 << 22, bytes_accessed=3 << 20, transcendentals=1 << 13),
         name="pack",
     )(
-        core.astype(jnp.int32).reshape(1),
+        jnp.stack([z, y, core]).astype(jnp.int32),
         mem_keys.transpose(1, 0, 2),
         mem_values.transpose(1, 0, 2),
         by_head,
@@ -269,15 +274,16 @@
     wanted = coded[:, :TOPK] * 64 + coded[:, TOPK:]
     owner, local = wanted // BLK_DEV, wanted % BLK_DEV
     owner_z, owner_y, owner_core = owner // (2 * Y), (owner // 2) % Y, owner % 2
-    here = jnp.where(first_core, owner_z == z, owner_y == y)
-    position = jnp.where(first_core, owner_y, owner_z)
-    index = (position * 2 + (owner_core != core).astype(jnp.int32)) * BLK_DEV + local
+    my_z, my_y, my_core = (placed[i : i + 1, :TOPK] for i in range(3))
+    here = jnp.where(my_core == 0, owner_z == my_z, owner_y == my_y)
+    position = jnp.where(my_core == 0, owner_y, owner_z)
+    index = (position * 2 + (owner_core != my_core).astype(jnp.int32)) * BLK_DEV + local
     rank = jnp.sum(
         (here[:, None, :] & (jnp.arange(TOPK)[None, None, :] < jnp.arange(TOPK)[None, :, None])).astype(jnp.int32),
         axis=2,
     )
     match = here[:, :, None] & (rank[:, :, None] == jnp.arange(BLK_DEV)[None, None, :])
-    indices = jnp.sum(jnp.where(match, index[:, :, None], 0), axis=1).reshape(-1)
+    indices = jnp.sum(jnp.where(match, index[:, :, None], 0), axis=1)
     places = (indices // (2 * BLK_DEV)) * SHARD + (indices % (2 * BLK_DEV)) * PAIR
     counts = jnp.sum(here.astype(jnp.int32), axis=1)
 

time: 172 us -> 158 us (0.919)
  other arithmetic: 13.8 us -> 4.06 us
  local copies, waits for them, and re-layouts: 12.7 us -> 5.11 us
  waiting for transfers between devices: 26.6 us -> 28.7 us
    convert_element_type x1, other arithmetic: 9.46 us -> 1.25 us  [on_device(): cache = gathered.astype(jnp.bfloat16)]
    unnamed x16 -> x14, local copies, waits for them, and re-layouts: 8.21 us -> 1.53 us
    ppermute x1, waiting for transfers between devices: 0.01 us -> 2.52 us  [on_device(): lists = lax.ppermute(parts[:, SHARD - 2 * QROWS:], 'core', swap)]
    pallas_call x1, Pallas kernels: 23.5 us -> 21.3 us  [on_device(): pl.pallas_call(memory_kernel, out_shape=jax.ShapeDtypeStruct((LINE, OROWS...]
  transfers between devices with their start and end apart: 5 -> 5, of which waited for: 4 -> 5; matrix products, arithmetic and copies ran while one was open for 6% -> 1% of each run, Pallas kernels for 0% -> 1%
where the time goes in v4:
time: 158 us; the launch traced here: 157 us
  blocking collectives  68.5 us (43%)
  waiting for transfers between devices  28.7 us (18%)
  Pallas kernels  25.4 us (16%)
  starting transfers between devices  25.1 us (16%)
  local copies, waits for them, and re-layouts  5.11 us (3%)
  other arithmetic  4.06 us (3%)
    all_gather x1, blocking collectives, on_device(): lax.all_gather(shard, SEQ, axis_index_groups=KV_LINES, tiled=True)  55.2 us
    pallas_call x1, Pallas kernels, on_device(): pl.pallas_call(memory_kernel, out_shape=jax.ShapeDtypeStruct((LINE, OROWS...  21.3 us
    ppermute x1, waiting for transfers between devices, on_device(): lax.ppermute(jnp.concatenate([k_second, v_second], axis=0), SEQ, onward)  18.2 us
    all_to_all x1, blocking collectives, on_device(): lax.all_to_all(mixed, ('head', 'core'), split_axis=0, concat_axis=0, tile...  13.3 us
    ppermute x1, starting transfers between devices, on_device(): theirs = lax.ppermute(other, 'core', swap)  8.79 us
    all_to_all x1, starting transfers between devices, on_device(): lax.all_to_all(partial, SEQ, split_axis=0, concat_axis=0, axis_index_grou...  8.41 us
    all_to_all x1, waiting for transfers between devices, on_device(): lax.all_to_all(partial, SEQ, split_axis=0, concat_axis=0, axis_index_grou...  5.41 us
    ppermute x1, starting transfers between devices, on_device(): lax.ppermute(jnp.concatenate([q_other, k_other, v_other], axis=0), 'core'...  3.22 us
  transfers between devices with their start and end apart: 5, of which 5 were waited for; matrix products, arithmetic and copies ran while one was open for 1% of the time, Pallas kernels for 1%

profile of v4, /device:TPU:1, one launch (start us, length us, event | category | flops | bytes accessed | tf_op | source)
XLA Modules:
  0.0 157.3 jit_solution(4133890910455939912)
XLA Ops:
  0.0 1.0 copy.39
  1.0 0.7 fusion.25
  1.7 1.3 copy_bitcast_fusion
  3.0 0.1 fusion.6.ids_ref
  3.1 0.1 pad_add_fusion.where_ref
  3.2 2.6 %pack.1 = (bf16[2048,128]{1,0:T(8,128)(2,1)S(1)}, bf16[16,128]{1,0:T(8,128)(2,1)S(1)}, bf16[528,128]{1,0:T(8,128)(2,1)S(1)}, bf16[2592,128]{1,0:T(8,128)(2,1)S(1)}, s32[8,128]{1,0:T(8,128)S(1)}) custom-call(s32[3]{0:T(128)S(1)} %pad_add_fusion.where_ref, bf16[2,1024,128]{2,1,0:T(8,128)(2,1)S(1)} %get-tuple-element.41.k_ref, ...), custom_call_target="tpu_custom_call" | custom-call | flops 4194304 | bytes 3145728 | tf_op jit(solution)/shard_map/pack/pallas_call | solution.py:239
  5.8 8.8 %collective-permute-start = (bf16[2592,128]{1,0:T(8,128)(2,1)S(1)}, bf16[2592,128]{1,0:T(8,128)(2,1)S(1)}, u32[]{:S(2)}, u32[]{:S(2)}) collective-permute-start(bf16[2592,128]{1,0:T(8,128)(2,1)S(1)} %get-tuple-element.12), channel_id=1, source_target_pairs={{0,4},{4,0},{1,5},{5,1},{2,6},{6,2},{3,7},{7,3},{8,12},{12,8},{9,1... | collective-permute-start | bytes 1990664 | tf_op jit(solution)/shard_map/ppermute | solution.py:261
  14.6 1.7 %collective-permute-done = bf16[2592,128]{1,0:T(8,128)(2,1)S(1)} collective-permute-done((bf16[2592,128]{1,0:T(8,128)(2,1)S(1)}, bf16[2592,128]{1,0:T(8,128)(2,1)S(1)}, u32[]{:S(2)}, u32[]{:S(2)}) %collective-permute-start) | collective-permute-done | bytes 663584 | tf_op jit(solution)/shard_map/ppermute | solution.py:261
  16.3 0.1 slice_dynamic-update-slice_fusion
  16.4 0.1 select_dynamic-update-slice_fusion.1
  16.5 0.1 select_dynamic-update-slice_fusion
  16.5 0.3 convert_element_type.45
  16.8 55.2 %all-gather.1 = f16[41472,128]{1,0:T(8,128)(2,1)S(1)} all-gather(f16[5184,128]{1,0:T(8,128)(2,1)S(1)} %convert_element_type.45), channel_id=1, replica_groups={{0,8,16,24,32,40,48,56},{64,72,80,88,96,104,112,120},{128,136,144,152,1..., dimensions={0}, use_global_device_ids=true | all-gather | bytes 11943936 | tf_op jit(solution)/shard_map/all_gather | solution.py:266
  71.9 0.4 slice.94
  72.4 2.3 %collective-permute-start.1 = (f16[8,1056,128]{2,1,0:T(8,128)(2,1)S(1)}, f16[8,1056,128]{2,1,0:T(8,128)(2,1)S(1)}, u32[]{:S(2)}, u32[]{:S(2)}) collective-permute-start(f16[8,1056,128]{2,1,0:T(8,128)(2,1)S(1)} %slice.94), channel_id=1, source_target_pairs={{0,4},{4,0},{1,5},{5,1},{2,6},{6,2},{3,7},{7,3},{8,12},{12,8},{9,1... | collective-permute-start | bytes 6488072 | tf_op jit(solution)/shard_map/ppermute | solution.py:268
  74.7 1.2 convert_element_type.56.kv_ref
  76.0 2.5 %collective-permute-done.1 = f16[8,1056,128]{2,1,0:T(8,128)(2,1)S(1)} collective-permute-done((f16[8,1056,128]{2,1,0:T(8,128)(2,1)S(1)}, f16[8,1056,128]{2,1,0:T(8,128)(2,1)S(1)}, u32[]{:S(2)}, u32[]{:S(2)}) %collective-permute-start.1) | collective-permute-done | bytes 2162720 | tf_op jit(solution)/shard_map/ppermute | solution.py:268
  78.5 0.4 convert_element_type.46
  78.9 0.1 fusion.11
  79.1 0.1 convert_reduce_fusion.1
  79.2 0.4 convert_reduce_fusion
  79.5 0.3 select_reduce_fusion.power_at_ref
  79.9 21.3 %memory.1 = bf16[8,272,512]{2,1,0:T(8,128)(2,1)S(1)} custom-call(s32[16]{0:T(128)S(1)} %get-tuple-element.17.count_ref, s32[16,16]{1,0:T(8,128)S(1)} %fusion.13.place_ref, s32[16,16]{1,0:T(8,128)S(1)} %select_reduce_fusion.power_at_ref, bf16[8448,128]{1,0:T(8,128)(2,1)S(1)} %bitcast.60, f32[256,128]{1,0:T(8,128)S(1)} %bitcast_convert_fusion.powers_ref, ...), custom_call_target="tpu_custom_call" | custom-call | flops 1073741824 | bytes 6291456 | tf_op jit(solution)/shard_map/memory/pallas_call | solution.py:290
  101.3 0.0 copy-start
  101.3 1.4 copy-done
  102.6 0.0 copy-start.1
  102.6 0.0 copy-start.2
  102.6 8.4 %all-to-all-start = ((bf16[8,272,512]{2,1,0:T(8,128)(2,1)}), bf16[8,272,512]{2,1,0:T(8,128)(2,1)S(1)}, u32[]{:S(2)}, u32[]{:S(2)}) async-start(bf16[8,272,512]{2,1,0:T(8,128)(2,1)} %copy-done), calls=%async_computation | async-start | bytes 4456448 | tf_op jit(solution)/shard_map/all_to_all | solution.py:311
  111.1 0.0 copy-done.1
  111.1 0.0 copy-start.3
  111.1 0.0 copy-done.2
  111.2 3.2 %collective-permute-start.2 = (bf16[768,128]{1,0:T(8,128)(2,1)S(1)}, bf16[768,128]{1,0:T(8,128)(2,1)S(1)}, u32[]{:S(2)}, u32[]{:S(2)}) collective-permute-start(bf16[768,128]{1,0:T(8,128)(2,1)S(1)} %pad_maximum_fusion.1), channel_id=1, source_target_pairs={{0,4},{4,0},{1,5},{5,1},{2,6},{6,2},{3,7},{7,3},{8,12},{12,8},{9,1... | collective-permute-start | bytes 589832 | tf_op jit(solution)/shard_map/ppermute | solution.py:318
  114.4 0.0 copy-done.3
  114.5 0.1 broadcast_select_fusion.4
  114.5 0.9 collective-permute-done.2
  115.5 2.4 %collective-permute-start.3 = (bf16[256,128]{1,0:T(8,128)(2,1)S(1)}, bf16[256,128]{1,0:T(8,128)(2,1)S(1)}, u32[]{:S(2)}, u32[]{:S(2)}) collective-permute-start(bf16[256,128]{1,0:T(8,128)(2,1)S(1)} %pad_maximum_fusion.4), channel_id=1, source_target_pairs={{0,8},{4,12},{8,16},{12,20},{16,24},{20,28},{24,32},{28,36},{32,40... | collective-permute-start | bytes 196616 | tf_op jit(solution)/shard_map/ppermute | solution.py:323
  118.0 18.2 %collective-permute-done.3 = bf16[256,128]{1,0:T(8,128)(2,1)S(1)} collective-permute-done((bf16[256,128]{1,0:T(8,128)(2,1)S(1)}, bf16[256,128]{1,0:T(8,128)(2,1)S(1)}, u32[]{:S(2)}, u32[]{:S(2)}) %collective-permute-start.3) | collective-permute-done | bytes 65568 | tf_op jit(solution)/shard_map/ppermute | solution.py:323
  136.2 0.8 window.1.window_ref
  137.1 5.4 %all-to-all-done.part_ref = bf16[8,272,512]{2,1,0:T(8,128)(2,1)S(1)} async-done(((bf16[8,272,512]{2,1,0:T(8,128)(2,1)}), bf16[8,272,512]{2,1,0:T(8,128)(2,1)S(1)}, u32[]{:S(2)}, u32[]{:S(2)}) %all-to-all-start) | async-done | bytes 2228256 | tf_op jit(solution)/shard_map/all_to_all | solution.py:311
  142.5 0.1 broadcast_in_dim.42
  142.6 0.6 merge.1
  143.2 13.3 %all_to_all.10 = bf16[8,32,512]{2,1,0:T(8,128)(2,1)S(1)} all-to-all(bf16[8,32,512]{2,1,0:T(8,128)(2,1)S(1)} %merge.1), channel_id=1, replica_groups=mesh['z'=8,'y'=8,'core'=2,'head'=4] {'head','core'}, dimensions={0} | all-to-all | bytes 524288 | tf_op jit(solution)/shard_map/all_to_all | solution.py:353
  156.5 0.7 copy.27
  (25 shorter events, 0.3 us)
Async XLA Ops:
  5.8 10.5 %collective-permute-start = (bf16[2592,128]{1,0:T(8,128)(2,1)S(1)}, bf16[2592,128]{1,0:T(8,128)(2,1)S(1)}, u32[]{:S(2)}, u32[]{:S(2)}) collective-permute-start(bf16[2592,128]{1,0:T(8,128)(2,1)S(1)} %get-tuple-element.12), channel_id=1, source_target_pairs={{0,4},{4,0},{1,5},{5,1},{2,6},{6,2},{3,7},{7,3},{8,12},{12,8},{9,1... | collective-permute-start | bytes 1990664 | tf_op jit(solution)/shard_map/ppermute | solution.py:261
  72.4 6.2 %collective-permute-start.1 = (f16[8,1056,128]{2,1,0:T(8,128)(2,1)S(1)}, f16[8,1056,128]{2,1,0:T(8,128)(2,1)S(1)}, u32[]{:S(2)}, u32[]{:S(2)}) collective-permute-start(f16[8,1056,128]{2,1,0:T(8,128)(2,1)S(1)} %slice.94), channel_id=1, source_target_pairs={{0,4},{4,0},{1,5},{5,1},{2,6},{6,2},{3,7},{7,3},{8,12},{12,8},{9,1... | collective-permute-start | bytes 6488072 | tf_op jit(solution)/shard_map/ppermute | solution.py:268
  101.3 1.4 copy-start
  102.6 8.4 %copy-start.1 = (bf16[128,2,128]{2,1,0:T(2,128)(2,1)S(1)}, bf16[128,2,128]{2,1,0:T(2,128)(2,1)}, u32[]{:S(2)}) copy-start(bf16[128,2,128]{2,1,0:T(2,128)(2,1)} %param.9) | copy-start | bytes 196612
  102.6 8.4 %copy-start.2 = (bf16[128,2,128]{2,1,0:T(2,128)(2,1)S(1)}, bf16[128,2,128]{2,1,0:T(2,128)(2,1)}, u32[]{:S(2)}) copy-start(bf16[128,2,128]{2,1,0:T(2,128)(2,1)} %param.8) | copy-start | bytes 196612
  102.6 39.8 %all-to-all-start = ((bf16[8,272,512]{2,1,0:T(8,128)(2,1)}), bf16[8,272,512]{2,1,0:T(8,128)(2,1)S(1)}, u32[]{:S(2)}, u32[]{:S(2)}) async-start(bf16[8,272,512]{2,1,0:T(8,128)(2,1)} %copy-done), calls=%async_computation | async-start | bytes 4456448 | tf_op jit(solution)/shard_map/all_to_all | solution.py:311
  111.1 3.4 %copy-start.3 = (f32[8]{0:T(128)S(1)}, f32[8]{0:T(128)}, u32[]{:S(2)}) copy-start(f32[8]{0:T(128)} %param.13) | copy-start | bytes 100
  111.2 4.3 %collective-permute-start.2 = (bf16[768,128]{1,0:T(8,128)(2,1)S(1)}, bf16[768,128]{1,0:T(8,128)(2,1)S(1)}, u32[]{:S(2)}, u32[]{:S(2)}) collective-permute-start(bf16[768,128]{1,0:T(8,128)(2,1)S(1)} %pad_maximum_fusion.1), channel_id=1, source_target_pairs={{0,4},{4,0},{1,5},{5,1},{2,6},{6,2},{3,7},{7,3},{8,12},{12,8},{9,1... | collective-permute-start | bytes 589832 | tf_op jit(solution)/shard_map/ppermute | solution.py:318
  115.5 20.7 %collective-permute-start.3 = (bf16[256,128]{1,0:T(8,128)(2,1)S(1)}, bf16[256,128]{1,0:T(8,128)(2,1)S(1)}, u32[]{:S(2)}, u32[]{:S(2)}) collective-permute-start(bf16[256,128]{1,0:T(8,128)(2,1)S(1)} %pad_maximum_fusion.4), channel_id=1, source_target_pairs={{0,8},{4,12},{8,16},{12,20},{16,24},{20,28},{24,32},{28,36},{32,40... | collective-permute-start | bytes 196616 | tf_op jit(solution)/shard_map/ppermute | solution.py:323

commit v5 on v4

--- a/solution.py
+++ b/solution.py
@@ -22,8 +22,9 @@
 CACHE = 2 * SHARE
 SHARD = CACHE + 2 * BLK_DEV + 2 * QROWS
 OROWS = 2 * HEAD + 16
-STEP = 4
+STEP = 8
 LOWEST = -3.0e38
+WAVES = ((4, 3, 5), (2, 6), (1, 7, 0))
 EXPO = HEAD**-0.5 * math.log2(math.e)
 SEQ = ("z", "y", "core")
 
@@ -36,6 +37,10 @@
 Z_LINES = [[[seq_index(z, y, core) for z in range(Z)] for y in range(Y)] for core in range(2)]
 KV_LINES = Y_LINES[0] + Z_LINES[1]
 Q_LINES = Z_LINES[0] + Y_LINES[1]
+
+
+def shift(value, lines, by):
+    return lax.ppermute(value, SEQ, [(line[i], line[(i + by) % LINE]) for line in lines for i in range(LINE)])
 
 
 def scaled(x):
@@ -53,9 +58,10 @@
 def pack_kernel(
     where_ref, k_ref, v_ref, q_ref, ids_ref, mine_ref, mine_powers_ref, mine_q_ref, other_ref, place_ref, powers
 ):
-    for i in range(3):
-        place_ref[i : i + 1, :] = jnp.full((1, 128), where_ref[i], jnp.int32)
     core = where_ref[2]
+    own = [where_ref[0], where_ref[1], core, jnp.where(core == 0, where_ref[0], where_ref[1])]
+    for i in range(4):
+        place_ref[i : i + 1, :] = jnp.full((1, 128), own[i], jnp.int32)
 
     def cache(head, out_ref):
         def one_block(b, carry):
@@ -110,110 +116,97 @@
         o_ref[rc] = out / total
 
 
-def memory_kernel(count_ref, place_ref, power_at_ref, q_ref, powers_ref, kv_ref, o_ref, buf, stage, q_buf, acc, top_s, sum_s, in_sems, out_sems):
-    buf[...] = jnp.zeros(buf.shape, buf.dtype)
-
-    def fetch(peer, rc, k):
-        at = pl.multiple_of(place_ref[peer * 2 + rc, k], 16)
-        return pltpu.make_async_copy(
-            kv_ref.at[pl.ds(at, PAIR)], buf.at[peer % 2, rc, k], in_sems.at[peer % 2, rc, k]
+def memory_kernel(deltas, count_ref, place_ref, power_at_ref, where_ref, q_ref, powers_ref, kv_ref, *rest):
+    o_refs = rest[: len(deltas)]
+    q_buf, acc, top_s, sum_s = rest[len(deltas) :]
+    eye = lax.broadcasted_iota(jnp.int32, (128, 128), 0) == lax.broadcasted_iota(jnp.int32, (128, 128), 1)
+    low = lax.broadcasted_iota(jnp.int32, (1, 128), 1) < BLOCK
+
+    def back(x, power_row):
+        scale = jnp.where(eye, jnp.exp2(-power_row), 0.0).astype(jnp.bfloat16)
+        return jnp.dot(scale, x, preferred_element_type=jnp.float32).astype(jnp.bfloat16)
+
+    def attend(index, rc, count, step):
+        keys, values = [], []
+        for i in range(0, STEP, 2):
+            places = [pl.multiple_of(place_ref[index, step * STEP + i + j], 16) for j in range(2)]
+            rows = [powers_ref[pl.ds(power_at_ref[index, step * STEP + i + j], 1), :] for j in range(2)]
+            turned = [pltpu.roll(row, BLOCK, 1) for row in rows]
+            both = jnp.concatenate([kv_ref[pl.ds(at, BLOCK), :] for at in places], axis=0)
+            keys.append(back(both, jnp.where(low, rows[0], turned[1])))
+            both = jnp.concatenate([kv_ref[pl.ds(at + BLOCK, BLOCK), :] for at in places], axis=0)
+            down = jnp.exp2(-jnp.where(low, turned[0], rows[1]))
+            values.append((both.T.astype(jnp.float32) * down).astype(jnp.bfloat16))
+        s = lax.dot_general(
+            jnp.concatenate(keys, axis=0), q_buf[rc], (((1,), (1,)), ((), ())), preferred_element_type=jnp.float32
         )
-
-    def fetch_all(peer):
+        s = jnp.concatenate(
+            [
+                jnp.where(step * STEP + i < count, s[i * BLOCK : (i + 1) * BLOCK], LOWEST)
+                for i in range(STEP)
+            ],
+            axis=0,
+        )
+        return s, jnp.max(s, axis=0, keepdims=True), jnp.concatenate(values, axis=1)
+
+    for o_ref, delta in zip(o_refs, deltas):
+        peer = lax.rem(where_ref[3, 0] + delta, LINE)
+        counts = [count_ref[peer * 2 + rc] for rc in range(2)]
         for rc in range(2):
-            def start(k, carry):
-                fetch(peer, rc, k).start()
-                return carry
-
-            lax.fori_loop(0, count_ref[peer * 2 + rc], start, 0)
-
-    def fetch_wait(peer):
-        for rc in range(2):
-            def wait(k, carry):
-                fetch(peer, rc, k).wait()
-                return carry
-
-            lax.fori_loop(0, count_ref[peer * 2 + rc], wait, 0)
-
-    def send(peer):
-        return pltpu.make_async_copy(stage.at[peer % 2], o_ref.at[peer], out_sems.at[peer % 2])
-
-    fetch_all(0)
-    for peer in range(LINE):
-        slot = peer % 2
-        if peer + 1 < LINE:
-            fetch_all(peer + 1)
-        counts = [count_ref[peer * 2 + rc] for rc in range(2)]
-        top_s[...] = jnp.full((2, 1, ROWS), LOWEST, jnp.float32)
-        sum_s[...] = jnp.zeros((2, 1, ROWS), jnp.float32)
-        acc[...] = jnp.zeros((2, HEAD, ROWS), jnp.float32)
-        for rc in range(2):
-            first = (peer * 2 + rc) * QROWS
-            extra = q_ref[first + ROWS : first + QROWS, :].astype(jnp.float32)
+            index = peer * 2 + rc
+            first = pl.multiple_of(index * QROWS, 16)
+            extra = q_ref[pl.ds(first + ROWS, 16), :].astype(jnp.float32)
             for i in range(ROWS // 128):
-                q_buf[rc, i * 128 : (i + 1) * 128, :] = restored(
-                    q_ref[first + i * 128 : first + (i + 1) * 128, :], extra[i : i + 1, :]
+                q_buf[rc, i * 128 : (i + 1) * 128, :] = back(
+                    q_ref[pl.ds(first + i * 128, 128), :], extra[i : i + 1, :]
                 )
-        fetch_wait(peer)
+            s, top, values = attend(index, rc, counts[rc], 0)
+            p = jnp.exp2((s - top) * EXPO)
+            top_s[rc] = top
+            sum_s[rc] = jnp.sum(p, axis=0, keepdims=True)
+            acc[rc] = jnp.dot(values, p.astype(jnp.bfloat16), preferred_element_type=jnp.float32)
 
         def one_step(step, carry):
             for rc in range(2):
-                pairs = []
-                for i in range(STEP):
-                    at = power_at_ref[peer * 2 + rc, step * STEP + i]
-                    pairs.append(restored(buf[slot, rc, step * STEP + i], powers_ref[pl.ds(at, 1), :]))
-                keys = jnp.concatenate([pair[:BLOCK] for pair in pairs], axis=0)
-                values = jnp.concatenate([pair[BLOCK:] for pair in pairs], axis=0)
-                s = lax.dot_general(
-                    keys, q_buf[rc], (((1,), (1,)), ((), ())), preferred_element_type=jnp.float32
-                )
-                rows = lax.broadcasted_iota(jnp.int32, s.shape, 0)
-                s = jnp.where(rows < (counts[rc] - step * STEP) * BLOCK, s, LOWEST)
-                top = jnp.maximum(top_s[rc], jnp.max(s, axis=0, keepdims=True))
-                live = (step * STEP < counts[rc]).astype(jnp.float32)
-                p = jnp.exp2((s - top) * EXPO) * live
+                s, top, values = attend(peer * 2 + rc, rc, counts[rc], step)
+                top = jnp.maximum(top_s[rc], top)
+                p = jnp.exp2((s - top) * EXPO)
                 alpha = jnp.exp2((top_s[rc] - top) * EXPO)
+                top_s[rc] = top
                 sum_s[rc] = sum_s[rc] * alpha + jnp.sum(p, axis=0, keepdims=True)
-                acc[rc] = acc[rc] * alpha + lax.dot_general(
-                    values, p.astype(jnp.bfloat16), (((0,), (0,)), ((), ())), preferred_element_type=jnp.float32
-                )
-                top_s[rc] = top
+                acc[rc] = acc[rc] * alpha + jnp.dot(values, p.astype(jnp.bfloat16), preferred_element_type=jnp.float32)
             return carry
 
-        lax.fori_loop(0, (jnp.maximum(counts[0], counts[1]) + STEP - 1) // STEP, one_step, 0)
-        if peer >= 2:
-            send(peer - 2).wait()
+        lax.fori_loop(1, (jnp.maximum(counts[0], counts[1]) + STEP - 1) // STEP, one_step, 0)
         rows = lax.broadcasted_iota(jnp.int32, (16, ROWS), 0)
         pieces = jnp.zeros((16, ROWS), jnp.float32)
         for rc in range(2):
-            total = sum_s[rc]
-            some = total > 0.0
-            safe = jnp.where(some, total, 1.0)
-            stage[slot, rc * HEAD : (rc + 1) * HEAD, :] = (acc[rc] / safe).astype(jnp.bfloat16)
-            level = jnp.where(some, top_s[rc] * EXPO + jnp.log2(safe), LOWEST)
+            some = counts[rc] > 0
+            total = jnp.where(some, sum_s[rc], 1.0)
+            o_ref[rc * HEAD : (rc + 1) * HEAD, :] = (acc[rc] * jnp.where(some, 1.0 / total, 0.0)).astype(jnp.bfloat16)
+            level = jnp.where(some, top_s[rc] * EXPO + jnp.log2(total), LOWEST)
             high = level.astype(jnp.bfloat16).astype(jnp.float32)
             mid = (level - high).astype(jnp.bfloat16).astype(jnp.float32)
             for i, piece in enumerate((high, mid, level - high - mid)):
                 pieces = jnp.where(rows == 3 * rc + i, piece, pieces)
-        stage[slot, 2 * HEAD :, :] = pieces.astype(jnp.bfloat16)
-        send(peer).start()
-    send(LINE - 2).wait()
-    send(LINE - 1).wait()
-
-
-def merge_kernel(part_ref, window_ref, gate_ref, o_ref):
+        o_ref[2 * HEAD :, :] = pieces.astype(jnp.bfloat16)
+
+
+def merge_kernel(*refs):
+    part_refs = refs[:LINE]
+    window_ref, gate_ref, o_ref = refs[LINE:]
     gate = gate_ref[...]
     for rc in range(2):
         levels = []
         for i in range(LINE):
-            pieces = part_ref[i, 2 * HEAD :, :].astype(jnp.float32)[3 * rc : 3 * rc + 3, :]
+            pieces = part_refs[i][2 * HEAD :, :].astype(jnp.float32)[3 * rc : 3 * rc + 3, :]
             levels.append(pieces[0:1] + pieces[1:2] + pieces[2:3])
         top = functools.reduce(jnp.maximum, levels)
         shares = [jnp.exp2(level - top) for level in levels]
         scale = gate / functools.reduce(jnp.add, shares)
         mixed = (1.0 - gate) * window_ref[rc]
         for i in range(LINE):
-            mixed = mixed + part_ref[i, rc * HEAD : (rc + 1) * HEAD, :].astype(jnp.float32) * (shares[i] * scale)
+            mixed = mixed + part_refs[i][rc * HEAD : (rc + 1) * HEAD, :].astype(jnp.float32) * (shares[i] * scale)
         for g in range(4):
             flat = mixed[:, g * 128 : (g + 1) * 128].T.astype(jnp.bfloat16)
             for x in range(X):
@@ -287,30 +280,29 @@
     places = (indices // (2 * BLK_DEV)) * SHARD + (indices % (2 * BLK_DEV)) * PAIR
     counts = jnp.sum(here.astype(jnp.int32), axis=1)
 
-    partial = pl.pallas_call(
-        memory_kernel,
-        out_shape=jax.ShapeDtypeStruct((LINE, OROWS, ROWS), jnp.bfloat16),
-        in_specs=[smem] * 3 + [vmem] * 2 + [pl.BlockSpec(memory_space=pltpu.HBM)],
-        out_specs=pl.BlockSpec(memory_space=pltpu.HBM),
-        scratch_shapes=[
-            pltpu.VMEM((2, 2, BLK_DEV, PAIR, HEAD), jnp.bfloat16),
-            pltpu.VMEM((2, OROWS, ROWS), jnp.bfloat16),
-            pltpu.VMEM((2, ROWS, HEAD), jnp.bfloat16),
-            pltpu.VMEM((2, HEAD, ROWS), jnp.float32),
-            pltpu.VMEM((2, 1, ROWS), jnp.float32),
-            pltpu.VMEM((2, 1, ROWS), jnp.float32),
-            pltpu.SemaphoreType.DMA((2, 2, BLK_DEV)),
-            pltpu.SemaphoreType.DMA((2,)),
-        ],
-        compiler_params=pltpu.CompilerParams(vmem_limit_bytes=24 << 20),
-        cost_estimate=pl.CostEstimate(
-            flops=4 * 64 * ROWS * BLOCK * HEAD, bytes_accessed=6 << 20, transcendentals=64 * ROWS * BLOCK
-        ),
-        name="memory",
-    )(counts, places, indices, lists, powers, cache)
-    returned = lax.all_to_all(
-        partial, SEQ, split_axis=0, concat_axis=0, axis_index_groups=Q_LINES, tiled=True
-    )
+    returned = {}
+    for deltas in WAVES:
+        partials = pl.pallas_call(
+            functools.partial(memory_kernel, deltas),
+            out_shape=[jax.ShapeDtypeStruct((OROWS, ROWS), jnp.bfloat16)] * len(deltas),
+            in_specs=[smem] * 4 + [vmem] * 3,
+            out_specs=[vmem] * len(deltas),
+            scratch_shapes=[
+                pltpu.VMEM((2, ROWS, HEAD), jnp.bfloat16),
+                pltpu.VMEM((2, HEAD, ROWS), jnp.float32),
+                pltpu.VMEM((2, 1, ROWS), jnp.float32),
+                pltpu.VMEM((2, 1, ROWS), jnp.float32),
+            ],
+            compiler_params=pltpu.CompilerParams(vmem_limit_bytes=24 << 20),
+            cost_estimate=pl.CostEstimate(
+                flops=len(deltas) * 16 * ROWS * BLOCK * HEAD * 8,
+                bytes_accessed=len(deltas) << 20,
+                transcendentals=len(deltas) * 16 * ROWS * BLOCK,
+            ),
+            name="memory",
+        )(counts, places, indices, placed, lists, powers, cache)
+        for delta, partial in zip(deltas, partials):
+            returned[delta] = shift(partial, Q_LINES, delta) if delta else partial
 
     q_mine, q_other = mine_and_other(by_head)
     k_mine, k_other = mine_and_other(keys.transpose(1, 0, 2))
@@ -344,12 +336,12 @@
     mixed = pl.pallas_call(
         merge_kernel,
         out_shape=jax.ShapeDtypeStruct((2 * X, 32, ROWS), jnp.bfloat16),
-        in_specs=[vmem] * 3,
+        in_specs=[vmem] * (LINE + 2),
         out_specs=vmem,
         compiler_params=pltpu.CompilerParams(vmem_limit_bytes=16 << 20),
         cost_estimate=pl.CostEstimate(flops=1 << 22, bytes_accessed=4 << 20, transcendentals=1 << 13),
         name="merge",
-    )(returned, window, gate)
+    )(*[returned[d] for d in range(LINE)], window, gate)
     rows = lax.all_to_all(mixed, ("head", "core"), split_axis=0, concat_axis=0, tiled=True)
     return rows.transpose(1, 0, 2).reshape(32, 2 * X * ROWS)
 

time: 158 us -> 167 us (1.057)
  starting transfers between devices: 25.1 us -> 45.3 us
  waiting for transfers between devices: 28.7 us -> 18 us
  Pallas kernels: 25.4 us -> 19.7 us
  other arithmetic: 4.06 us -> 8.63 us
    ppermute x0 -> x7, starting transfers between devices: none -> 28.7 us  [shift(): lax.ppermute(value, SEQ, [(line[i], line[(i + by) % LINE]) for line in li...]
    ppermute x1, waiting for transfers between devices: 18.2 us -> 0.01 us  [on_device(): lax.ppermute(jnp.concatenate([k_second, v_second], axis=0), SEQ, onward)]
    ppermute x0 -> x7, waiting for transfers between devices: none -> 14.8 us  [shift(): lax.ppermute(value, SEQ, [(line[i], line[(i + by) % LINE]) for line in li...]
    all_to_all x1 -> x0, starting transfers between devices: 8.41 us -> none  [on_device(): lax.all_to_all(partial, SEQ, split_axis=0, concat_axis=0, axis_index_grou...]
    pallas_call x1 -> x3, Pallas kernels: 21.3 us -> 15.6 us  [on_device(): pl.pallas_call(functools.partial(memory_kernel, deltas), out_shape=[jax.S...]
    all_to_all x1 -> x0, waiting for transfers between devices: 5.41 us -> none  [on_device(): lax.all_to_all(partial, SEQ, split_axis=0, concat_axis=0, axis_index_grou...]
    convert_element_type x1, other arithmetic: 1.25 us -> 5.8 us  [on_device(): cache = gathered.astype(jnp.bfloat16)]
    ppermute x1, waiting for transfers between devices: 2.52 us -> 0.01 us  [on_device(): lists = lax.ppermute(parts[:, SHARD - 2 * QROWS:], 'core', swap)]
  transfers between devices with their start and end apart: 5 -> 11, of which waited for: 5 -> 6; matrix products, arithmetic and copies ran while one was open for 1% -> 5% of each run, Pallas kernels for 1% -> 10%
where the time goes in v5:
time: 167 us; the launch traced here: 166 us
  blocking collectives  67.4 us (40%)
  starting transfers between devices  45.3 us (27%)
  Pallas kernels  19.7 us (12%)
  waiting for transfers between devices  18 us (11%)
  other arithmetic  8.63 us (5%)
  local copies, waits for them, and re-layouts  6.31 us (4%)
    all_gather x1, blocking collectives, on_device(): lax.all_gather(shard, SEQ, axis_index_groups=KV_LINES, tiled=True)  55.2 us
    ppermute x7, starting transfers between devices, shift(): lax.ppermute(value, SEQ, [(line[i], line[(i + by) % LINE]) for line in li...  28.7 us
    pallas_call x3, Pallas kernels, on_device(): pl.pallas_call(functools.partial(memory_kernel, deltas), out_shape=[jax.S...  15.6 us
    ppermute x7, waiting for transfers between devices, shift(): lax.ppermute(value, SEQ, [(line[i], line[(i + by) % LINE]) for line in li...  14.8 us
    all_to_all x1, blocking collectives, on_device(): lax.all_to_all(mixed, ('head', 'core'), split_axis=0, concat_axis=0, tile...  12.2 us
    ppermute x1, starting transfers between devices, on_device(): theirs = lax.ppermute(other, 'core', swap)  8.79 us
    convert_element_type x1, other arithmetic, on_device(): cache = gathered.astype(jnp.bfloat16)  5.8 us
  transfers between devices with their start and end apart: 11, of which 6 were waited for; matrix products, arithmetic and copies ran while one was open for 5% of the time, Pallas kernels for 10%

profile of v5, /device:TPU:1, one launch (start us, length us, event | category | flops | bytes accessed | tf_op | source)
XLA Modules:
  0.0 165.7 jit_solution(11312911133158526071)
XLA Ops:
  0.0 1.0 copy.39
  1.0 0.7 fusion.25
  1.7 1.3 copy_bitcast_fusion
  3.0 0.1 fusion.6.ids_ref
  3.1 0.1 pad_add_fusion.where_ref
  3.2 2.6 %pack.1 = (bf16[2048,128]{1,0:T(8,128)(2,1)S(1)}, bf16[16,128]{1,0:T(8,128)(2,1)S(1)}, bf16[528,128]{1,0:T(8,128)(2,1)S(1)}, bf16[2592,128]{1,0:T(8,128)(2,1)S(1)}, s32[8,128]{1,0:T(8,128)S(1)}) custom-call(s32[3]{0:T(128)S(1)} %pad_add_fusion.where_ref, bf16[2,1024,128]{2,1,0:T(8,128)(2,1)S(1)} %get-tuple-element.57.k_ref, ...), custom_call_target="tpu_custom_call" | custom-call | flops 4194304 | bytes 3145728 | tf_op jit(solution)/shard_map/pack/pallas_call | solution.py:232
  5.8 8.8 %collective-permute-start = (bf16[2592,128]{1,0:T(8,128)(2,1)S(1)}, bf16[2592,128]{1,0:T(8,128)(2,1)S(1)}, u32[]{:S(2)}, u32[]{:S(2)}) collective-permute-start(bf16[2592,128]{1,0:T(8,128)(2,1)S(1)} %get-tuple-element.20), channel_id=1, source_target_pairs={{0,4},{4,0},{1,5},{5,1},{2,6},{6,2},{3,7},{7,3},{8,12},{12,8},{9,1... | collective-permute-start | bytes 1990664 | tf_op jit(solution)/shard_map/ppermute | solution.py:254
  14.6 1.7 %collective-permute-done = bf16[2592,128]{1,0:T(8,128)(2,1)S(1)} collective-permute-done((bf16[2592,128]{1,0:T(8,128)(2,1)S(1)}, bf16[2592,128]{1,0:T(8,128)(2,1)S(1)}, u32[]{:S(2)}, u32[]{:S(2)}) %collective-permute-start) | collective-permute-done | bytes 663584 | tf_op jit(solution)/shard_map/ppermute | solution.py:254
  16.3 0.1 slice_dynamic-update-slice_fusion
  16.4 0.1 select_dynamic-update-slice_fusion.1
  16.5 0.1 select_dynamic-update-slice_fusion
  16.5 0.3 convert_element_type.45
  16.8 55.2 %all-gather.1 = f16[41472,128]{1,0:T(8,128)(2,1)S(1)} all-gather(f16[5184,128]{1,0:T(8,128)(2,1)S(1)} %convert_element_type.45), channel_id=1, replica_groups={{0,8,16,24,32,40,48,56},{64,72,80,88,96,104,112,120},{128,136,144,152,1..., dimensions={0}, use_global_device_ids=true | all-gather | bytes 11943936 | tf_op jit(solution)/shard_map/all_gather | solution.py:259
  72.0 0.0 copy-start
  72.0 0.0 copy-start.1
  72.0 0.0 copy-start.2
  72.0 2.1 %slice.94 = f16[8,1056,128]{2,1,0:T(8,128)(2,1)} slice(f16[8,5184,128]{2,1,0:T(8,128)(2,1)S(1)} %bitcast.66), slice={[0:8], [4128:5184], [0:128]} | slice | bytes 4325376 | tf_op jit(solution)/shard_map/slice | solution.py:261
  74.1 0.0 copy-start.3
  74.1 2.4 %collective-permute-start.1 = (f16[8,1056,128]{2,1,0:T(8,128)(2,1)}, f16[8,1056,128]{2,1,0:T(8,128)(2,1)S(1)}, u32[]{:S(2)}, u32[]{:S(2)}) collective-permute-start(f16[8,1056,128]{2,1,0:T(8,128)(2,1)} %slice.94), channel_id=1, source_target_pairs={{0,4},{4,0},{1,5},{5,1},{2,6},{6,2},{3,7},{7,3},{8,12},{12,8},{9,1... | collective-permute-start | bytes 6488072 | tf_op jit(solution)/shard_map/ppermute | solution.py:261
  76.5 0.0 copy-done.1
  76.5 0.0 copy-done.2
  76.6 0.0 copy-done
  76.7 2.3 %collective-permute-start.9 = (bf16[768,128]{1,0:T(8,128)(2,1)S(1)}, bf16[768,128]{1,0:T(8,128)(2,1)S(1)}, u32[]{:S(2)}, u32[]{:S(2)}) collective-permute-start(bf16[768,128]{1,0:T(8,128)(2,1)S(1)} %pad_maximum_fusion.1), channel_id=1, source_target_pairs={{0,4},{4,0},{1,5},{5,1},{2,6},{6,2},{3,7},{7,3},{8,12},{12,8},{9,1... | collective-permute-start | bytes 589832 | tf_op jit(solution)/shard_map/ppermute | solution.py:310
  79.0 0.0 copy-done.3
  79.1 0.1 broadcast_select_fusion.4
  79.1 1.5 collective-permute-done.9
  80.7 3.0 %collective-permute-start.10 = (bf16[256,128]{1,0:T(8,128)(2,1)S(1)}, bf16[256,128]{1,0:T(8,128)(2,1)S(1)}, u32[]{:S(2)}, u32[]{:S(2)}) collective-permute-start(bf16[256,128]{1,0:T(8,128)(2,1)S(1)} %pad_maximum_fusion.4), channel_id=1, source_target_pairs={{0,8},{4,12},{8,16},{12,20},{16,24},{20,28},{24,32},{28,36},{32,40... | collective-permute-start | bytes 196616 | tf_op jit(solution)/shard_map/ppermute | solution.py:315
  83.7 0.9 slice.98
  84.6 5.8 %convert_element_type.56.kv_ref = bf16[41472,128]{1,0:T(8,128)(2,1)S(1)} convert(f16[41472,128]{1,0:T(8,128)(2,1)} %copy-done) | non-fusion elementwise | flops 5308416 | bytes 21233664 | tf_op jit(solution)/shard_map/convert_element_type | solution.py:263
  90.4 0.0 collective-permute-done.1
  90.4 0.4 convert_element_type.46
  90.8 0.1 fusion.11
  90.9 0.1 convert_reduce_fusion.1
  91.1 0.4 convert_reduce_fusion
  91.4 0.3 select_reduce_fusion.power_at_ref
  91.8 5.8 %memory.3 = (bf16[272,512]{1,0:T(8,128)(2,1)S(1)}, bf16[272,512]{1,0:T(8,128)(2,1)S(1)}, bf16[272,512]{1,0:T(8,128)(2,1)S(1)}) custom-call(s32[16]{0:T(128)S(1)} %get-tuple-element.33.count_ref, s32[16,16]{1,0:T(8,128)S(1)} %fusion.13.place_ref, s32[16,16]{1,0:T(8,128)S(1)} %select_reduce_fusion.power_at_ref, s32[8,128]{1,0:T(8,128)S(1)} %get-tuple-element.18.where_ref, ...), custom_call_target="tpu_custom_call" | custom-call | flops 1610612736 | bytes 3145728 | tf_op jit(solution)/shard_map/memory/pallas_call | solution.py:285
  97.7 4.1 %memory.4 = (bf16[272,512]{1,0:T(8,128)(2,1)S(1)}, bf16[272,512]{1,0:T(8,128)(2,1)S(1)}) custom-call(s32[16]{0:T(128)S(1)} %get-tuple-element.33.count_ref, s32[16,16]{1,0:T(8,128)S(1)} %fusion.13.place_ref, s32[16,16]{1,0:T(8,128)S(1)} %select_reduce_fusion.power_at_ref, s32[8,128]{1,0:T(8,128)S(1)} %get-tuple-element.18.where_ref, ...), custom_call_target="tpu_custom_call" | custom-call | flops 1073741824 | bytes 2097152 | tf_op jit(solution)/shard_map/memory/pallas_call | solution.py:285
  101.8 3.2 %collective-permute-start.2 = (bf16[272,512]{1,0:T(8,128)(2,1)S(1)}, bf16[272,512]{1,0:T(8,128)(2,1)S(1)}, u32[]{:S(2)}, u32[]{:S(2)}) collective-permute-start(bf16[272,512]{1,0:T(8,128)(2,1)S(1)} %get-tuple-element.24), channel_id=1, source_target_pairs={{0,64},{64,128},{128,192},{192,256},{256,320},{320,384},{384,448},... | collective-permute-start | bytes 835592 | tf_op jit(solution)/shard_map/ppermute | solution.py:43
  105.0 7.0 %collective-permute-start.3 = (bf16[272,512]{1,0:T(8,128)(2,1)S(1)}, bf16[272,512]{1,0:T(8,128)(2,1)S(1)}, u32[]{:S(2)}, u32[]{:S(2)}) collective-permute-start(bf16[272,512]{1,0:T(8,128)(2,1)S(1)} %get-tuple-element.25), channel_id=1, source_target_pairs={{0,128},{64,192},{128,256},{192,320},{256,384},{320,448},{384,0},{... | collective-permute-start | bytes 835592 | tf_op jit(solution)/shard_map/ppermute | solution.py:43
  112.1 5.7 %memory.5 = (bf16[272,512]{1,0:T(8,128)(2,1)S(1)}, bf16[272,512]{1,0:T(8,128)(2,1)S(1)}, bf16[272,512]{1,0:T(8,128)(2,1)S(1)}) custom-call(s32[16]{0:T(128)S(1)} %get-tuple-element.33.count_ref, s32[16,16]{1,0:T(8,128)S(1)} %fusion.13.place_ref, s32[16,16]{1,0:T(8,128)S(1)} %select_reduce_fusion.power_at_ref, s32[8,128]{1,0:T(8,128)S(1)} %get-tuple-element.18.where_ref, ...), custom_call_target="tpu_custom_call" | custom-call | flops 1610612736 | bytes 3145728 | tf_op jit(solution)/shard_map/memory/pallas_call | solution.py:285
  117.8 3.3 %collective-permute-start.4 = (bf16[272,512]{1,0:T(8,128)(2,1)S(1)}, bf16[272,512]{1,0:T(8,128)(2,1)S(1)}, u32[]{:S(2)}, u32[]{:S(2)}) collective-permute-start(bf16[272,512]{1,0:T(8,128)(2,1)S(1)} %get-tuple-element.26), channel_id=1, source_target_pairs={{0,192},{64,256},{128,320},{192,384},{256,448},{320,0},{384,64},{4... | collective-permute-start | bytes 835592 | tf_op jit(solution)/shard_map/ppermute | solution.py:43
  121.0 2.1 %collective-permute-start.5 = (bf16[272,512]{1,0:T(8,128)(2,1)S(1)}, bf16[272,512]{1,0:T(8,128)(2,1)S(1)}, u32[]{:S(2)}, u32[]{:S(2)}) collective-permute-start(bf16[272,512]{1,0:T(8,128)(2,1)S(1)} %get-tuple-element.27), channel_id=1, source_target_pairs={{0,256},{64,320},{128,384},{192,448},{256,0},{320,64},{384,128},{4... | collective-permute-start | bytes 835592 | tf_op jit(solution)/shard_map/ppermute | solution.py:43
  123.2 0.0 collective-permute-done.10
  123.2 4.8 %collective-permute-start.6 = (bf16[272,512]{1,0:T(8,128)(2,1)S(1)}, bf16[272,512]{1,0:T(8,128)(2,1)S(1)}, u32[]{:S(2)}, u32[]{:S(2)}) collective-permute-start(bf16[272,512]{1,0:T(8,128)(2,1)S(1)} %get-tuple-element.28), channel_id=1, source_target_pairs={{0,320},{64,384},{128,448},{192,0},{256,64},{320,128},{384,192},{4... | collective-permute-start | bytes 835592 | tf_op jit(solution)/shard_map/ppermute | solution.py:43
  128.0 0.0 collective-permute-done.2.refs_1_
  128.0 5.2 %collective-permute-start.7 = (bf16[272,512]{1,0:T(8,128)(2,1)S(1)}, bf16[272,512]{1,0:T(8,128)(2,1)S(1)}, u32[]{:S(2)}, u32[]{:S(2)}) collective-permute-start(bf16[272,512]{1,0:T(8,128)(2,1)S(1)} %get-tuple-element.29), channel_id=1, source_target_pairs={{0,384},{64,448},{128,0},{192,64},{256,128},{320,192},{384,256},{4... | collective-permute-start | bytes 835592 | tf_op jit(solution)/shard_map/ppermute | solution.py:43
  133.2 0.0 collective-permute-done.3.refs_2_
  133.2 3.1 %collective-permute-start.8 = (bf16[272,512]{1,0:T(8,128)(2,1)S(1)}, bf16[272,512]{1,0:T(8,128)(2,1)S(1)}, u32[]{:S(2)}, u32[]{:S(2)}) collective-permute-start(bf16[272,512]{1,0:T(8,128)(2,1)S(1)} %get-tuple-element.30), channel_id=1, source_target_pairs={{0,448},{64,0},{128,64},{192,128},{256,192},{320,256},{384,320},{4... | collective-permute-start | bytes 835592 | tf_op jit(solution)/shard_map/ppermute | solution.py:43
  136.4 0.8 window.1.refs_8_
  137.2 0.0 collective-permute-done.4.refs_3_
  137.3 1.0 collective-permute-done.5.refs_4_
  138.2 4.2 %collective-permute-done.6.refs_5_ = bf16[272,512]{1,0:T(8,128)(2,1)S(1)} collective-permute-done((bf16[272,512]{1,0:T(8,128)(2,1)S(1)}, bf16[272,512]{1,0:T(8,128)(2,1)S(1)}, u32[]{:S(2)}, u32[]{:S(2)}) %collective-permute-start.6) | collective-permute-done | bytes 278560 | tf_op jit(solution)/shard_map/ppermute | solution.py:43
  142.4 6.8 %collective-permute-done.7.refs_6_ = bf16[272,512]{1,0:T(8,128)(2,1)S(1)} collective-permute-done((bf16[272,512]{1,0:T(8,128)(2,1)S(1)}, bf16[272,512]{1,0:T(8,128)(2,1)S(1)}, u32[]{:S(2)}, u32[]{:S(2)}) %collective-permute-start.7) | collective-permute-done | bytes 278560 | tf_op jit(solution)/shard_map/ppermute | solution.py:43
  149.2 2.8 %collective-permute-done.8.refs_7_ = bf16[272,512]{1,0:T(8,128)(2,1)S(1)} collective-permute-done((bf16[272,512]{1,0:T(8,128)(2,1)S(1)}, bf16[272,512]{1,0:T(8,128)(2,1)S(1)}, u32[]{:S(2)}, u32[]{:S(2)}) %collective-permute-start.8) | collective-permute-done | bytes 278560 | tf_op jit(solution)/shard_map/ppermute | solution.py:43
  152.1 0.1 broadcast_in_dim.42
  152.1 0.7 merge.1
  152.8 12.2 %all_to_all.5 = bf16[8,32,512]{2,1,0:T(8,128)(2,1)S(1)} all-to-all(bf16[8,32,512]{2,1,0:T(8,128)(2,1)S(1)} %merge.1), channel_id=1, replica_groups=mesh['z'=8,'y'=8,'core'=2,'head'=4] {'head','core'}, dimensions={0} | all-to-all | bytes 524288 | tf_op jit(solution)/shard_map/all_to_all | solution.py:345
  165.0 0.7 copy.27
  (24 shorter events, 0.3 us)
Async XLA Ops:
  5.8 10.5 %collective-permute-start = (bf16[2592,128]{1,0:T(8,128)(2,1)S(1)}, bf16[2592,128]{1,0:T(8,128)(2,1)S(1)}, u32[]{:S(2)}, u32[]{:S(2)}) collective-permute-start(bf16[2592,128]{1,0:T(8,128)(2,1)S(1)} %get-tuple-element.20), channel_id=1, source_target_pairs={{0,4},{4,0},{1,5},{5,1},{2,6},{6,2},{3,7},{7,3},{8,12},{12,8},{9,1... | collective-permute-start | bytes 1990664 | tf_op jit(solution)/shard_map/ppermute | solution.py:254
  72.0 4.7 %copy-start = (f16[41472,128]{1,0:T(8,128)(2,1)}, f16[41472,128]{1,0:T(8,128)(2,1)S(1)}, u32[]{:S(2)}) copy-start(f16[41472,128]{1,0:T(8,128)(2,1)S(1)} %all-gather.1) | copy-start | bytes 31850500
  72.0 4.6 %copy-start.1 = (bf16[128,2,128]{2,1,0:T(2,128)(2,1)S(1)}, bf16[128,2,128]{2,1,0:T(2,128)(2,1)}, u32[]{:S(2)}) copy-start(bf16[128,2,128]{2,1,0:T(2,128)(2,1)} %param.9) | copy-start | bytes 196612
  72.0 4.6 %copy-start.2 = (bf16[128,2,128]{2,1,0:T(2,128)(2,1)S(1)}, bf16[128,2,128]{2,1,0:T(2,128)(2,1)}, u32[]{:S(2)}) copy-start(bf16[128,2,128]{2,1,0:T(2,128)(2,1)} %param.8) | copy-start | bytes 196612
  74.1 4.9 %copy-start.3 = (f32[8]{0:T(128)S(1)}, f32[8]{0:T(128)}, u32[]{:S(2)}) copy-start(f32[8]{0:T(128)} %param.13) | copy-start | bytes 100
  74.1 16.3 %collective-permute-start.1 = (f16[8,1056,128]{2,1,0:T(8,128)(2,1)}, f16[8,1056,128]{2,1,0:T(8,128)(2,1)S(1)}, u32[]{:S(2)}, u32[]{:S(2)}) collective-permute-start(f16[8,1056,128]{2,1,0:T(8,128)(2,1)} %slice.94), channel_id=1, source_target_pairs={{0,4},{4,0},{1,5},{5,1},{2,6},{6,2},{3,7},{7,3},{8,12},{12,8},{9,1... | collective-permute-start | bytes 6488072 | tf_op jit(solution)/shard_map/ppermute | solution.py:261
  76.7 4.0 %collective-permute-start.9 = (bf16[768,128]{1,0:T(8,128)(2,1)S(1)}, bf16[768,128]{1,0:T(8,128)(2,1)S(1)}, u32[]{:S(2)}, u32[]{:S(2)}) collective-permute-start(bf16[768,128]{1,0:T(8,128)(2,1)S(1)} %pad_maximum_fusion.1), channel_id=1, source_target_pairs={{0,4},{4,0},{1,5},{5,1},{2,6},{6,2},{3,7},{7,3},{8,12},{12,8},{9,1... | collective-permute-start | bytes 589832 | tf_op jit(solution)/shard_map/ppermute | solution.py:310
  80.7 42.5 %collective-permute-start.10 = (bf16[256,128]{1,0:T(8,128)(2,1)S(1)}, bf16[256,128]{1,0:T(8,128)(2,1)S(1)}, u32[]{:S(2)}, u32[]{:S(2)}) collective-permute-start(bf16[256,128]{1,0:T(8,128)(2,1)S(1)} %pad_maximum_fusion.4), channel_id=1, source_target_pairs={{0,8},{4,12},{8,16},{12,20},{16,24},{20,28},{24,32},{28,36},{32,40... | collective-permute-start | bytes 196616 | tf_op jit(solution)/shard_map/ppermute | solution.py:315
  101.8 26.2 %collective-permute-start.2 = (bf16[272,512]{1,0:T(8,128)(2,1)S(1)}, bf16[272,512]{1,0:T(8,128)(2,1)S(1)}, u32[]{:S(2)}, u32[]{:S(2)}) collective-permute-start(bf16[272,512]{1,0:T(8,128)(2,1)S(1)} %get-tuple-element.24), channel_id=1, source_target_pairs={{0,64},{64,128},{128,192},{192,256},{256,320},{320,384},{384,448},... | collective-permute-start | bytes 835592 | tf_op jit(solution)/shard_map/ppermute | solution.py:43
  105.0 28.3 %collective-permute-start.3 = (bf16[272,512]{1,0:T(8,128)(2,1)S(1)}, bf16[272,512]{1,0:T(8,128)(2,1)S(1)}, u32[]{:S(2)}, u32[]{:S(2)}) collective-permute-start(bf16[272,512]{1,0:T(8,128)(2,1)S(1)} %get-tuple-element.25), channel_id=1, source_target_pairs={{0,128},{64,192},{128,256},{192,320},{256,384},{320,448},{384,0},{... | collective-permute-start | bytes 835592 | tf_op jit(solution)/shard_map/ppermute | solution.py:43
  117.8 19.5 %collective-permute-start.4 = (bf16[272,512]{1,0:T(8,128)(2,1)S(1)}, bf16[272,512]{1,0:T(8,128)(2,1)S(1)}, u32[]{:S(2)}, u32[]{:S(2)}) collective-permute-start(bf16[272,512]{1,0:T(8,128)(2,1)S(1)} %get-tuple-element.26), channel_id=1, source_target_pairs={{0,192},{64,256},{128,320},{192,384},{256,448},{320,0},{384,64},{4... | collective-permute-start | bytes 835592 | tf_op jit(solution)/shard_map/ppermute | solution.py:43
  121.0 17.2 %collective-permute-start.5 = (bf16[272,512]{1,0:T(8,128)(2,1)S(1)}, bf16[272,512]{1,0:T(8,128)(2,1)S(1)}, u32[]{:S(2)}, u32[]{:S(2)}) collective-permute-start(bf16[272,512]{1,0:T(8,128)(2,1)S(1)} %get-tuple-element.27), channel_id=1, source_target_pairs={{0,256},{64,320},{128,384},{192,448},{256,0},{320,64},{384,128},{4... | collective-permute-start | bytes 835592 | tf_op jit(solution)/shard_map/ppermute | solution.py:43
  123.2 19.2 %collective-permute-start.6 = (bf16[272,512]{1,0:T(8,128)(2,1)S(1)}, bf16[272,512]{1,0:T(8,128)(2,1)S(1)}, u32[]{:S(2)}, u32[]{:S(2)}) collective-permute-start(bf16[272,512]{1,0:T(8,128)(2,1)S(1)} %get-tuple-element.28), channel_id=1, source_target_pairs={{0,320},{64,384},{128,448},{192,0},{256,64},{320,128},{384,192},{4... | collective-permute-start | bytes 835592 | tf_op jit(solution)/shard_map/ppermute | solution.py:43
  128.0 21.2 %collective-permute-start.7 = (bf16[272,512]{1,0:T(8,128)(2,1)S(1)}, bf16[272,512]{1,0:T(8,128)(2,1)S(1)}, u32[]{:S(2)}, u32[]{:S(2)}) collective-permute-start(bf16[272,512]{1,0:T(8,128)(2,1)S(1)} %get-tuple-element.29), channel_id=1, source_target_pairs={{0,384},{64,448},{128,0},{192,64},{256,128},{320,192},{384,256},{4... | collective-permute-start | bytes 835592 | tf_op jit(solution)/shard_map/ppermute | solution.py:43
  133.2 18.8 %collective-permute-start.8 = (bf16[272,512]{1,0:T(8,128)(2,1)S(1)}, bf16[272,512]{1,0:T(8,128)(2,1)S(1)}, u32[]{:S(2)}, u32[]{:S(2)}) collective-permute-start(bf16[272,512]{1,0:T(8,128)(2,1)S(1)} %get-tuple-element.30), channel_id=1, source_target_pairs={{0,448},{64,0},{128,64},{192,128},{256,192},{320,256},{384,320},{4... | collective-permute-start | bytes 835592 | tf_op jit(solution)/shard_map/ppermute | solution.py:43

commit v6 on v5

--- a/solution.py
+++ b/solution.py
@@ -24,7 +24,6 @@
 OROWS = 2 * HEAD + 16
 STEP = 8
 LOWEST = -3.0e38
-WAVES = ((4, 3, 5), (2, 6), (1, 7, 0))
 EXPO = HEAD**-0.5 * math.log2(math.e)
 SEQ = ("z", "y", "core")
 
@@ -37,10 +36,6 @@
 Z_LINES = [[[seq_index(z, y, core) for z in range(Z)] for y in range(Y)] for core in range(2)]
 KV_LINES = Y_LINES[0] + Z_LINES[1]
 Q_LINES = Z_LINES[0] + Y_LINES[1]
-
-
-def shift(value, lines, by):
-    return lax.ppermute(value, SEQ, [(line[i], line[(i + by) % LINE]) for line in lines for i in range(LINE)])
 
 
 def scaled(x):
@@ -58,10 +53,9 @@
 def pack_kernel(
     where_ref, k_ref, v_ref, q_ref, ids_ref, mine_ref, mine_powers_ref, mine_q_ref, other_ref, place_ref, powers
 ):
+    for i in range(3):
+        place_ref[i : i + 1, :] = jnp.full((1, 128), where_ref[i], jnp.int32)
     core = where_ref[2]
-    own = [where_ref[0], where_ref[1], core, jnp.where(core == 0, where_ref[0], where_ref[1])]
-    for i in range(4):
-        place_ref[i : i + 1, :] = jnp.full((1, 128), own[i], jnp.int32)
 
     def cache(head, out_ref):
         def one_block(b, carry):
@@ -116,15 +110,16 @@
         o_ref[rc] = out / total
 
 
-def memory_kernel(deltas, count_ref, place_ref, power_at_ref, where_ref, q_ref, powers_ref, kv_ref, *rest):
-    o_refs = rest[: len(deltas)]
-    q_buf, acc, top_s, sum_s = rest[len(deltas) :]
+def memory_kernel(count_ref, place_ref, power_at_ref, q_ref, powers_ref, kv_ref, o_ref, stage, q_buf, acc, top_s, sum_s, out_sems):
     eye = lax.broadcasted_iota(jnp.int32, (128, 128), 0) == lax.broadcasted_iota(jnp.int32, (128, 128), 1)
     low = lax.broadcasted_iota(jnp.int32, (1, 128), 1) < BLOCK
 
     def back(x, power_row):
         scale = jnp.where(eye, jnp.exp2(-power_row), 0.0).astype(jnp.bfloat16)
         return jnp.dot(scale, x, preferred_element_type=jnp.float32).astype(jnp.bfloat16)
+
+    def send(peer):
+        return pltpu.make_async_copy(stage.at[peer % 2], o_ref.at[peer], out_sems.at[peer % 2])
 
     def attend(index, rc, count, step):
         keys, values = [], []
@@ -147,18 +142,19 @@
             ],
             axis=0,
         )
-        return s, jnp.max(s, axis=0, keepdims=True), jnp.concatenate(values, axis=1)
-
-    for o_ref, delta in zip(o_refs, deltas):
-        peer = lax.rem(where_ref[3, 0] + delta, LINE)
+        top = jnp.max(s, axis=0, keepdims=True)
+        return s, top, jnp.concatenate(values, axis=1)
+
+    for peer in range(LINE):
+        slot = peer % 2
         counts = [count_ref[peer * 2 + rc] for rc in range(2)]
         for rc in range(2):
             index = peer * 2 + rc
-            first = pl.multiple_of(index * QROWS, 16)
-            extra = q_ref[pl.ds(first + ROWS, 16), :].astype(jnp.float32)
+            first = index * QROWS
+            extra = q_ref[first + ROWS : first + QROWS, :].astype(jnp.float32)
             for i in range(ROWS // 128):
                 q_buf[rc, i * 128 : (i + 1) * 128, :] = back(
-                    q_ref[pl.ds(first + i * 128, 128), :], extra[i : i + 1, :]
+                    q_ref[first + i * 128 : first + (i + 1) * 128, :], extra[i : i + 1, :]
                 )
             s, top, values = attend(index, rc, counts[rc], 0)
             p = jnp.exp2((s - top) * EXPO)
@@ -178,35 +174,38 @@
             return carry
 
         lax.fori_loop(1, (jnp.maximum(counts[0], counts[1]) + STEP - 1) // STEP, one_step, 0)
+        if peer >= 2:
+            send(peer - 2).wait()
         rows = lax.broadcasted_iota(jnp.int32, (16, ROWS), 0)
         pieces = jnp.zeros((16, ROWS), jnp.float32)
         for rc in range(2):
             some = counts[rc] > 0
             total = jnp.where(some, sum_s[rc], 1.0)
-            o_ref[rc * HEAD : (rc + 1) * HEAD, :] = (acc[rc] * jnp.where(some, 1.0 / total, 0.0)).astype(jnp.bfloat16)
+            stage[slot, rc * HEAD : (rc + 1) * HEAD, :] = (acc[rc] * jnp.where(some, 1.0 / total, 0.0)).astype(jnp.bfloat16)
             level = jnp.where(some, top_s[rc] * EXPO + jnp.log2(total), LOWEST)
             high = level.astype(jnp.bfloat16).astype(jnp.float32)
             mid = (level - high).astype(jnp.bfloat16).astype(jnp.float32)
             for i, piece in enumerate((high, mid, level - high - mid)):
                 pieces = jnp.where(rows == 3 * rc + i, piece, pieces)
-        o_ref[2 * HEAD :, :] = pieces.astype(jnp.bfloat16)
-
-
-def merge_kernel(*refs):
-    part_refs = refs[:LINE]
-    window_ref, gate_ref, o_ref = refs[LINE:]
+        stage[slot, 2 * HEAD :, :] = pieces.astype(jnp.bfloat16)
+        send(peer).start()
+    send(LINE - 2).wait()
+    send(LINE - 1).wait()
+
+
+def merge_kernel(part_ref, window_ref, gate_ref, o_ref):
     gate = gate_ref[...]
     for rc in range(2):
         levels = []
         for i in range(LINE):
-            pieces = part_refs[i][2 * HEAD :, :].astype(jnp.float32)[3 * rc : 3 * rc + 3, :]
+            pieces = part_ref[i, 2 * HEAD :, :].astype(jnp.float32)[3 * rc : 3 * rc + 3, :]
             levels.append(pieces[0:1] + pieces[1:2] + pieces[2:3])
         top = functools.reduce(jnp.maximum, levels)
         shares = [jnp.exp2(level - top) for level in levels]
         scale = gate / functools.reduce(jnp.add, shares)
         mixed = (1.0 - gate) * window_ref[rc]
         for i in range(LINE):
-            mixed = mixed + part_refs[i][rc * HEAD : (rc + 1) * HEAD, :].astype(jnp.float32) * (shares[i] * scale)
+            mixed = mixed + part_ref[i, rc * HEAD : (rc + 1) * HEAD, :].astype(jnp.float32) * (shares[i] * scale)
         for g in range(4):
             flat = mixed[:, g * 128 : (g + 1) * 128].T.astype(jnp.bfloat16)
             for x in range(X):
@@ -280,29 +279,28 @@
     places = (indices // (2 * BLK_DEV)) * SHARD + (indices % (2 * BLK_DEV)) * PAIR
     counts = jnp.sum(here.astype(jnp.int32), axis=1)
 
-    returned = {}
-    for deltas in WAVES:
-        partials = pl.pallas_call(
-            functools.partial(memory_kernel, deltas),
-            out_shape=[jax.ShapeDtypeStruct((OROWS, ROWS), jnp.bfloat16)] * len(deltas),
-            in_specs=[smem] * 4 + [vmem] * 3,
-            out_specs=[vmem] * len(deltas),
-            scratch_shapes=[
-                pltpu.VMEM((2, ROWS, HEAD), jnp.bfloat16),
-                pltpu.VMEM((2, HEAD, ROWS), jnp.float32),
-                pltpu.VMEM((2, 1, ROWS), jnp.float32),
-                pltpu.VMEM((2, 1, ROWS), jnp.float32),
-            ],
-            compiler_params=pltpu.CompilerParams(vmem_limit_bytes=24 << 20),
-            cost_estimate=pl.CostEstimate(
-                flops=len(deltas) * 16 * ROWS * BLOCK * HEAD * 8,
-                bytes_accessed=len(deltas) << 20,
-                transcendentals=len(deltas) * 16 * ROWS * BLOCK,
-            ),
-            name="memory",
-        )(counts, places, indices, placed, lists, powers, cache)
-        for delta, partial in zip(deltas, partials):
-            returned[delta] = shift(partial, Q_LINES, delta) if delta else partial
+    partial = pl.pallas_call(
+        memory_kernel,
+        out_shape=pltpu.HBM((LINE, OROWS, ROWS), jnp.bfloat16),
+        in_specs=[smem] * 3 + [vmem] * 3,
+        out_specs=pl.BlockSpec(memory_space=pltpu.HBM),
+        scratch_shapes=[
+            pltpu.VMEM((2, OROWS, ROWS), jnp.bfloat16),
+            pltpu.VMEM((2, ROWS, HEAD), jnp.bfloat16),
+            pltpu.VMEM((2, HEAD, ROWS), jnp.float32),
+            pltpu.VMEM((2, 1, ROWS), jnp.float32),
+            pltpu.VMEM((2, 1, ROWS), jnp.float32),
+            pltpu.SemaphoreType.DMA((2,)),
+        ],
+        compiler_params=pltpu.CompilerParams(vmem_limit_bytes=24 << 20),
+        cost_estimate=pl.CostEstimate(
+            flops=4 * 64 * ROWS * BLOCK * HEAD, bytes_accessed=6 << 20, transcendentals=64 * ROWS * BLOCK
+        ),
+        name="memory",
+    )(counts, places, indices, lists, powers, cache)
+    returned = lax.all_to_all(
+        partial, SEQ, split_axis=0, concat_axis=0, axis_index_groups=Q_LINES, tiled=True
+    )
 
     q_mine, q_other = mine_and_other(by_head)
     k_mine, k_other = mine_and_other(keys.transpose(1, 0, 2))
@@ -336,12 +334,12 @@
     mixed = pl.pallas_call(
         merge_kernel,
         out_shape=jax.ShapeDtypeStruct((2 * X, 32, ROWS), jnp.bfloat16),
-        in_specs=[vmem] * (LINE + 2),
+        in_specs=[vmem] * 3,
         out_specs=vmem,
         compiler_params=pltpu.CompilerParams(vmem_limit_bytes=16 << 20),
         cost_estimate=pl.CostEstimate(flops=1 << 22, bytes_accessed=4 << 20, transcendentals=1 << 13),
         name="merge",
-    )(*[returned[d] for d in range(LINE)], window, gate)
+    )(returned, window, gate)
     rows = lax.all_to_all(mixed, ("head", "core"), split_axis=0, concat_axis=0, tiled=True)
     return rows.transpose(1, 0, 2).reshape(32, 2 * X * ROWS)
 

time: 167 us -> 149 us (0.89)
  starting transfers between devices: 45.3 us -> 23.4 us
  waiting for transfers between devices: 18 us -> 28.6 us
  other arithmetic: 8.63 us -> 4.07 us
  local copies, waits for them, and re-layouts: 6.31 us -> 3.74 us
  blocking collectives: 67.4 us -> 69.4 us
    ppermute x7 -> x0, starting transfers between devices: 28.7 us -> none  [shift(): lax.ppermute(value, SEQ, [(line[i], line[(i + by) % LINE]) for line in li...]
    ppermute x1, waiting for transfers between devices: 0.01 us -> 18.2 us  [on_device(): lax.ppermute(jnp.concatenate([k_second, v_second], axis=0), SEQ, onward)]
    ppermute x7 -> x0, waiting for transfers between devices: 14.8 us -> none  [shift(): lax.ppermute(value, SEQ, [(line[i], line[(i + by) % LINE]) for line in li...]
    all_to_all x0 -> x1, starting transfers between devices: none -> 6.8 us  [on_device(): lax.all_to_all(partial, SEQ, split_axis=0, concat_axis=0, axis_index_grou...]
    all_to_all x0 -> x1, waiting for transfers between devices: none -> 5.17 us  [on_device(): lax.all_to_all(partial, SEQ, split_axis=0, concat_axis=0, axis_index_grou...]
    convert_element_type x1, other arithmetic: 5.8 us -> 1.25 us  [on_device(): cache = gathered.astype(jnp.bfloat16)]
    ppermute x1, waiting for transfers between devices: 0.01 us -> 2.52 us  [on_device(): lists = lax.ppermute(parts[:, SHARD - 2 * QROWS:], 'core', swap)]
    all_to_all x1, blocking collectives: 12.2 us -> 14.3 us  [on_device(): lax.all_to_all(mixed, ('head', 'core'), split_axis=0, concat_axis=0, tile...]
  transfers between devices with their start and end apart: 11 -> 5, of which waited for: 6 -> 5; matrix products, arithmetic and copies ran while one was open for 5% -> 1% of each run, Pallas kernels for 10% -> 1%
where the time goes in v6:
time: 149 us; the launch traced here: 148 us
  blocking collectives  69.4 us (47%)
  waiting for transfers between devices  28.6 us (19%)
  starting transfers between devices  23.4 us (16%)
  Pallas kernels  18.6 us (12%)
  other arithmetic  4.07 us (3%)
  local copies, waits for them, and re-layouts  3.74 us (3%)
    all_gather x1, blocking collectives, on_device(): lax.all_gather(shard, SEQ, axis_index_groups=KV_LINES, tiled=True)  55.2 us
    ppermute x1, waiting for transfers between devices, on_device(): lax.ppermute(jnp.concatenate([k_second, v_second], axis=0), SEQ, onward)  18.2 us
    pallas_call x1, Pallas kernels, on_device(): pl.pallas_call(memory_kernel, out_shape=pltpu.HBM((LINE, OROWS, ROWS), jn...  14.5 us
    all_to_all x1, blocking collectives, on_device(): lax.all_to_all(mixed, ('head', 'core'), split_axis=0, concat_axis=0, tile...  14.3 us
    ppermute x1, starting transfers between devices, on_device(): theirs = lax.ppermute(other, 'core', swap)  8.79 us
    all_to_all x1, starting transfers between devices, on_device(): lax.all_to_all(partial, SEQ, split_axis=0, concat_axis=0, axis_index_grou...  6.8 us
    all_to_all x1, waiting for transfers between devices, on_device(): lax.all_to_all(partial, SEQ, split_axis=0, concat_axis=0, axis_index_grou...  5.17 us
    ppermute x1, starting transfers between devices, on_device(): lax.ppermute(jnp.concatenate([k_second, v_second], axis=0), SEQ, onward)  3.35 us
  transfers between devices with their start and end apart: 5, of which 5 were waited for; matrix products, arithmetic and copies ran while one was open for 1% of the time, Pallas kernels for 1%

profile of v6, /device:TPU:1, one launch (start us, length us, event | category | flops | bytes accessed | tf_op | source)
XLA Modules:
  0.0 148.1 jit_solution(3513197201525590276)
XLA Ops:
  0.0 1.0 copy.39
  1.0 0.7 fusion.25
  1.7 1.3 copy_bitcast_fusion
  3.0 0.1 fusion.6.ids_ref
  3.1 0.1 pad_add_fusion.where_ref
  3.2 2.6 %pack.1 = (bf16[2048,128]{1,0:T(8,128)(2,1)S(1)}, bf16[16,128]{1,0:T(8,128)(2,1)S(1)}, bf16[528,128]{1,0:T(8,128)(2,1)S(1)}, bf16[2592,128]{1,0:T(8,128)(2,1)S(1)}, s32[8,128]{1,0:T(8,128)S(1)}) custom-call(s32[3]{0:T(128)S(1)} %pad_add_fusion.where_ref, bf16[2,1024,128]{2,1,0:T(8,128)(2,1)S(1)} %get-tuple-element.41.k_ref, ...), custom_call_target="tpu_custom_call" | custom-call | flops 4194304 | bytes 3145728 | tf_op jit(solution)/shard_map/pack/pallas_call | solution.py:231
  5.8 8.8 %collective-permute-start = (bf16[2592,128]{1,0:T(8,128)(2,1)S(1)}, bf16[2592,128]{1,0:T(8,128)(2,1)S(1)}, u32[]{:S(2)}, u32[]{:S(2)}) collective-permute-start(bf16[2592,128]{1,0:T(8,128)(2,1)S(1)} %get-tuple-element.12), channel_id=1, source_target_pairs={{0,4},{4,0},{1,5},{5,1},{2,6},{6,2},{3,7},{7,3},{8,12},{12,8},{9,1... | collective-permute-start | bytes 1990664 | tf_op jit(solution)/shard_map/ppermute | solution.py:253
  14.6 1.7 %collective-permute-done = bf16[2592,128]{1,0:T(8,128)(2,1)S(1)} collective-permute-done((bf16[2592,128]{1,0:T(8,128)(2,1)S(1)}, bf16[2592,128]{1,0:T(8,128)(2,1)S(1)}, u32[]{:S(2)}, u32[]{:S(2)}) %collective-permute-start) | collective-permute-done | bytes 663584 | tf_op jit(solution)/shard_map/ppermute | solution.py:253
  16.3 0.1 slice_dynamic-update-slice_fusion
  16.4 0.1 select_dynamic-update-slice_fusion.1
  16.5 0.1 select_dynamic-update-slice_fusion
  16.5 0.3 convert_element_type.45
  16.8 55.2 %all-gather.1 = f16[41472,128]{1,0:T(8,128)(2,1)S(1)} all-gather(f16[5184,128]{1,0:T(8,128)(2,1)S(1)} %convert_element_type.45), channel_id=1, replica_groups={{0,8,16,24,32,40,48,56},{64,72,80,88,96,104,112,120},{128,136,144,152,1..., dimensions={0}, use_global_device_ids=true | all-gather | bytes 11943936 | tf_op jit(solution)/shard_map/all_gather | solution.py:258
  72.0 0.4 slice.94
  72.4 2.3 %collective-permute-start.1 = (f16[8,1056,128]{2,1,0:T(8,128)(2,1)S(1)}, f16[8,1056,128]{2,1,0:T(8,128)(2,1)S(1)}, u32[]{:S(2)}, u32[]{:S(2)}) collective-permute-start(f16[8,1056,128]{2,1,0:T(8,128)(2,1)S(1)} %slice.94), channel_id=1, source_target_pairs={{0,4},{4,0},{1,5},{5,1},{2,6},{6,2},{3,7},{7,3},{8,12},{12,8},{9,1... | collective-permute-start | bytes 6488072 | tf_op jit(solution)/shard_map/ppermute | solution.py:260
  74.8 1.2 convert_element_type.56.kv_ref
  76.0 2.5 %collective-permute-done.1 = f16[8,1056,128]{2,1,0:T(8,128)(2,1)S(1)} collective-permute-done((f16[8,1056,128]{2,1,0:T(8,128)(2,1)S(1)}, f16[8,1056,128]{2,1,0:T(8,128)(2,1)S(1)}, u32[]{:S(2)}, u32[]{:S(2)}) %collective-permute-start.1) | collective-permute-done | bytes 2162720 | tf_op jit(solution)/shard_map/ppermute | solution.py:260
  78.5 0.4 convert_element_type.46
  79.0 0.1 fusion.11
  79.1 0.1 convert_reduce_fusion.1
  79.2 0.4 convert_reduce_fusion
  79.5 0.3 select_reduce_fusion.power_at_ref
  79.9 14.5 %memory.1 = bf16[8,272,512]{2,1,0:T(8,128)(2,1)} custom-call(s32[16]{0:T(128)S(1)} %get-tuple-element.17.count_ref, s32[16,16]{1,0:T(8,128)S(1)} %fusion.13.place_ref, s32[16,16]{1,0:T(8,128)S(1)} %select_reduce_fusion.power_at_ref, bf16[8448,128]{1,0:T(8,128)(2,1)S(1)} %bitcast.60, f32[256,128]{1,0:T(8,128)S(1)} %bitcast_convert_fusion.powers_ref, ...), custom_call_target="tpu_custom_call" | custom-call | flops 1073741824 | bytes 6291456 | tf_op jit(solution)/shard_map/memory/pallas_call | solution.py:282
  94.4 0.0 copy-start
  94.4 0.0 copy-start.1
  94.4 6.8 %all-to-all-start = ((bf16[8,272,512]{2,1,0:T(8,128)(2,1)}), bf16[8,272,512]{2,1,0:T(8,128)(2,1)S(1)}, u32[]{:S(2)}, u32[]{:S(2)}) async-start(bf16[8,272,512]{2,1,0:T(8,128)(2,1)} %memory.1), calls=%async_computation | async-start | bytes 4456448 | tf_op jit(solution)/shard_map/all_to_all | solution.py:301
  101.2 0.0 copy-done
  101.2 0.0 copy-start.2
  101.3 0.0 copy-done.1
  101.4 2.1 %collective-permute-start.2 = (bf16[768,128]{1,0:T(8,128)(2,1)S(1)}, bf16[768,128]{1,0:T(8,128)(2,1)S(1)}, u32[]{:S(2)}, u32[]{:S(2)}) collective-permute-start(bf16[768,128]{1,0:T(8,128)(2,1)S(1)} %pad_maximum_fusion.1), channel_id=1, source_target_pairs={{0,4},{4,0},{1,5},{5,1},{2,6},{6,2},{3,7},{7,3},{8,12},{12,8},{9,1... | collective-permute-start | bytes 589832 | tf_op jit(solution)/shard_map/ppermute | solution.py:308
  103.5 0.0 copy-done.2
  103.6 0.1 broadcast_select_fusion.4
  103.6 1.1 collective-permute-done.2
  104.7 3.4 %collective-permute-start.3 = (bf16[256,128]{1,0:T(8,128)(2,1)S(1)}, bf16[256,128]{1,0:T(8,128)(2,1)S(1)}, u32[]{:S(2)}, u32[]{:S(2)}) collective-permute-start(bf16[256,128]{1,0:T(8,128)(2,1)S(1)} %pad_maximum_fusion.4), channel_id=1, source_target_pairs={{0,8},{4,12},{8,16},{12,20},{16,24},{20,28},{24,32},{28,36},{32,40... | collective-permute-start | bytes 196616 | tf_op jit(solution)/shard_map/ppermute | solution.py:313
  108.2 18.2 %collective-permute-done.3 = bf16[256,128]{1,0:T(8,128)(2,1)S(1)} collective-permute-done((bf16[256,128]{1,0:T(8,128)(2,1)S(1)}, bf16[256,128]{1,0:T(8,128)(2,1)S(1)}, u32[]{:S(2)}, u32[]{:S(2)}) %collective-permute-start.3) | collective-permute-done | bytes 65568 | tf_op jit(solution)/shard_map/ppermute | solution.py:313
  126.4 0.8 window.1.window_ref
  127.3 5.2 %all-to-all-done.part_ref = bf16[8,272,512]{2,1,0:T(8,128)(2,1)S(1)} async-done(((bf16[8,272,512]{2,1,0:T(8,128)(2,1)}), bf16[8,272,512]{2,1,0:T(8,128)(2,1)S(1)}, u32[]{:S(2)}, u32[]{:S(2)}) %all-to-all-start) | async-done | bytes 2228256 | tf_op jit(solution)/shard_map/all_to_all | solution.py:301
  132.4 0.1 broadcast_in_dim.42
  132.5 0.6 merge.1
  133.1 14.3 %all_to_all.10 = bf16[8,32,512]{2,1,0:T(8,128)(2,1)S(1)} all-to-all(bf16[8,32,512]{2,1,0:T(8,128)(2,1)S(1)} %merge.1), channel_id=1, replica_groups=mesh['z'=8,'y'=8,'core'=2,'head'=4] {'head','core'}, dimensions={0} | all-to-all | bytes 524288 | tf_op jit(solution)/shard_map/all_to_all | solution.py:343
  147.4 0.7 copy.27
  (25 shorter events, 0.3 us)
Async XLA Ops:
  5.8 10.5 %collective-permute-start = (bf16[2592,128]{1,0:T(8,128)(2,1)S(1)}, bf16[2592,128]{1,0:T(8,128)(2,1)S(1)}, u32[]{:S(2)}, u32[]{:S(2)}) collective-permute-start(bf16[2592,128]{1,0:T(8,128)(2,1)S(1)} %get-tuple-element.12), channel_id=1, source_target_pairs={{0,4},{4,0},{1,5},{5,1},{2,6},{6,2},{3,7},{7,3},{8,12},{12,8},{9,1... | collective-permute-start | bytes 1990664 | tf_op jit(solution)/shard_map/ppermute | solution.py:253
  72.4 6.2 %collective-permute-start.1 = (f16[8,1056,128]{2,1,0:T(8,128)(2,1)S(1)}, f16[8,1056,128]{2,1,0:T(8,128)(2,1)S(1)}, u32[]{:S(2)}, u32[]{:S(2)}) collective-permute-start(f16[8,1056,128]{2,1,0:T(8,128)(2,1)S(1)} %slice.94), channel_id=1, source_target_pairs={{0,4},{4,0},{1,5},{5,1},{2,6},{6,2},{3,7},{7,3},{8,12},{12,8},{9,1... | collective-permute-start | bytes 6488072 | tf_op jit(solution)/shard_map/ppermute | solution.py:260
  94.4 6.8 %copy-start = (bf16[128,2,128]{2,1,0:T(2,128)(2,1)S(1)}, bf16[128,2,128]{2,1,0:T(2,128)(2,1)}, u32[]{:S(2)}) copy-start(bf16[128,2,128]{2,1,0:T(2,128)(2,1)} %param.9) | copy-start | bytes 196612
  94.4 6.9 %copy-start.1 = (bf16[128,2,128]{2,1,0:T(2,128)(2,1)S(1)}, bf16[128,2,128]{2,1,0:T(2,128)(2,1)}, u32[]{:S(2)}) copy-start(bf16[128,2,128]{2,1,0:T(2,128)(2,1)} %param.8) | copy-start | bytes 196612
  94.4 38.0 %all-to-all-start = ((bf16[8,272,512]{2,1,0:T(8,128)(2,1)}), bf16[8,272,512]{2,1,0:T(8,128)(2,1)S(1)}, u32[]{:S(2)}, u32[]{:S(2)}) async-start(bf16[8,272,512]{2,1,0:T(8,128)(2,1)} %memory.1), calls=%async_computation | async-start | bytes 4456448 | tf_op jit(solution)/shard_map/all_to_all | solution.py:301
  101.2 2.3 %copy-start.2 = (f32[8]{0:T(128)S(1)}, f32[8]{0:T(128)}, u32[]{:S(2)}) copy-start(f32[8]{0:T(128)} %param.13) | copy-start | bytes 100
  101.4 3.3 %collective-permute-start.2 = (bf16[768,128]{1,0:T(8,128)(2,1)S(1)}, bf16[768,128]{1,0:T(8,128)(2,1)S(1)}, u32[]{:S(2)}, u32[]{:S(2)}) collective-permute-start(bf16[768,128]{1,0:T(8,128)(2,1)S(1)} %pad_maximum_fusion.1), channel_id=1, source_target_pairs={{0,4},{4,0},{1,5},{5,1},{2,6},{6,2},{3,7},{7,3},{8,12},{12,8},{9,1... | collective-permute-start | bytes 589832 | tf_op jit(solution)/shard_map/ppermute | solution.py:308
  104.7 21.6 %collective-permute-start.3 = (bf16[256,128]{1,0:T(8,128)(2,1)S(1)}, bf16[256,128]{1,0:T(8,128)(2,1)S(1)}, u32[]{:S(2)}, u32[]{:S(2)}) collective-permute-start(bf16[256,128]{1,0:T(8,128)(2,1)S(1)} %pad_maximum_fusion.4), channel_id=1, source_target_pairs={{0,8},{4,12},{8,16},{12,20},{16,24},{20,28},{24,32},{28,36},{32,40... | collective-permute-start | bytes 196616 | tf_op jit(solution)/shard_map/ppermute | solution.py:313

commit v7 on v6

--- a/solution.py
+++ b/solution.py
@@ -71,7 +71,9 @@
 
     def queries(head, out_ref, first):
         rows = lax.broadcasted_iota(jnp.int32, (16, 128), 0)
-        extra = ids_ref[head].astype(jnp.float32)
+        ids = ids_ref[head]
+        coded = jnp.concatenate([ids >> 6, ids & 63, jnp.zeros((1, HEAD - 2 * TOPK), jnp.int32)], axis=1)
+        extra = jnp.where(rows == ROWS // 128, coded.astype(jnp.float32), 0.0)
         for i in range(ROWS // 128):
             out, row = scaled(q_ref[head, i * 128 : (i + 1) * 128, :].astype(jnp.float32))
             out_ref[first + i * 128 : first + (i + 1) * 128, :] = out
@@ -84,33 +86,26 @@
     queries(core, other_ref, SHARE + BLK_DEV)
 
 
-def window_kernel(first_ref, q_ref, k_ref, v_ref, o_ref):
-    for rc in range(2):
+def window_kernel(where_ref, q_ref, k_ref, v_ref, o_ref):
+    has_before = where_ref[0] + where_ref[1] + where_ref[2] > 0
+    for head in range(2):
         s = lax.dot_general(
-            k_ref[pl.ds(128 * rc, 256), :],
-            q_ref[rc],
-            (((1,), (1,)), ((), ())),
-            preferred_element_type=jnp.float32,
+            k_ref[head], q_ref[head], (((1,), (1,)), ((), ())), preferred_element_type=jnp.float32
         )
         kpos = lax.broadcasted_iota(jnp.int32, s.shape, 0) - 128
         qpos = lax.broadcasted_iota(jnp.int32, s.shape, 1) & 127
-        allowed = (kpos <= qpos) & (kpos > qpos - 128)
-        if rc == 0:
-            allowed = allowed & ((kpos >= 0) | (first_ref[0] == 0))
+        allowed = (kpos <= qpos) & (kpos > qpos - 128) & ((kpos >= 0) | has_before)
         s = jnp.where(allowed, s, LOWEST)
         top = jnp.max(s, axis=0, keepdims=True)
         p = jnp.exp2((s - top) * EXPO)
         total = jnp.sum(p, axis=0, keepdims=True)
         out = lax.dot_general(
-            v_ref[pl.ds(128 * rc, 256), :],
-            p.astype(jnp.bfloat16),
-            (((0,), (0,)), ((), ())),
-            preferred_element_type=jnp.float32,
+            v_ref[head], p.astype(jnp.bfloat16), (((0,), (0,)), ((), ())), preferred_element_type=jnp.float32
         )
-        o_ref[rc] = out / total
-
-
-def memory_kernel(count_ref, place_ref, power_at_ref, q_ref, powers_ref, kv_ref, o_ref, stage, q_buf, acc, top_s, sum_s, out_sems):
+        o_ref[head ^ where_ref[2]] = out / total
+
+
+def memory_kernel(count_ref, place_ref, power_at_ref, q_ref, powers_ref, kv_ref, near_ref, o_ref, stage, q_buf, acc, top_s, sum_s, out_sems):
     eye = lax.broadcasted_iota(jnp.int32, (128, 128), 0) == lax.broadcasted_iota(jnp.int32, (128, 128), 1)
     low = lax.broadcasted_iota(jnp.int32, (1, 128), 1) < BLOCK
 
@@ -156,7 +151,9 @@
                 q_buf[rc, i * 128 : (i + 1) * 128, :] = back(
                     q_ref[first + i * 128 : first + (i + 1) * 128, :], extra[i : i + 1, :]
                 )
-            s, top, values = attend(index, rc, counts[rc], 0)
+        held = [attend(peer * 2 + rc, rc, counts[rc], 0) for rc in range(2)]
+        for rc in range(2):
+            s, top, values = held[rc]
             p = jnp.exp2((s - top) * EXPO)
             top_s[rc] = top
             sum_s[rc] = jnp.sum(p, axis=0, keepdims=True)
@@ -193,7 +190,7 @@
     send(LINE - 1).wait()
 
 
-def merge_kernel(part_ref, window_ref, gate_ref, o_ref):
+def merge_kernel(where_ref, part_ref, window_ref, their_window_ref, gate_ref, o_ref):
     gate = gate_ref[...]
     for rc in range(2):
         levels = []
@@ -203,7 +200,7 @@
         top = functools.reduce(jnp.maximum, levels)
         shares = [jnp.exp2(level - top) for level in levels]
         scale = gate / functools.reduce(jnp.add, shares)
-        mixed = (1.0 - gate) * window_ref[rc]
+        mixed = (1.0 - gate) * jnp.where(where_ref[2] == rc, window_ref[0], their_window_ref[...])
         for i in range(LINE):
             mixed = mixed + part_ref[i, rc * HEAD : (rc + 1) * HEAD, :].astype(jnp.float32) * (shares[i] * scale)
         for g in range(4):
@@ -219,15 +216,11 @@
     vmem = pl.BlockSpec(memory_space=pltpu.VMEM)
     swap = [(0, 1), (1, 0)]
 
-    def mine_and_other(array):
-        return jnp.where(first_core, array[0], array[1]), jnp.where(first_core, array[1], array[0])
-
     def by_core(mine, other):
         return jnp.where(first_core, mine, other), jnp.where(first_core, other, mine)
 
+    where = jnp.stack([z, y, core]).astype(jnp.int32)
     by_head = queries.reshape(128, 2, 4, HEAD).transpose(1, 2, 0, 3).reshape(2, ROWS, HEAD)
-    ids = jnp.concatenate([mem_ids // 64, mem_ids % 64], axis=2).astype(jnp.bfloat16)
-    ids = jnp.pad(ids, ((0, 0), (4, 11), (0, HEAD - 2 * TOPK)))
     mine, mine_powers, mine_q, other, placed = pl.pallas_call(
         pack_kernel,
         out_shape=[
@@ -244,11 +237,14 @@
         cost_estimate=pl.CostEstimate(flops=1 << 22, bytes_accessed=3 << 20, transcendentals=1 << 13),
         name="pack",
     )(
-        jnp.stack([z, y, core]).astype(jnp.int32),
+        where,
         mem_keys.transpose(1, 0, 2),
         mem_values.transpose(1, 0, 2),
         by_head,
-        ids,
+        mem_ids,
+    )
+    near = lax.ppermute(
+        jnp.concatenate([keys, values], axis=0).transpose(1, 0, 2), SEQ, [(i, i + 1) for i in range(2 * Z * Y - 1)]
     )
     theirs = lax.ppermute(other, "core", swap)
     their_cache, their_powers, their_q = jnp.split(theirs, [SHARE, SHARE + BLK_DEV])
@@ -282,7 +278,7 @@
     partial = pl.pallas_call(
         memory_kernel,
         out_shape=pltpu.HBM((LINE, OROWS, ROWS), jnp.bfloat16),
-        in_specs=[smem] * 3 + [vmem] * 3,
+        in_specs=[smem] * 3 + [vmem] * 3 + [pl.BlockSpec(memory_space=pl.ANY)],
         out_specs=pl.BlockSpec(memory_space=pltpu.HBM),
         scratch_shapes=[
             pltpu.VMEM((2, OROWS, ROWS), jnp.bfloat16),
@@ -297,21 +293,11 @@
             flops=4 * 64 * ROWS * BLOCK * HEAD, bytes_accessed=6 << 20, transcendentals=64 * ROWS * BLOCK
         ),
         name="memory",
-    )(counts, places, indices, lists, powers, cache)
+    )(counts, places, indices, lists, powers, cache, near)
     returned = lax.all_to_all(
         partial, SEQ, split_axis=0, concat_axis=0, axis_index_groups=Q_LINES, tiled=True
     )
 
-    q_mine, q_other = mine_and_other(by_head)
-    k_mine, k_other = mine_and_other(keys.transpose(1, 0, 2))
-    v_mine, v_other = mine_and_other(values.transpose(1, 0, 2))
-    near = lax.ppermute(jnp.concatenate([q_other, k_other, v_other], axis=0), "core", swap)
-    q_first, q_second = by_core(q_mine, near[:ROWS])
-    k_first, k_second = by_core(k_mine, near[ROWS : ROWS + 128])
-    v_first, v_second = by_core(v_mine, near[ROWS + 128 :])
-    onward = [(2 * i + c, 2 * i + 2 + c) for i in range(Z * Y - 1) for c in range(2)]
-    before = lax.ppermute(jnp.concatenate([k_second, v_second], axis=0), SEQ, onward)
-    is_first = ((z == 0) & (y == 0)).astype(jnp.int32).reshape(1)
     window = pl.pallas_call(
         window_kernel,
         out_shape=jax.ShapeDtypeStruct((2, HEAD, ROWS), jnp.float32),
@@ -323,23 +309,24 @@
         ),
         name="window",
     )(
-        is_first,
-        jnp.stack([q_first, q_second]),
-        jnp.concatenate([before[:128], k_first, k_second], axis=0),
-        jnp.concatenate([before[128:], v_first, v_second], axis=0),
-    )
+        where,
+        by_head,
+        jnp.concatenate([near[:, :128], keys.transpose(1, 0, 2)], axis=1),
+        jnp.concatenate([near[:, 128:], values.transpose(1, 0, 2)], axis=1),
+    )
+    their_window = lax.ppermute(window[1], "core", swap)
 
     gate = jax.nn.sigmoid(gate_logits).reshape(2, 4)
     gate = jnp.repeat(jnp.where(first_core, gate[0], gate[1]), 128)[None, :]
     mixed = pl.pallas_call(
         merge_kernel,
         out_shape=jax.ShapeDtypeStruct((2 * X, 32, ROWS), jnp.bfloat16),
-        in_specs=[vmem] * 3,
+        in_specs=[smem] + [vmem] * 4,
         out_specs=vmem,
         compiler_params=pltpu.CompilerParams(vmem_limit_bytes=16 << 20),
         cost_estimate=pl.CostEstimate(flops=1 << 22, bytes_accessed=4 << 20, transcendentals=1 << 13),
         name="merge",
-    )(returned, window, gate)
+    )(where, returned, window, their_window, gate)
     rows = lax.all_to_all(mixed, ("head", "core"), split_axis=0, concat_axis=0, tiled=True)
     return rows.transpose(1, 0, 2).reshape(32, 2 * X * ROWS)
 

time: 149 us -> 148 us (level)
  waiting for transfers between devices: 28.6 us -> 24.6 us
  starting transfers between devices: 23.4 us -> 26.4 us
  blocking collectives: 69.4 us -> 71.4 us
    ppermute x2, waiting for transfers between devices: 19.3 us -> 1.05 us  [the longest x1 1.04 us: on_device(): their_window = lax.ppermute(window[1], 'core', swap)]
    all_to_all x1, waiting for transfers between devices: 5.17 us -> 21.9 us  [on_device(): lax.all_to_all(partial, SEQ, split_axis=0, concat_axis=0, axis_index_grou...]
    ppermute x2, starting transfers between devices: 5.5 us -> 9.24 us  [the longest x1 6.18 us: on_device(): their_window = lax.ppermute(window[1], 'core', swap)]
    ppermute x1, waiting for transfers between devices: 2.52 us -> 0.01 us  [on_device(): lists = lax.ppermute(parts[:, SHARD - 2 * QROWS:], 'core', swap)]
    all_to_all x1, blocking collectives: 14.3 us -> 16.2 us  [on_device(): lax.all_to_all(mixed, ('head', 'core'), split_axis=0, concat_axis=0, tile...]
    pallas_call x1, Pallas kernels: 14.5 us -> 12.6 us  [on_device(): pl.pallas_call(memory_kernel, out_shape=pltpu.HBM((LINE, OROWS, ROWS), jn...]
  transfers between devices with their start and end apart: 5 -> 5, of which waited for: 5 -> 3; matrix products, arithmetic and copies ran while one was open for 1% -> 2% of each run, Pallas kernels for 1% -> 1%
where the time goes in v7:
time: 148 us; the launch traced here: 147 us
  blocking collectives  71.4 us (48%)
  starting transfers between devices  26.4 us (18%)
  waiting for transfers between devices  24.6 us (17%)
  Pallas kernels  17.8 us (12%)
  local copies, waits for them, and re-layouts  3.79 us (3%)
  other arithmetic  3.19 us (2%)
    all_gather x1, blocking collectives, on_device(): lax.all_gather(shard, SEQ, axis_index_groups=KV_LINES, tiled=True)  55.2 us
    all_to_all x1, waiting for transfers between devices, on_device(): lax.all_to_all(partial, SEQ, split_axis=0, concat_axis=0, axis_index_grou...  21.9 us
    all_to_all x1, blocking collectives, on_device(): lax.all_to_all(mixed, ('head', 'core'), split_axis=0, concat_axis=0, tile...  16.2 us
    pallas_call x1, Pallas kernels, on_device(): pl.pallas_call(memory_kernel, out_shape=pltpu.HBM((LINE, OROWS, ROWS), jn...  12.6 us
    ppermute x1, starting transfers between devices, on_device(): theirs = lax.ppermute(other, 'core', swap)  8.8 us
    ppermute x1, starting transfers between devices, on_device(): their_window = lax.ppermute(window[1], 'core', swap)  6.18 us
    all_to_all x1, starting transfers between devices, on_device(): lax.all_to_all(partial, SEQ, split_axis=0, concat_axis=0, axis_index_grou...  6.03 us
    ppermute x1, starting transfers between devices, on_device(): lax.ppermute(jnp.concatenate([keys, values], axis=0).transpose(1, 0, 2),...  3.06 us
  transfers between devices with their start and end apart: 5, of which 3 were waited for; matrix products, arithmetic and copies ran while one was open for 2% of the time, Pallas kernels for 1%

profile of v7, /device:TPU:1, one launch (start us, length us, event | category | flops | bytes accessed | tf_op | source)
XLA Modules:
  0.0 147.4 jit_solution(10441957477697779675)
XLA Ops:
  0.0 0.0 copy-start
  0.0 1.0 copy.25
  1.0 1.3 copy_bitcast_fusion
  2.3 0.1 pad_add_fusion.where_ref
  2.4 0.0 copy-done
  2.4 2.6 %pack.1 = (bf16[2048,128]{1,0:T(8,128)(2,1)S(1)}, bf16[16,128]{1,0:T(8,128)(2,1)S(1)}, bf16[528,128]{1,0:T(8,128)(2,1)S(1)}, bf16[2592,128]{1,0:T(8,128)(2,1)S(1)}, s32[8,128]{1,0:T(8,128)S(1)}) custom-call(s32[3]{0:T(128)S(1)} %pad_add_fusion.where_ref, bf16[2,1024,128]{2,1,0:T(8,128)(2,1)S(1)} %get-tuple-element.31.k_ref, ...), custom_call_target="tpu_custom_call" | custom-call | flops 4194304 | bytes 3145728 | tf_op jit(solution)/shard_map/pack/pallas_call | solution.py:224
  5.0 8.8 %collective-permute-start = (bf16[2592,128]{1,0:T(8,128)(2,1)S(1)}, bf16[2592,128]{1,0:T(8,128)(2,1)S(1)}, u32[]{:S(2)}, u32[]{:S(2)}) collective-permute-start(bf16[2592,128]{1,0:T(8,128)(2,1)S(1)} %get-tuple-element.12), channel_id=1, source_target_pairs={{0,4},{4,0},{1,5},{5,1},{2,6},{6,2},{3,7},{7,3},{8,12},{12,8},{9,1... | collective-permute-start | bytes 1990664 | tf_op jit(solution)/shard_map/ppermute | solution.py:249
  13.9 1.7 %collective-permute-done = bf16[2592,128]{1,0:T(8,128)(2,1)S(1)} collective-permute-done((bf16[2592,128]{1,0:T(8,128)(2,1)S(1)}, bf16[2592,128]{1,0:T(8,128)(2,1)S(1)}, u32[]{:S(2)}, u32[]{:S(2)}) %collective-permute-start) | collective-permute-done | bytes 663584 | tf_op jit(solution)/shard_map/ppermute | solution.py:249
  15.6 0.1 slice_dynamic-update-slice_fusion
  15.7 0.1 select_dynamic-update-slice_fusion.1
  15.7 0.1 select_dynamic-update-slice_fusion
  15.8 0.3 convert_element_type.33
  16.0 55.2 %all-gather.1 = f16[41472,128]{1,0:T(8,128)(2,1)S(1)} all-gather(f16[5184,128]{1,0:T(8,128)(2,1)S(1)} %convert_element_type.33), channel_id=1, replica_groups={{0,8,16,24,32,40,48,56},{64,72,80,88,96,104,112,120},{128,136,144,152,1..., dimensions={0}, use_global_device_ids=true | all-gather | bytes 11943936 | tf_op jit(solution)/shard_map/all_gather | solution.py:254
  71.2 0.0 copy-start.1
  71.2 0.0 copy-start.2
  71.2 0.4 slice.54
  71.6 2.3 %collective-permute-start.1 = (f16[8,1056,128]{2,1,0:T(8,128)(2,1)S(1)}, f16[8,1056,128]{2,1,0:T(8,128)(2,1)S(1)}, u32[]{:S(2)}, u32[]{:S(2)}) collective-permute-start(f16[8,1056,128]{2,1,0:T(8,128)(2,1)S(1)} %slice.54), channel_id=1, source_target_pairs={{0,4},{4,0},{1,5},{5,1},{2,6},{6,2},{3,7},{7,3},{8,12},{12,8},{9,1... | collective-permute-start | bytes 6488072 | tf_op jit(solution)/shard_map/ppermute | solution.py:256
  74.0 0.0 copy-done.1
  74.0 0.0 copy-done.2
  74.0 3.1 %collective-permute-start.2 = (bf16[2,256,128]{2,1,0:T(8,128)(2,1)S(1)}, bf16[2,256,128]{2,1,0:T(8,128)(2,1)S(1)}, u32[]{:S(2)}, u32[]{:S(2)}) collective-permute-start(bf16[2,256,128]{2,1,0:T(8,128)(2,1)S(1)} %maximum_bitcast_fusion), channel_id=1, source_target_pairs={{0,4},{4,8},{8,12},{12,16},{16,20},{20,24},{24,28},{28,32},{32,36}... | collective-permute-start | bytes 393224 | tf_op jit(solution)/shard_map/ppermute | solution.py:246
  77.2 1.2 convert_element_type.44.kv_ref
  78.4 0.0 collective-permute-done.1
  78.5 0.4 convert_element_type.34
  78.9 0.1 fusion.4
  79.0 0.1 convert_reduce_fusion.1
  79.1 0.4 convert_reduce_fusion
  79.5 0.3 select_reduce_fusion.power_at_ref
  79.8 0.0 collective-permute-done.2.near_ref
  79.9 12.6 %memory.1 = bf16[8,272,512]{2,1,0:T(8,128)(2,1)} custom-call(s32[16]{0:T(128)S(1)} %get-tuple-element.17.count_ref, s32[16,16]{1,0:T(8,128)S(1)} %fusion.6.place_ref, s32[16,16]{1,0:T(8,128)S(1)} %select_reduce_fusion.power_at_ref, bf16[8448,128]{1,0:T(8,128)(2,1)S(1)} %bitcast.43, f32[256,128]{1,0:T(8,128)S(1)} %bitcast_convert_fusion.powers_ref, ...), custom_call_target="tpu_custom_call" | custom-call | flops 1073741824 | bytes 6291456 | tf_op jit(solution)/shard_map/memory/pallas_call | solution.py:278
  92.4 6.0 %all-to-all-start = ((bf16[8,272,512]{2,1,0:T(8,128)(2,1)}), bf16[8,272,512]{2,1,0:T(8,128)(2,1)S(1)}, u32[]{:S(2)}, u32[]{:S(2)}) async-start(bf16[8,272,512]{2,1,0:T(8,128)(2,1)} %memory.1), calls=%async_computation | async-start | bytes 4456448 | tf_op jit(solution)/shard_map/all_to_all | solution.py:297
  98.5 0.0 copy-start.3
  98.5 1.4 window.1.window_ref
  99.9 6.2 %collective-permute-start.3 = (f32[128,512]{1,0:T(8,128)S(1)}, f32[128,512]{1,0:T(8,128)S(1)}, u32[]{:S(2)}, u32[]{:S(2)}) collective-permute-start(f32[128,512]{1,0:T(8,128)S(1)} %slice_bitcast_fusion), channel_id=1, source_target_pairs={{0,4},{4,0},{1,5},{5,1},{2,6},{6,2},{3,7},{7,3},{8,12},{12,8},{9,1... | collective-permute-start | bytes 786440 | tf_op jit(solution)/shard_map/ppermute | solution.py:317
  106.1 0.0 copy-done.3
  106.2 0.1 broadcast_select_fusion
  106.2 1.0 collective-permute-done.3.their_window_ref
  107.3 21.9 %all-to-all-done.part_ref = bf16[8,272,512]{2,1,0:T(8,128)(2,1)S(1)} async-done(((bf16[8,272,512]{2,1,0:T(8,128)(2,1)}), bf16[8,272,512]{2,1,0:T(8,128)(2,1)S(1)}, u32[]{:S(2)}, u32[]{:S(2)}) %all-to-all-start) | async-done | bytes 2228256 | tf_op jit(solution)/shard_map/all_to_all | solution.py:297
  129.2 0.1 broadcast_in_dim.42
  129.3 1.2 merge.1
  130.5 16.2 %all_to_all.10 = bf16[8,32,512]{2,1,0:T(8,128)(2,1)S(1)} all-to-all(bf16[8,32,512]{2,1,0:T(8,128)(2,1)S(1)} %merge.1), channel_id=1, replica_groups=mesh['z'=8,'y'=8,'core'=2,'head'=4] {'head','core'}, dimensions={0} | all-to-all | bytes 524288 | tf_op jit(solution)/shard_map/all_to_all | solution.py:330
  146.7 0.7 copy.33
  (18 shorter events, 0.3 us)
Async XLA Ops:
  0.0 2.4 %copy-start = (s32[2,1,32]{2,1,0:T(1,128)S(1)}, s32[2,1,32]{2,1,0:T(1,128)}, u32[]{:S(2)}) copy-start(s32[2,1,32]{2,1,0:T(1,128)} %ids_ref.1) | copy-start | bytes 772
  5.0 10.5 %collective-permute-start = (bf16[2592,128]{1,0:T(8,128)(2,1)S(1)}, bf16[2592,128]{1,0:T(8,128)(2,1)S(1)}, u32[]{:S(2)}, u32[]{:S(2)}) collective-permute-start(bf16[2592,128]{1,0:T(8,128)(2,1)S(1)} %get-tuple-element.12), channel_id=1, source_target_pairs={{0,4},{4,0},{1,5},{5,1},{2,6},{6,2},{3,7},{7,3},{8,12},{12,8},{9,1... | collective-permute-start | bytes 1990664 | tf_op jit(solution)/shard_map/ppermute | solution.py:249
  71.2 2.7 %copy-start.1 = (bf16[128,2,128]{2,1,0:T(2,128)(2,1)S(1)}, bf16[128,2,128]{2,1,0:T(2,128)(2,1)}, u32[]{:S(2)}) copy-start(bf16[128,2,128]{2,1,0:T(2,128)(2,1)} %param.9) | copy-start | bytes 196612
  71.2 2.8 %copy-start.2 = (bf16[128,2,128]{2,1,0:T(2,128)(2,1)S(1)}, bf16[128,2,128]{2,1,0:T(2,128)(2,1)}, u32[]{:S(2)}) copy-start(bf16[128,2,128]{2,1,0:T(2,128)(2,1)} %param.8) | copy-start | bytes 196612
  71.6 6.8 %collective-permute-start.1 = (f16[8,1056,128]{2,1,0:T(8,128)(2,1)S(1)}, f16[8,1056,128]{2,1,0:T(8,128)(2,1)S(1)}, u32[]{:S(2)}, u32[]{:S(2)}) collective-permute-start(f16[8,1056,128]{2,1,0:T(8,128)(2,1)S(1)} %slice.54), channel_id=1, source_target_pairs={{0,4},{4,0},{1,5},{5,1},{2,6},{6,2},{3,7},{7,3},{8,12},{12,8},{9,1... | collective-permute-start | bytes 6488072 | tf_op jit(solution)/shard_map/ppermute | solution.py:256
  74.0 5.8 %collective-permute-start.2 = (bf16[2,256,128]{2,1,0:T(8,128)(2,1)S(1)}, bf16[2,256,128]{2,1,0:T(8,128)(2,1)S(1)}, u32[]{:S(2)}, u32[]{:S(2)}) collective-permute-start(bf16[2,256,128]{2,1,0:T(8,128)(2,1)S(1)} %maximum_bitcast_fusion), channel_id=1, source_target_pairs={{0,4},{4,8},{8,12},{12,16},{16,20},{20,24},{24,28},{28,32},{32,36}... | collective-permute-start | bytes 393224 | tf_op jit(solution)/shard_map/ppermute | solution.py:246
  92.4 36.8 %all-to-all-start = ((bf16[8,272,512]{2,1,0:T(8,128)(2,1)}), bf16[8,272,512]{2,1,0:T(8,128)(2,1)S(1)}, u32[]{:S(2)}, u32[]{:S(2)}) async-start(bf16[8,272,512]{2,1,0:T(8,128)(2,1)} %memory.1), calls=%async_computation | async-start | bytes 4456448 | tf_op jit(solution)/shard_map/all_to_all | solution.py:297
  98.5 7.7 %copy-start.3 = (f32[8]{0:T(128)S(1)}, f32[8]{0:T(128)}, u32[]{:S(2)}) copy-start(f32[8]{0:T(128)} %param.13) | copy-start | bytes 100
  99.9 7.3 %collective-permute-start.3 = (f32[128,512]{1,0:T(8,128)S(1)}, f32[128,512]{1,0:T(8,128)S(1)}, u32[]{:S(2)}, u32[]{:S(2)}) collective-permute-start(f32[128,512]{1,0:T(8,128)S(1)} %slice_bitcast_fusion), channel_id=1, source_target_pairs={{0,4},{4,0},{1,5},{5,1},{2,6},{6,2},{3,7},{7,3},{8,12},{12,8},{9,1... | collective-permute-start | bytes 786440 | tf_op jit(solution)/shard_map/ppermute | solution.py:317

commit v8 on v7

--- a/solution.py
+++ b/solution.py
@@ -42,48 +42,46 @@
     largest = jnp.max(jnp.abs(x), axis=1, keepdims=True)
     power = 14.0 - jnp.floor(jnp.log2(jnp.maximum(largest, 1e-37)))
     power = jnp.clip(power, -113.0, 126.0)
-    return (x * jnp.exp2(power)).astype(jnp.bfloat16), jnp.broadcast_to(power, x.shape).T[0:1, :]
-
-
-def restored(x, power_row):
-    down = jnp.broadcast_to(jnp.exp2(-power_row), (128, 128)).T
-    return (x.astype(jnp.float32) * down).astype(jnp.bfloat16)
-
-
-def pack_kernel(
-    where_ref, k_ref, v_ref, q_ref, ids_ref, mine_ref, mine_powers_ref, mine_q_ref, other_ref, place_ref, powers
-):
+    return (x * jnp.exp2(power)).astype(jnp.bfloat16), power
+
+
+def pack_cache(k_ref, v_ref, head, out_ref):
+    lane = lax.broadcasted_iota(jnp.int32, (128, 128), 1)
+    powers = jnp.zeros((128, 128), jnp.float32)
+    for b in range(BLK_DEV):
+        at = slice(b * BLOCK, (b + 1) * BLOCK)
+        rows = jnp.concatenate([k_ref[head, at, :], v_ref[head, at, :]], axis=0).astype(jnp.float32)
+        out_ref[b * PAIR : (b + 1) * PAIR, :], power = scaled(rows)
+        powers = jnp.where(lane == b, power, powers)
+    return powers.T[:BLK_DEV, :].astype(jnp.bfloat16)
+
+
+def pack_queries(q_ref, ids_ref, head, out_ref, first):
+    lane = lax.broadcasted_iota(jnp.int32, (128, 128), 1)
+    powers = jnp.zeros((128, 128), jnp.float32)
+    for i in range(ROWS // 128):
+        rows = q_ref[head, i * 128 : (i + 1) * 128, :].astype(jnp.float32)
+        out_ref[first + i * 128 : first + (i + 1) * 128, :], power = scaled(rows)
+        powers = jnp.where(lane == i, power, powers)
+    ids = ids_ref[head]
+    coded = jnp.concatenate([ids >> 6, ids & 63, jnp.zeros((1, HEAD - 2 * TOPK), jnp.int32)], axis=1)
+    row = lax.broadcasted_iota(jnp.int32, (16, 128), 0)
+    extra = jnp.where(row == ROWS // 128, coded.astype(jnp.float32), powers.T[:16, :])
+    out_ref[first + ROWS : first + QROWS, :] = extra.astype(jnp.bfloat16)
+
+
+def pack_other_kernel(where_ref, k_ref, v_ref, q_ref, ids_ref, other_ref, place_ref):
     for i in range(3):
         place_ref[i : i + 1, :] = jnp.full((1, 128), where_ref[i], jnp.int32)
     core = where_ref[2]
-
-    def cache(head, out_ref):
-        def one_block(b, carry):
-            at = pl.multiple_of(b * BLOCK, BLOCK)
-            rows = jnp.concatenate([k_ref[head, pl.ds(at, BLOCK), :], v_ref[head, pl.ds(at, BLOCK), :]], axis=0)
-            out, row = scaled(rows.astype(jnp.float32))
-            out_ref[pl.ds(pl.multiple_of(b * PAIR, PAIR), PAIR), :] = out
-            powers[pl.ds(b, 1), :] = row
-            return carry
-
-        lax.fori_loop(0, BLK_DEV, one_block, 0, unroll=4)
-        return powers[...].astype(jnp.bfloat16)
-
-    def queries(head, out_ref, first):
-        rows = lax.broadcasted_iota(jnp.int32, (16, 128), 0)
-        ids = ids_ref[head]
-        coded = jnp.concatenate([ids >> 6, ids & 63, jnp.zeros((1, HEAD - 2 * TOPK), jnp.int32)], axis=1)
-        extra = jnp.where(rows == ROWS // 128, coded.astype(jnp.float32), 0.0)
-        for i in range(ROWS // 128):
-            out, row = scaled(q_ref[head, i * 128 : (i + 1) * 128, :].astype(jnp.float32))
-            out_ref[first + i * 128 : first + (i + 1) * 128, :] = out
-            extra = jnp.where(rows == i, row, extra)
-        out_ref[first + ROWS : first + QROWS, :] = extra.astype(jnp.bfloat16)
-
-    mine_powers_ref[...] = cache(core, mine_ref)
-    other_ref[SHARE : SHARE + BLK_DEV, :] = cache(1 - core, other_ref)
-    queries(1 - core, mine_q_ref, 0)
-    queries(core, other_ref, SHARE + BLK_DEV)
+    other_ref[SHARE : SHARE + BLK_DEV, :] = pack_cache(k_ref, v_ref, 1 - core, other_ref)
+    pack_queries(q_ref, ids_ref, core, other_ref, SHARE + BLK_DEV)
+
+
+def pack_mine_kernel(where_ref, k_ref, v_ref, q_ref, ids_ref, mine_ref, powers_ref, queries_ref):
+    core = where_ref[2]
+    powers_ref[...] = pack_cache(k_ref, v_ref, core, mine_ref)
+    pack_queries(q_ref, ids_ref, 1 - core, queries_ref, 0)
 
 
 def window_kernel(where_ref, q_ref, k_ref, v_ref, o_ref):
@@ -192,17 +190,20 @@
 
 def merge_kernel(where_ref, part_ref, window_ref, their_window_ref, gate_ref, o_ref):
     gate = gate_ref[...]
-    for rc in range(2):
+    for i, near in enumerate((window_ref.at[0], their_window_ref)):
+        rc = where_ref[2] ^ i
+        at = pl.ds(pl.multiple_of(rc * HEAD, HEAD), HEAD)
         levels = []
-        for i in range(LINE):
-            pieces = part_ref[i, 2 * HEAD :, :].astype(jnp.float32)[3 * rc : 3 * rc + 3, :]
+        for peer in range(LINE):
+            pieces = part_ref[peer, 2 * HEAD :, :].astype(jnp.float32)
+            pieces = jnp.where(rc == 0, pieces[0:3, :], pieces[3:6, :])
             levels.append(pieces[0:1] + pieces[1:2] + pieces[2:3])
         top = functools.reduce(jnp.maximum, levels)
         shares = [jnp.exp2(level - top) for level in levels]
         scale = gate / functools.reduce(jnp.add, shares)
-        mixed = (1.0 - gate) * jnp.where(where_ref[2] == rc, window_ref[0], their_window_ref[...])
-        for i in range(LINE):
-            mixed = mixed + part_ref[i, rc * HEAD : (rc + 1) * HEAD, :].astype(jnp.float32) * (shares[i] * scale)
+        mixed = (1.0 - gate) * near[...]
+        for peer in range(LINE):
+            mixed = mixed + part_ref[peer, at, :].astype(jnp.float32) * (shares[peer] * scale)
         for g in range(4):
             flat = mixed[:, g * 128 : (g + 1) * 128].T.astype(jnp.bfloat16)
             for x in range(X):
@@ -221,27 +222,31 @@
 
     where = jnp.stack([z, y, core]).astype(jnp.int32)
     by_head = queries.reshape(128, 2, 4, HEAD).transpose(1, 2, 0, 3).reshape(2, ROWS, HEAD)
-    mine, mine_powers, mine_q, other, placed = pl.pallas_call(
-        pack_kernel,
-        out_shape=[
-            jax.ShapeDtypeStruct((SHARE, HEAD), jnp.bfloat16),
-            jax.ShapeDtypeStruct((BLK_DEV, HEAD), jnp.bfloat16),
-            jax.ShapeDtypeStruct((QROWS, HEAD), jnp.bfloat16),
-            jax.ShapeDtypeStruct((SHARE + BLK_DEV + QROWS, HEAD), jnp.bfloat16),
-            jax.ShapeDtypeStruct((8, 128), jnp.int32),
-        ],
-        in_specs=[smem] + [vmem] * 4,
-        out_specs=[vmem] * 5,
-        scratch_shapes=[pltpu.VMEM((BLK_DEV, HEAD), jnp.float32)],
-        compiler_params=pltpu.CompilerParams(vmem_limit_bytes=16 << 20),
-        cost_estimate=pl.CostEstimate(flops=1 << 22, bytes_accessed=3 << 20, transcendentals=1 << 13),
-        name="pack",
-    )(
-        where,
-        mem_keys.transpose(1, 0, 2),
-        mem_values.transpose(1, 0, 2),
-        by_head,
-        mem_ids,
+    packed = (where, mem_keys.transpose(1, 0, 2), mem_values.transpose(1, 0, 2), by_head, mem_ids)
+
+    def pack(kernel, name, *shapes):
+        return pl.pallas_call(
+            kernel,
+            out_shape=[jax.ShapeDtypeStruct(*shape) for shape in shapes],
+            in_specs=[smem] + [vmem] * 4,
+            out_specs=[vmem] * len(shapes),
+            compiler_params=pltpu.CompilerParams(vmem_limit_bytes=16 << 20),
+            cost_estimate=pl.CostEstimate(flops=1 << 22, bytes_accessed=2 << 20, transcendentals=1 << 13),
+            name=name,
+        )(*packed)
+
+    other, placed = pack(
+        pack_other_kernel,
+        "pack_other",
+        ((SHARE + BLK_DEV + QROWS, HEAD), jnp.bfloat16),
+        ((8, 128), jnp.int32),
+    )
+    mine, mine_powers, mine_q = pack(
+        pack_mine_kernel,
+        "pack_mine",
+        ((SHARE, HEAD), jnp.bfloat16),
+        ((BLK_DEV, HEAD), jnp.bfloat16),
+        ((QROWS, HEAD), jnp.bfloat16),
     )
     near = lax.ppermute(
         jnp.concatenate([keys, values], axis=0).transpose(1, 0, 2), SEQ, [(i, i + 1) for i in range(2 * Z * Y - 1)]

time: 148 us -> 146 us (0.986)
  transfers between devices with their start and end apart: 5 -> 5, of which waited for: 3 -> 3; matrix products, arithmetic and copies ran while one was open for 2% -> 2% of each run, Pallas kernels for 1% -> 2%
where the time goes in v8:
time: 146 us
  blocking collectives  71 us (49%)
  starting transfers between devices  26.3 us (18%)
  waiting for transfers between devices  23.5 us (16%)
  Pallas kernels  17.5 us (12%)
  local copies, waits for them, and re-layouts  3.79 us (3%)
  other arithmetic  3.19 us (2%)
    all_gather x1, blocking collectives, on_device(): lax.all_gather(shard, SEQ, axis_index_groups=KV_LINES, tiled=True)  55.2 us
    all_to_all x1, waiting for transfers between devices, on_device(): lax.all_to_all(partial, SEQ, split_axis=0, concat_axis=0, axis_index_grou...  21.9 us
    all_to_all x1, blocking collectives, on_device(): lax.all_to_all(mixed, ('head', 'core'), split_axis=0, concat_axis=0, tile...  15.8 us
    pallas_call x1, Pallas kernels, on_device(): pl.pallas_call(memory_kernel, out_shape=pltpu.HBM((LINE, OROWS, ROWS), jn...  12.6 us
    ppermute x1, starting transfers between devices, on_device(): theirs = lax.ppermute(other, 'core', swap)  8.78 us
    ppermute x1, starting transfers between devices, on_device(): their_window = lax.ppermute(window[1], 'core', swap)  6.19 us
    all_to_all x1, starting transfers between devices, on_device(): lax.all_to_all(partial, SEQ, split_axis=0, concat_axis=0, axis_index_grou...  6 us
    ppermute x1, starting transfers between devices, on_device(): lax.ppermute(jnp.concatenate([keys, values], axis=0).transpose(1, 0, 2),...  3.06 us
  transfers between devices with their start and end apart: 5, of which 3 were waited for; matrix products, arithmetic and copies ran while one was open for 2% of the time, Pallas kernels for 2%

profile of v8, /device:TPU:1, one launch (start us, length us, event | category | flops | bytes accessed | tf_op | source)
XLA Modules:
  0.0 145.5 jit_solution(13988208399126742501)
XLA Ops:
  0.0 0.0 copy-start
  0.0 1.0 copy.25
  1.0 1.3 copy_bitcast_fusion
  2.3 0.1 pad_add_fusion.where_ref
  2.4 0.0 copy-done
  2.4 1.1 pack_other.1
  3.6 8.8 %collective-permute-start = (bf16[2592,128]{1,0:T(8,128)(2,1)S(1)}, bf16[2592,128]{1,0:T(8,128)(2,1)S(1)}, u32[]{:S(2)}, u32[]{:S(2)}) collective-permute-start(bf16[2592,128]{1,0:T(8,128)(2,1)S(1)} %get-tuple-element.12), channel_id=1, source_target_pairs={{0,4},{4,0},{1,5},{5,1},{2,6},{6,2},{3,7},{7,3},{8,12},{12,8},{9,1... | collective-permute-start | bytes 1990664 | tf_op jit(solution)/shard_map/ppermute | solution.py:254
  12.4 1.1 pack_mine.1
  13.6 0.5 collective-permute-done
  14.1 0.1 slice_dynamic-update-slice_fusion
  14.2 0.1 select_dynamic-update-slice_fusion.1
  14.2 0.1 select_dynamic-update-slice_fusion
  14.3 0.3 convert_element_type.33
  14.6 55.2 %all-gather.1 = f16[41472,128]{1,0:T(8,128)(2,1)S(1)} all-gather(f16[5184,128]{1,0:T(8,128)(2,1)S(1)} %convert_element_type.33), channel_id=1, replica_groups={{0,8,16,24,32,40,48,56},{64,72,80,88,96,104,112,120},{128,136,144,152,1..., dimensions={0}, use_global_device_ids=true | all-gather | bytes 11943936 | tf_op jit(solution)/shard_map/all_gather | solution.py:259
  69.7 0.0 copy-start.1
  69.7 0.0 copy-start.2
  69.7 0.4 slice.54
  70.2 2.3 %collective-permute-start.1 = (f16[8,1056,128]{2,1,0:T(8,128)(2,1)S(1)}, f16[8,1056,128]{2,1,0:T(8,128)(2,1)S(1)}, u32[]{:S(2)}, u32[]{:S(2)}) collective-permute-start(f16[8,1056,128]{2,1,0:T(8,128)(2,1)S(1)} %slice.54), channel_id=1, source_target_pairs={{0,4},{4,0},{1,5},{5,1},{2,6},{6,2},{3,7},{7,3},{8,12},{12,8},{9,1... | collective-permute-start | bytes 6488072 | tf_op jit(solution)/shard_map/ppermute | solution.py:261
  72.5 0.0 copy-done.1
  72.5 0.0 copy-done.2
  72.6 3.1 %collective-permute-start.2 = (bf16[2,256,128]{2,1,0:T(8,128)(2,1)S(1)}, bf16[2,256,128]{2,1,0:T(8,128)(2,1)S(1)}, u32[]{:S(2)}, u32[]{:S(2)}) collective-permute-start(bf16[2,256,128]{2,1,0:T(8,128)(2,1)S(1)} %maximum_bitcast_fusion), channel_id=1, source_target_pairs={{0,4},{4,8},{8,12},{12,16},{16,20},{20,24},{24,28},{28,32},{32,36}... | collective-permute-start | bytes 393224 | tf_op jit(solution)/shard_map/ppermute | solution.py:251
  75.7 1.2 convert_element_type.44.kv_ref
  77.0 0.0 collective-permute-done.1
  77.0 0.4 convert_element_type.34
  77.4 0.1 fusion.4
  77.5 0.1 convert_reduce_fusion.1
  77.6 0.4 convert_reduce_fusion
  78.0 0.3 select_reduce_fusion.power_at_ref
  78.4 0.0 collective-permute-done.2.near_ref
  78.4 12.6 %memory.1 = bf16[8,272,512]{2,1,0:T(8,128)(2,1)} custom-call(s32[16]{0:T(128)S(1)} %get-tuple-element.17.count_ref, s32[16,16]{1,0:T(8,128)S(1)} %fusion.6.place_ref, s32[16,16]{1,0:T(8,128)S(1)} %select_reduce_fusion.power_at_ref, bf16[8448,128]{1,0:T(8,128)(2,1)S(1)} %bitcast.43, f32[256,128]{1,0:T(8,128)S(1)} %bitcast_convert_fusion.powers_ref, ...), custom_call_target="tpu_custom_call" | custom-call | flops 1073741824 | bytes 6291456 | tf_op jit(solution)/shard_map/memory/pallas_call | solution.py:283
  91.0 6.0 %all-to-all-start = ((bf16[8,272,512]{2,1,0:T(8,128)(2,1)}), bf16[8,272,512]{2,1,0:T(8,128)(2,1)S(1)}, u32[]{:S(2)}, u32[]{:S(2)}) async-start(bf16[8,272,512]{2,1,0:T(8,128)(2,1)} %memory.1), calls=%async_computation | async-start | bytes 4456448 | tf_op jit(solution)/shard_map/all_to_all | solution.py:302
  97.0 0.0 copy-start.3
  97.0 1.4 window.1.window_ref
  98.4 6.2 %collective-permute-start.3 = (f32[128,512]{1,0:T(8,128)S(1)}, f32[128,512]{1,0:T(8,128)S(1)}, u32[]{:S(2)}, u32[]{:S(2)}) collective-permute-start(f32[128,512]{1,0:T(8,128)S(1)} %slice_bitcast_fusion), channel_id=1, source_target_pairs={{0,4},{4,0},{1,5},{5,1},{2,6},{6,2},{3,7},{7,3},{8,12},{12,8},{9,1... | collective-permute-start | bytes 786440 | tf_op jit(solution)/shard_map/ppermute | solution.py:322
  104.6 0.0 copy-done.3
  104.7 0.1 broadcast_select_fusion
  104.7 1.0 collective-permute-done.3.their_window_ref
  105.8 21.9 %all-to-all-done.part_ref = bf16[8,272,512]{2,1,0:T(8,128)(2,1)S(1)} async-done(((bf16[8,272,512]{2,1,0:T(8,128)(2,1)}), bf16[8,272,512]{2,1,0:T(8,128)(2,1)S(1)}, u32[]{:S(2)}, u32[]{:S(2)}) %all-to-all-start) | async-done | bytes 2228256 | tf_op jit(solution)/shard_map/all_to_all | solution.py:302
  127.7 0.1 broadcast_in_dim.42
  127.8 1.2 merge.1
  129.0 15.8 %all_to_all.10 = bf16[8,32,512]{2,1,0:T(8,128)(2,1)S(1)} all-to-all(bf16[8,32,512]{2,1,0:T(8,128)(2,1)S(1)} %merge.1), channel_id=1, replica_groups=mesh['z'=8,'y'=8,'core'=2,'head'=4] {'head','core'}, dimensions={0} | all-to-all | bytes 524288 | tf_op jit(solution)/shard_map/all_to_all | solution.py:335
  144.8 0.7 copy.33
  (18 shorter events, 0.3 us)
Async XLA Ops:
  0.0 2.4 %copy-start = (s32[2,1,32]{2,1,0:T(1,128)S(1)}, s32[2,1,32]{2,1,0:T(1,128)}, u32[]{:S(2)}) copy-start(s32[2,1,32]{2,1,0:T(1,128)} %ids_ref.3) | copy-start | bytes 772
  3.6 10.5 %collective-permute-start = (bf16[2592,128]{1,0:T(8,128)(2,1)S(1)}, bf16[2592,128]{1,0:T(8,128)(2,1)S(1)}, u32[]{:S(2)}, u32[]{:S(2)}) collective-permute-start(bf16[2592,128]{1,0:T(8,128)(2,1)S(1)} %get-tuple-element.12), channel_id=1, source_target_pairs={{0,4},{4,0},{1,5},{5,1},{2,6},{6,2},{3,7},{7,3},{8,12},{12,8},{9,1... | collective-permute-start | bytes 1990664 | tf_op jit(solution)/shard_map/ppermute | solution.py:254
  69.7 2.7 %copy-start.1 = (bf16[128,2,128]{2,1,0:T(2,128)(2,1)S(1)}, bf16[128,2,128]{2,1,0:T(2,128)(2,1)}, u32[]{:S(2)}) copy-start(bf16[128,2,128]{2,1,0:T(2,128)(2,1)} %param.9) | copy-start | bytes 196612
  69.7 2.8 %copy-start.2 = (bf16[128,2,128]{2,1,0:T(2,128)(2,1)S(1)}, bf16[128,2,128]{2,1,0:T(2,128)(2,1)}, u32[]{:S(2)}) copy-start(bf16[128,2,128]{2,1,0:T(2,128)(2,1)} %param.8) | copy-start | bytes 196612
  70.2 6.8 %collective-permute-start.1 = (f16[8,1056,128]{2,1,0:T(8,128)(2,1)S(1)}, f16[8,1056,128]{2,1,0:T(8,128)(2,1)S(1)}, u32[]{:S(2)}, u32[]{:S(2)}) collective-permute-start(f16[8,1056,128]{2,1,0:T(8,128)(2,1)S(1)} %slice.54), channel_id=1, source_target_pairs={{0,4},{4,0},{1,5},{5,1},{2,6},{6,2},{3,7},{7,3},{8,12},{12,8},{9,1... | collective-permute-start | bytes 6488072 | tf_op jit(solution)/shard_map/ppermute | solution.py:261
  72.6 5.8 %collective-permute-start.2 = (bf16[2,256,128]{2,1,0:T(8,128)(2,1)S(1)}, bf16[2,256,128]{2,1,0:T(8,128)(2,1)S(1)}, u32[]{:S(2)}, u32[]{:S(2)}) collective-permute-start(bf16[2,256,128]{2,1,0:T(8,128)(2,1)S(1)} %maximum_bitcast_fusion), channel_id=1, source_target_pairs={{0,4},{4,8},{8,12},{12,16},{16,20},{20,24},{24,28},{28,32},{32,36}... | collective-permute-start | bytes 393224 | tf_op jit(solution)/shard_map/ppermute | solution.py:251
  91.0 36.7 %all-to-all-start = ((bf16[8,272,512]{2,1,0:T(8,128)(2,1)}), bf16[8,272,512]{2,1,0:T(8,128)(2,1)S(1)}, u32[]{:S(2)}, u32[]{:S(2)}) async-start(bf16[8,272,512]{2,1,0:T(8,128)(2,1)} %memory.1), calls=%async_computation | async-start | bytes 4456448 | tf_op jit(solution)/shard_map/all_to_all | solution.py:302
  97.0 7.7 %copy-start.3 = (f32[8]{0:T(128)S(1)}, f32[8]{0:T(128)}, u32[]{:S(2)}) copy-start(f32[8]{0:T(128)} %param.13) | copy-start | bytes 100
  98.4 7.3 %collective-permute-start.3 = (f32[128,512]{1,0:T(8,128)S(1)}, f32[128,512]{1,0:T(8,128)S(1)}, u32[]{:S(2)}, u32[]{:S(2)}) collective-permute-start(f32[128,512]{1,0:T(8,128)S(1)} %slice_bitcast_fusion), channel_id=1, source_target_pairs={{0,4},{4,0},{1,5},{5,1},{2,6},{6,2},{3,7},{7,3},{8,12},{12,8},{9,1... | collective-permute-start | bytes 786440 | tf_op jit(solution)/shard_map/ppermute | solution.py:322

commit v9 on v8

--- a/solution.py
+++ b/solution.py
@@ -188,20 +188,21 @@
     send(LINE - 1).wait()
 
 
-def merge_kernel(where_ref, part_ref, window_ref, their_window_ref, gate_ref, o_ref):
+def merge_kernel(place_ref, part_ref, window_ref, their_window_ref, gate_ref, o_ref):
     gate = gate_ref[...]
-    for i, near in enumerate((window_ref.at[0], their_window_ref)):
-        rc = where_ref[2] ^ i
-        at = pl.ds(pl.multiple_of(rc * HEAD, HEAD), HEAD)
+    first_core = place_ref[2:3, 0:1] == 0
+    for rc in range(2):
+        at = slice(rc * HEAD, (rc + 1) * HEAD)
+        near = jnp.where(first_core == (rc == 0), window_ref[0], their_window_ref[...])
         levels = []
         for peer in range(LINE):
             pieces = part_ref[peer, 2 * HEAD :, :].astype(jnp.float32)
-            pieces = jnp.where(rc == 0, pieces[0:3, :], pieces[3:6, :])
+            pieces = pieces[3 * rc : 3 * rc + 3, :]
             levels.append(pieces[0:1] + pieces[1:2] + pieces[2:3])
         top = functools.reduce(jnp.maximum, levels)
         shares = [jnp.exp2(level - top) for level in levels]
         scale = gate / functools.reduce(jnp.add, shares)
-        mixed = (1.0 - gate) * near[...]
+        mixed = (1.0 - gate) * near
         for peer in range(LINE):
             mixed = mixed + part_ref[peer, at, :].astype(jnp.float32) * (shares[peer] * scale)
         for g in range(4):
@@ -326,12 +327,12 @@
     mixed = pl.pallas_call(
         merge_kernel,
         out_shape=jax.ShapeDtypeStruct((2 * X, 32, ROWS), jnp.bfloat16),
-        in_specs=[smem] + [vmem] * 4,
+        in_specs=[vmem] * 5,
         out_specs=vmem,
         compiler_params=pltpu.CompilerParams(vmem_limit_bytes=16 << 20),
         cost_estimate=pl.CostEstimate(flops=1 << 22, bytes_accessed=4 << 20, transcendentals=1 << 13),
         name="merge",
-    )(where, returned, window, their_window, gate)
+    )(placed, returned, window, their_window, gate)
     rows = lax.all_to_all(mixed, ("head", "core"), split_axis=0, concat_axis=0, tiled=True)
     return rows.transpose(1, 0, 2).reshape(32, 2 * X * ROWS)
 

time: 146 us -> 146 us (level)
  waiting for transfers between devices: 23.5 us -> 21.2 us
  starting transfers between devices: 26.3 us -> 28.3 us
    all_to_all x1, waiting for transfers between devices: 21.9 us -> 19.7 us  [on_device(): lax.all_to_all(partial, SEQ, split_axis=0, concat_axis=0, axis_index_grou...]
    ppermute x1, starting transfers between devices: 6.19 us -> 8.2 us  [on_device(): their_window = lax.ppermute(window[1], 'core', swap)]
where the time goes in v9:
time: 146 us; the launch traced here: 145 us
  blocking collectives  71.6 us (49%)
  starting transfers between devices  28.3 us (19%)
  waiting for transfers between devices  21.2 us (15%)
  Pallas kernels  16.9 us (12%)
  local copies, waits for them, and re-layouts  3.79 us (3%)
  other arithmetic  3.17 us (2%)
    all_gather x1, blocking collectives, on_device(): lax.all_gather(shard, SEQ, axis_index_groups=KV_LINES, tiled=True)  55.2 us
    all_to_all x1, waiting for transfers between devices, on_device(): lax.all_to_all(partial, SEQ, split_axis=0, concat_axis=0, axis_index_grou...  19.7 us
    all_to_all x1, blocking collectives, on_device(): lax.all_to_all(mixed, ('head', 'core'), split_axis=0, concat_axis=0, tile...  16.4 us
    pallas_call x1, Pallas kernels, on_device(): pl.pallas_call(memory_kernel, out_shape=pltpu.HBM((LINE, OROWS, ROWS), jn...  12.6 us
    ppermute x1, starting transfers between devices, on_device(): theirs = lax.ppermute(other, 'core', swap)  8.78 us
    ppermute x1, starting transfers between devices, on_device(): their_window = lax.ppermute(window[1], 'core', swap)  8.2 us
    all_to_all x1, starting transfers between devices, on_device(): lax.all_to_all(partial, SEQ, split_axis=0, concat_axis=0, axis_index_grou...  6.01 us
    ppermute x1, starting transfers between devices, on_device(): lax.ppermute(jnp.concatenate([keys, values], axis=0).transpose(1, 0, 2),...  3.06 us
  transfers between devices with their start and end apart: 5, of which 3 were waited for; matrix products, arithmetic and copies ran while one was open for 2% of the time, Pallas kernels for 2%

profile of v9, /device:TPU:1, one launch (start us, length us, event | category | flops | bytes accessed | tf_op | source)
XLA Modules:
  0.0 145.3 jit_solution(3024132220613806611)
XLA Ops:
  0.0 0.0 copy-start
  0.0 1.0 copy.25
  1.0 1.3 copy_bitcast_fusion
  2.3 0.1 pad_add_fusion.where_ref
  2.4 0.0 copy-done
  2.4 1.1 pack_other.1
  3.6 8.8 %collective-permute-start = (bf16[2592,128]{1,0:T(8,128)(2,1)S(1)}, bf16[2592,128]{1,0:T(8,128)(2,1)S(1)}, u32[]{:S(2)}, u32[]{:S(2)}) collective-permute-start(bf16[2592,128]{1,0:T(8,128)(2,1)S(1)} %get-tuple-element.12), channel_id=1, source_target_pairs={{0,4},{4,0},{1,5},{5,1},{2,6},{6,2},{3,7},{7,3},{8,12},{12,8},{9,1... | collective-permute-start | bytes 1990664 | tf_op jit(solution)/shard_map/ppermute | solution.py:255
  12.4 1.1 pack_mine.1
  13.6 0.5 collective-permute-done
  14.1 0.1 slice_dynamic-update-slice_fusion
  14.2 0.1 select_dynamic-update-slice_fusion.1
  14.2 0.1 select_dynamic-update-slice_fusion
  14.3 0.3 convert_element_type.33
  14.6 55.2 %all-gather.1 = f16[41472,128]{1,0:T(8,128)(2,1)S(1)} all-gather(f16[5184,128]{1,0:T(8,128)(2,1)S(1)} %convert_element_type.33), channel_id=1, replica_groups={{0,8,16,24,32,40,48,56},{64,72,80,88,96,104,112,120},{128,136,144,152,1..., dimensions={0}, use_global_device_ids=true | all-gather | bytes 11943936 | tf_op jit(solution)/shard_map/all_gather | solution.py:260
  69.7 0.0 copy-start.1
  69.7 0.0 copy-start.2
  69.7 0.4 slice.54
  70.2 2.3 %collective-permute-start.1 = (f16[8,1056,128]{2,1,0:T(8,128)(2,1)S(1)}, f16[8,1056,128]{2,1,0:T(8,128)(2,1)S(1)}, u32[]{:S(2)}, u32[]{:S(2)}) collective-permute-start(f16[8,1056,128]{2,1,0:T(8,128)(2,1)S(1)} %slice.54), channel_id=1, source_target_pairs={{0,4},{4,0},{1,5},{5,1},{2,6},{6,2},{3,7},{7,3},{8,12},{12,8},{9,1... | collective-permute-start | bytes 6488072 | tf_op jit(solution)/shard_map/ppermute | solution.py:262
  72.5 0.0 copy-done.1
  72.5 0.0 copy-done.2
  72.5 3.1 %collective-permute-start.2 = (bf16[2,256,128]{2,1,0:T(8,128)(2,1)S(1)}, bf16[2,256,128]{2,1,0:T(8,128)(2,1)S(1)}, u32[]{:S(2)}, u32[]{:S(2)}) collective-permute-start(bf16[2,256,128]{2,1,0:T(8,128)(2,1)S(1)} %maximum_bitcast_fusion), channel_id=1, source_target_pairs={{0,4},{4,8},{8,12},{12,16},{16,20},{20,24},{24,28},{28,32},{32,36}... | collective-permute-start | bytes 393224 | tf_op jit(solution)/shard_map/ppermute | solution.py:252
  75.7 1.2 convert_element_type.44.kv_ref
  77.0 0.0 collective-permute-done.1
  77.0 0.4 convert_element_type.34
  77.4 0.1 fusion.4
  77.5 0.1 convert_reduce_fusion.1
  77.6 0.4 convert_reduce_fusion
  78.0 0.3 select_reduce_fusion.power_at_ref
  78.4 0.0 collective-permute-done.2.near_ref
  78.4 12.6 %memory.1 = bf16[8,272,512]{2,1,0:T(8,128)(2,1)} custom-call(s32[16]{0:T(128)S(1)} %get-tuple-element.17.count_ref, s32[16,16]{1,0:T(8,128)S(1)} %fusion.6.place_ref, s32[16,16]{1,0:T(8,128)S(1)} %select_reduce_fusion.power_at_ref, bf16[8448,128]{1,0:T(8,128)(2,1)S(1)} %bitcast.43, f32[256,128]{1,0:T(8,128)S(1)} %bitcast_convert_fusion.powers_ref, ...), custom_call_target="tpu_custom_call" | custom-call | flops 1073741824 | bytes 6291456 | tf_op jit(solution)/shard_map/memory/pallas_call | solution.py:284
  90.9 6.0 %all-to-all-start = ((bf16[8,272,512]{2,1,0:T(8,128)(2,1)}), bf16[8,272,512]{2,1,0:T(8,128)(2,1)S(1)}, u32[]{:S(2)}, u32[]{:S(2)}) async-start(bf16[8,272,512]{2,1,0:T(8,128)(2,1)} %memory.1), calls=%async_computation | async-start | bytes 4456448 | tf_op jit(solution)/shard_map/all_to_all | solution.py:303
  97.0 0.0 copy-start.3
  97.0 1.4 window.1.window_ref
  98.4 8.2 %collective-permute-start.3 = (f32[128,512]{1,0:T(8,128)S(1)}, f32[128,512]{1,0:T(8,128)S(1)}, u32[]{:S(2)}, u32[]{:S(2)}) collective-permute-start(f32[128,512]{1,0:T(8,128)S(1)} %slice_bitcast_fusion), channel_id=1, source_target_pairs={{0,4},{4,0},{1,5},{5,1},{2,6},{6,2},{3,7},{7,3},{8,12},{12,8},{9,1... | collective-permute-start | bytes 786440 | tf_op jit(solution)/shard_map/ppermute | solution.py:323
  106.6 0.0 copy-done.3
  106.7 0.1 broadcast_select_fusion
  106.7 1.0 collective-permute-done.3.their_window_ref
  107.8 19.7 %all-to-all-done.part_ref = bf16[8,272,512]{2,1,0:T(8,128)(2,1)S(1)} async-done(((bf16[8,272,512]{2,1,0:T(8,128)(2,1)}), bf16[8,272,512]{2,1,0:T(8,128)(2,1)S(1)}, u32[]{:S(2)}, u32[]{:S(2)}) %all-to-all-start) | async-done | bytes 2228256 | tf_op jit(solution)/shard_map/all_to_all | solution.py:303
  127.4 0.1 broadcast_in_dim.42
  127.5 0.7 merge.1
  128.2 16.4 %all_to_all.10 = bf16[8,32,512]{2,1,0:T(8,128)(2,1)S(1)} all-to-all(bf16[8,32,512]{2,1,0:T(8,128)(2,1)S(1)} %merge.1), channel_id=1, replica_groups=mesh['z'=8,'y'=8,'core'=2,'head'=4] {'head','core'}, dimensions={0} | all-to-all | bytes 524288 | tf_op jit(solution)/shard_map/all_to_all | solution.py:336
  144.6 0.7 copy.33
  (18 shorter events, 0.3 us)
Async XLA Ops:
  0.0 2.4 %copy-start = (s32[2,1,32]{2,1,0:T(1,128)S(1)}, s32[2,1,32]{2,1,0:T(1,128)}, u32[]{:S(2)}) copy-start(s32[2,1,32]{2,1,0:T(1,128)} %ids_ref.3) | copy-start | bytes 772
  3.6 10.5 %collective-permute-start = (bf16[2592,128]{1,0:T(8,128)(2,1)S(1)}, bf16[2592,128]{1,0:T(8,128)(2,1)S(1)}, u32[]{:S(2)}, u32[]{:S(2)}) collective-permute-start(bf16[2592,128]{1,0:T(8,128)(2,1)S(1)} %get-tuple-element.12), channel_id=1, source_target_pairs={{0,4},{4,0},{1,5},{5,1},{2,6},{6,2},{3,7},{7,3},{8,12},{12,8},{9,1... | collective-permute-start | bytes 1990664 | tf_op jit(solution)/shard_map/ppermute | solution.py:255
  69.7 2.7 %copy-start.1 = (bf16[128,2,128]{2,1,0:T(2,128)(2,1)S(1)}, bf16[128,2,128]{2,1,0:T(2,128)(2,1)}, u32[]{:S(2)}) copy-start(bf16[128,2,128]{2,1,0:T(2,128)(2,1)} %param.9) | copy-start | bytes 196612
  69.7 2.8 %copy-start.2 = (bf16[128,2,128]{2,1,0:T(2,128)(2,1)S(1)}, bf16[128,2,128]{2,1,0:T(2,128)(2,1)}, u32[]{:S(2)}) copy-start(bf16[128,2,128]{2,1,0:T(2,128)(2,1)} %param.8) | copy-start | bytes 196612
  70.2 6.8 %collective-permute-start.1 = (f16[8,1056,128]{2,1,0:T(8,128)(2,1)S(1)}, f16[8,1056,128]{2,1,0:T(8,128)(2,1)S(1)}, u32[]{:S(2)}, u32[]{:S(2)}) collective-permute-start(f16[8,1056,128]{2,1,0:T(8,128)(2,1)S(1)} %slice.54), channel_id=1, source_target_pairs={{0,4},{4,0},{1,5},{5,1},{2,6},{6,2},{3,7},{7,3},{8,12},{12,8},{9,1... | collective-permute-start | bytes 6488072 | tf_op jit(solution)/shard_map/ppermute | solution.py:262
  72.5 5.8 %collective-permute-start.2 = (bf16[2,256,128]{2,1,0:T(8,128)(2,1)S(1)}, bf16[2,256,128]{2,1,0:T(8,128)(2,1)S(1)}, u32[]{:S(2)}, u32[]{:S(2)}) collective-permute-start(bf16[2,256,128]{2,1,0:T(8,128)(2,1)S(1)} %maximum_bitcast_fusion), channel_id=1, source_target_pairs={{0,4},{4,8},{8,12},{12,16},{16,20},{20,24},{24,28},{28,32},{32,36}... | collective-permute-start | bytes 393224 | tf_op jit(solution)/shard_map/ppermute | solution.py:252
  90.9 36.5 %all-to-all-start = ((bf16[8,272,512]{2,1,0:T(8,128)(2,1)}), bf16[8,272,512]{2,1,0:T(8,128)(2,1)S(1)}, u32[]{:S(2)}, u32[]{:S(2)}) async-start(bf16[8,272,512]{2,1,0:T(8,128)(2,1)} %memory.1), calls=%async_computation | async-start | bytes 4456448 | tf_op jit(solution)/shard_map/all_to_all | solution.py:303
  97.0 9.7 %copy-start.3 = (f32[8]{0:T(128)S(1)}, f32[8]{0:T(128)}, u32[]{:S(2)}) copy-start(f32[8]{0:T(128)} %param.13) | copy-start | bytes 100
  98.4 9.3 %collective-permute-start.3 = (f32[128,512]{1,0:T(8,128)S(1)}, f32[128,512]{1,0:T(8,128)S(1)}, u32[]{:S(2)}, u32[]{:S(2)}) collective-permute-start(f32[128,512]{1,0:T(8,128)S(1)} %slice_bitcast_fusion), channel_id=1, source_target_pairs={{0,4},{4,0},{1,5},{5,1},{2,6},{6,2},{3,7},{7,3},{8,12},{12,8},{9,1... | collective-permute-start | bytes 786440 | tf_op jit(solution)/shard_map/ppermute | solution.py:323
